TPU v7x, 128 devices: a whole 4x4x4 slice. The times are simulated.
128 devices in a mesh: grp: 16 (over y, x), seq: 8 (over z, core).
Axes of the slice: x: 4, y: 4, z: 4, core: 2. Of those that a mesh axis runs over, the one named last changes fastest.
Arguments:
- tokens: bfloat16 [16384, 768], P(('grp', 'seq')), may hold values from -24 to 24
- segments: int32 [16, 1024], P('grp', 'seq'), may hold values from 0 to 3, never falling along the last dimension, each value on 1 to 512 neighbouring positions
- rel_bucket: int32 [1024], replicated, may hold values from 0 to 31
- routes: int32 [16384, 2], P(('grp', 'seq')), may hold values from 0 to 15, all different within a row; in each aligned block of 128 rows (0 to 127, 128 to 255, ...) at most 24 rows name the same one
- gain_attn: bfloat16 [2, 768], replicated, may hold values from 0.5 to 1.5
- wqkv: bfloat16 [2, 768, 2304], P(None, ('grp', 'seq')), may hold values from -0.21875 to 0.21875
- wout: bfloat16 [2, 768, 768], P(None, ('grp', 'seq')), may hold values from -0.875 to 0.875
- bucket_bias_table: bfloat16 [2, 32, 12], replicated, may hold values from -3 to 3
- gain_ffn: bfloat16 [2, 768], replicated, may hold values from 0.5 to 1.5
- router: bfloat16 [2, 768, 16], replicated, may hold values from -0.21875 to 0.21875
- w_in: bfloat16 [2, 16, 768, 3072], P(None, 'grp', 'seq'), may hold values from -0.21875 to 0.21875
- w_out: bfloat16 [2, 16, 3072, 768], P(None, 'grp', 'seq'), may hold values from -0.875 to 0.875
- cotangent: float32 [16384, 768], P(('grp', 'seq')), may hold values from -6 to 6
Outputs:
- out_tokens: bfloat16 [16384, 768], P(('grp', 'seq'))
- grad_tokens: float32 [16384, 768], P(('grp', 'seq'))
- grad_gain_attn: float32 [2, 768], replicated
- grad_wqkv: float32 [2, 768, 2304], P(None, ('grp', 'seq'))
- grad_wout: float32 [2, 768, 768], P(None, ('grp', 'seq'))
- grad_table: float32 [2, 32, 12], replicated
- grad_gain_ffn: float32 [2, 768], replicated
- grad_router: float32 [2, 768, 16], replicated
- grad_w_in: float32 [2, 16, 768, 3072], P(None, 'grp', 'seq')
- grad_w_out: float32 [2, 16, 3072, 768], P(None, 'grp', 'seq')
Inputs may be any that keep to these rules, and one draw needn't show every extreme that they name: `segments`: along a sequence the document numbers never fall; each document spans at most half of 1024 positions, and one spans exactly that many. `routes`: each row names 2 different experts. Within the 128 rows of one device no expert is named more than 24 times, and in every draw some expert is named exactly 24 times in some device's rows.
All inputs are finite; a program needn't handle non-finite values.
Results may differ from a plain program's by a relative error of at most 0.022.
Values may be sent and summed in bfloat16 or wider, within the bound.
A program may use at most 256 MiB of HBM per device.

v0:
```python
import jax
import jax.numpy as jnp
from jax import lax
from jax.sharding import PartitionSpec as P

HEADS = 12
HEAD_DIM = 64
TOP = 2
BUCKETS = 32
LAYERS = 2


EPS = 1e-06
MASKED = -1e30
highest = lax.Precision.HIGHEST


def inv_root(values):
    return lax.rsqrt(jnp.mean(values * values, axis=-1, keepdims=True) + EPS)


def norm_backward(values, scale_rows, gain_row, grad_out):
    scaled = grad_out * gain_row
    grad_gain = jnp.sum(grad_out * values * scale_rows, axis=0)
    cubed = scale_rows * scale_rows * scale_rows
    input_gradient = scale_rows * scaled - values * cubed * jnp.mean(
        values * scaled, axis=-1, keepdims=True
    )
    return (input_gradient, grad_gain)


def mask_tables(segment_local, seg_keys, rel_bucket, query_start):
    count_q = segment_local.shape[0]
    count_k = seg_keys.shape[0]
    query_pos = query_start + jnp.arange(count_q, dtype=jnp.int32)
    key_pos = jnp.arange(count_k, dtype=jnp.int32)
    distance = query_pos[:, None] - key_pos[None, :]
    allowed = (distance >= 0) & (segment_local[:, None] == seg_keys[None, :])
    bucket_ids = jnp.take(rel_bucket, jnp.maximum(distance, 0))
    bucket_onehot = (
        bucket_ids[None, :, :] == jnp.arange(BUCKETS, dtype=jnp.int32)[:, None, None]
    ).astype(jnp.bfloat16)
    return (allowed, bucket_onehot)


def score_block(queries, key_block, allowed, bucket_onehot, bias_row_values):
    count_q = queries.shape[0]
    count_k = key_block.shape[0]
    q_heads = queries.reshape(count_q, HEADS, HEAD_DIM)
    k_heads = key_block.reshape(count_k, HEADS, HEAD_DIM)
    scores = jnp.einsum(
        "qhd,khd->hqk", q_heads, k_heads, preferred_element_type=jnp.float32
    ) * HEAD_DIM ** (-0.5)
    scores = scores + jnp.einsum(
        "snr,sx->xnr", bucket_onehot, bias_row_values, preferred_element_type=jnp.float32
    )
    return jnp.where(allowed[None], scores, MASKED)


def attend_forward(queries, key_block, value_block, allowed, bucket_onehot, bias_row_values):
    count_q = queries.shape[0]
    count_k = key_block.shape[0]
    scores = score_block(queries, key_block, allowed, bucket_onehot, bias_row_values)
    row_max = jnp.max(scores, axis=-1, keepdims=True)
    exponent = jnp.exp(scores - row_max)
    row_total = jnp.sum(exponent, axis=-1, keepdims=True)
    weights_low = (exponent / row_total).astype(jnp.bfloat16)
    v_heads = value_block.reshape(count_k, HEADS, HEAD_DIM)
    combined = jnp.einsum("hqk,khd->qhd", weights_low, v_heads, preferred_element_type=jnp.float32)
    log_total = row_max[:, :, 0] + jnp.log(row_total[:, :, 0])
    return (combined.reshape(count_q, HEADS * HEAD_DIM).astype(jnp.bfloat16), log_total)


def attend_backward(
    queries, key_block, value_block, allowed, bucket_onehot, bias_row_values, log_total, grad_out
):
    count_q = queries.shape[0]
    count_k = key_block.shape[0]
    scale = HEAD_DIM ** (-0.5)
    scores = score_block(queries, key_block, allowed, bucket_onehot, bias_row_values)
    probs = jnp.exp(scores - log_total[:, :, None])
    q_heads = queries.reshape(count_q, HEADS, HEAD_DIM)
    k_heads = key_block.reshape(count_k, HEADS, HEAD_DIM)
    v_heads = value_block.reshape(count_k, HEADS, HEAD_DIM)
    grad_heads = grad_out.reshape(count_q, HEADS, HEAD_DIM)
    grad_probs = jnp.einsum("qhd,khd->hqk", grad_heads, v_heads, preferred_element_type=jnp.float32)
    row_inner = jnp.sum(probs * grad_probs, axis=-1, keepdims=True)
    score_gradient = (probs * (grad_probs - row_inner)).astype(jnp.bfloat16)
    grad_query = (
        jnp.einsum("hqk,khd->qhd", score_gradient, k_heads, preferred_element_type=jnp.float32)
        * scale
    )
    grad_key = (
        jnp.einsum("hqk,qhd->khd", score_gradient, q_heads, preferred_element_type=jnp.float32)
        * scale
    )
    grad_value = jnp.einsum(
        "hqk,qhd->khd", probs.astype(jnp.bfloat16), grad_heads, preferred_element_type=jnp.float32
    )
    grad_bias = jnp.einsum(
        "rnc,dnc->dr", score_gradient, bucket_onehot, preferred_element_type=jnp.float32
    )
    return (
        grad_query.reshape(count_q, -1),
        grad_key.reshape(count_k, -1),
        grad_value.reshape(count_k, -1),
        grad_bias,
    )


def attention_weights(wqkv, wout, layer_index):
    return (
        lax.all_gather(wqkv[layer_index], ("grp", "seq"), axis=0, tiled=True),
        lax.all_gather(wout[layer_index], ("grp", "seq"), axis=0, tiled=True),
    )


def expert_weights(w_in, w_out, layer_index):
    both = (
        lax.all_gather(w_in[layer_index], "seq", axis=1, tiled=True),
        lax.all_gather(w_out[layer_index], "seq", axis=1, tiled=True),
    )
    return (both[0][0], both[1][0])


def key_rows(keys_own, values_own, seg_own):
    return (
        lax.all_gather(keys_own, "seq", axis=0, tiled=True),
        lax.all_gather(values_own, "seq", axis=0, tiled=True),
        lax.all_gather(seg_own, "seq", axis=0, tiled=True),
    )


def to_experts(rows, experts, capacity, model_width):
    return lax.all_to_all(
        rows.reshape(experts, capacity, model_width), "grp", split_axis=0, concat_axis=0, tiled=True
    ).reshape(-1, model_width)


def on_device(
    tokens,
    segments,
    rel_bucket,
    routes,
    gain_attn,
    wqkv,
    wout,
    bucket_bias_table,
    gain_ffn,
    router,
    w_in,
    w_out,
    cotangent,
):
    count_q = tokens.shape[0]
    model_width = tokens.shape[1]
    experts = lax.axis_size("grp")
    capacity = max(2, 3 * count_q * TOP // (2 * experts))
    query_start = lax.axis_index("seq") * count_q
    seg_own = segments[0].astype(jnp.bfloat16)
    flat_routes = routes.reshape(-1)
    expert_ids = jnp.arange(experts, dtype=jnp.int32)
    expert_hot = (flat_routes[:, None] == expert_ids[None, :]).astype(jnp.int32)
    rank_counts = jnp.cumsum(expert_hot, axis=0) - expert_hot
    target = flat_routes * capacity + jnp.sum(rank_counts * expert_hot, axis=1)
    dispatch = (jnp.arange(experts * capacity, dtype=jnp.int32)[:, None] == target[None, :]).astype(
        jnp.bfloat16
    )
    route_hot = (routes[:, :, None] == expert_ids[None, None, :]).astype(jnp.float32)
    hidden_state = tokens.astype(jnp.float32)
    stored_layers = []
    for layer_index in range(LAYERS):
        attn_full = attention_weights(wqkv, wout, layer_index)
        first_mat, second_mat = expert_weights(w_in, w_out, layer_index)
        scale_one = inv_root(hidden_state)
        normed = (hidden_state * scale_one * gain_attn[layer_index].astype(jnp.float32)).astype(
            jnp.bfloat16
        )
        projected = jnp.dot(normed, attn_full[0], preferred_element_type=jnp.float32).astype(
            jnp.bfloat16
        )
        queries = projected[:, :model_width]
        keys_own = projected[:, model_width : 2 * model_width]
        values_own = projected[:, 2 * model_width :]
        keys_all, values_all, seg_keys = key_rows(keys_own, values_own, seg_own)
        allowed, bucket_onehot = mask_tables(seg_own, seg_keys, rel_bucket, query_start)
        attended, log_total = attend_forward(
            queries, keys_all, values_all, allowed, bucket_onehot, bucket_bias_table[layer_index]
        )
        middle = hidden_state + jnp.dot(attended, attn_full[1], preferred_element_type=jnp.float32)
        scale_two = inv_root(middle)
        mixed_in = (middle * scale_two * gain_ffn[layer_index].astype(jnp.float32)).astype(
            jnp.bfloat16
        )
        router_probs = jax.nn.softmax(
            jnp.dot(mixed_in, router[layer_index], preferred_element_type=jnp.float32), axis=-1
        )
        gate_values = jnp.sum(router_probs[:, None, :] * route_hot, axis=2)
        pair_rows = jnp.repeat(mixed_in, TOP, axis=0)
        send_rows = jnp.dot(dispatch, pair_rows, preferred_element_type=jnp.float32).astype(
            jnp.bfloat16
        )
        expert_rows = to_experts(send_rows, experts, capacity, model_width)
        pre_act = jnp.dot(expert_rows, first_mat, preferred_element_type=jnp.float32)
        activated = jax.nn.gelu(pre_act).astype(jnp.bfloat16)
        expert_out = jnp.dot(activated, second_mat, preferred_element_type=jnp.float32).astype(
            jnp.bfloat16
        )
        returned = lax.all_to_all(
            expert_out.reshape(experts, capacity, model_width),
            "grp",
            split_axis=0,
            concat_axis=0,
            tiled=True,
        )
        pair_out = jnp.take(returned.reshape(-1, model_width), target, axis=0).reshape(
            count_q, TOP, model_width
        )
        new_state = middle + jnp.sum(gate_values[:, :, None] * pair_out.astype(jnp.float32), axis=1)
        stored_layers.append(
            (
                hidden_state,
                scale_one,
                normed,
                queries,
                keys_own,
                values_own,
                log_total,
                attended,
                middle,
                scale_two,
                mixed_in,
                router_probs,
                gate_values,
                pair_out,
                expert_rows,
                pre_act,
                activated,
                attn_full,
                first_mat,
                second_mat,
            )
        )
        hidden_state = new_state
    out_tokens = hidden_state.astype(jnp.bfloat16)
    grad_state = cotangent
    gain_a_grads = [None] * LAYERS
    gain_f_grads = [None] * LAYERS
    router_grads = [None] * LAYERS
    table_grads = [None] * LAYERS
    qkv_grads = [None] * LAYERS
    outproj_grads = [None] * LAYERS
    first_grads = [None] * LAYERS
    second_grads = [None] * LAYERS
    for layer_index in reversed(range(LAYERS)):
        (
            state_in,
            scale_one,
            normed,
            queries,
            keys_own,
            values_own,
            log_total,
            attended,
            middle,
            scale_two,
            mixed_in,
            router_probs,
            gate_values,
            pair_out,
            expert_rows,
            pre_act,
            activated,
            attn_full,
            first_mat,
            second_mat,
        ) = stored_layers[layer_index]
        attn_back = attention_weights(wqkv, wout, layer_index)
        first_back, second_back = expert_weights(w_in, w_out, layer_index)
        grad_gates = jnp.sum(grad_state[:, None, :] * pair_out.astype(jnp.float32), axis=2)
        grad_pairs = (
            (gate_values[:, :, None] * grad_state[:, None, :])
            .astype(jnp.bfloat16)
            .reshape(-1, model_width)
        )
        send_grads = jnp.dot(dispatch, grad_pairs, preferred_element_type=jnp.float32).astype(
            jnp.bfloat16
        )
        grad_rows = to_experts(send_grads, experts, capacity, model_width)
        grad_act = jnp.dot(grad_rows, second_back.T, preferred_element_type=jnp.float32)
        unused_value, gelu_pull = jax.vjp(jax.nn.gelu, pre_act)
        grad_pre = gelu_pull(grad_act)[0].astype(jnp.bfloat16)
        grad_second = jnp.dot(activated.T, grad_rows, preferred_element_type=jnp.float32)
        grad_first = jnp.dot(expert_rows.T, grad_pre, preferred_element_type=jnp.float32)
        grad_inputs = jnp.dot(grad_pre, first_back.T, preferred_element_type=jnp.float32)
        first_grads[layer_index], second_grads[layer_index] = (
            lax.psum_scatter(
                grad_first[None].astype(jnp.bfloat16), "seq", scatter_dimension=1, tiled=True
            ).astype(jnp.float32),
            lax.psum_scatter(
                grad_second[None].astype(jnp.bfloat16), "seq", scatter_dimension=1, tiled=True
            ).astype(jnp.float32),
        )
        grad_back = lax.all_to_all(
            grad_inputs.reshape(experts, capacity, model_width).astype(jnp.bfloat16),
            "grp",
            split_axis=0,
            concat_axis=0,
            tiled=True,
        ).astype(jnp.float32)
        grad_mixed = jnp.sum(
            jnp.take(grad_back.reshape(-1, model_width), target, axis=0).reshape(
                count_q, TOP, model_width
            ),
            axis=1,
        )
        grad_probs = jnp.sum(grad_gates[:, :, None] * route_hot, axis=1)
        grad_logits = router_probs * (
            grad_probs - jnp.sum(router_probs * grad_probs, axis=-1, keepdims=True)
        )
        router_rows = router[layer_index].astype(jnp.float32)
        router_grads[layer_index] = jnp.dot(
            mixed_in.astype(jnp.float32).T, grad_logits, precision=highest
        )
        grad_mixed = grad_mixed + jnp.dot(grad_logits, router_rows.T, precision=highest)
        grad_mid, gain_f_grads[layer_index] = norm_backward(
            middle, scale_two, gain_ffn[layer_index].astype(jnp.float32), grad_mixed
        )
        grad_mid = grad_mid + grad_state
        branch_grad = grad_mid.astype(jnp.bfloat16)
        grad_out_proj = jnp.dot(attended.T, branch_grad, preferred_element_type=jnp.float32)
        grad_attended = jnp.dot(
            branch_grad, attn_back[1].T, preferred_element_type=jnp.float32
        ).astype(jnp.bfloat16)
        keys_all, values_all, seg_keys = key_rows(keys_own, values_own, seg_own)
        allowed, bucket_onehot = mask_tables(seg_own, seg_keys, rel_bucket, query_start)
        grad_queries, grad_keys_all, grad_values_all, table_grads[layer_index] = attend_backward(
            queries,
            keys_all,
            values_all,
            allowed,
            bucket_onehot,
            bucket_bias_table[layer_index],
            log_total,
            grad_attended,
        )
        grad_keys, grad_values = (
            lax.psum_scatter(
                grad_keys_all.astype(jnp.bfloat16), "seq", scatter_dimension=0, tiled=True
            ).astype(jnp.float32),
            lax.psum_scatter(
                grad_values_all.astype(jnp.bfloat16), "seq", scatter_dimension=0, tiled=True
            ).astype(jnp.float32),
        )
        grad_proj = jnp.concatenate([grad_queries, grad_keys, grad_values], axis=1).astype(
            jnp.bfloat16
        )
        grad_in_proj = jnp.dot(normed.T, grad_proj, preferred_element_type=jnp.float32)
        grad_normed = jnp.dot(grad_proj, attn_back[0].T, preferred_element_type=jnp.float32)
        grad_prev, gain_a_grads[layer_index] = norm_backward(
            state_in, scale_one, gain_attn[layer_index].astype(jnp.float32), grad_normed
        )
        grad_state = grad_mid + grad_prev
        qkv_grads[layer_index], outproj_grads[layer_index] = (
            lax.psum_scatter(grad_in_proj, ("grp", "seq"), scatter_dimension=0, tiled=True),
            lax.psum_scatter(grad_out_proj, ("grp", "seq"), scatter_dimension=0, tiled=True),
        )
    small_sums = lax.psum(
        (
            jnp.stack(gain_a_grads),
            jnp.stack(gain_f_grads),
            jnp.stack(router_grads),
            jnp.stack(table_grads),
        ),
        ("grp", "seq"),
    )
    return (
        out_tokens,
        grad_state,
        small_sums[0],
        jnp.stack(qkv_grads),
        jnp.stack(outproj_grads),
        small_sums[3],
        small_sums[1],
        small_sums[2],
        jnp.stack(first_grads),
        jnp.stack(second_grads),
    )


def solution(mesh):
    placed = (
        P(("grp", "seq"), None),
        P("grp", "seq"),
        P(),
        P(("grp", "seq"), None),
        P(),
        P(None, ("grp", "seq"), None),
        P(None, ("grp", "seq"), None),
        P(),
        P(),
        P(),
        P(None, "grp", "seq", None),
        P(None, "grp", "seq", None),
        P(("grp", "seq"), None),
    )
    return jax.shard_map(
        on_device,
        mesh=mesh,
        in_specs=placed,
        out_specs=(
            P(("grp", "seq"), None),
            P(("grp", "seq"), None),
            P(),
            P(None, ("grp", "seq"), None),
            P(None, ("grp", "seq"), None),
            P(),
            P(),
            P(),
            P(None, "grp", "seq", None),
            P(None, "grp", "seq", None),
        ),
        check_vma=False,
    )
```

profile of v0, /device:TPU:1, one launch (start us, length us, event | category | flops | bytes accessed | tf_op | source)
XLA Modules:
  0.0 2143.3 jit_solution(18033386583653546171)
XLA Ops:
  12.0 72.3 %all-gather.30.cloned.1.call-done = bf16[1,768,2304]{2,0,1:T(2,128)(2,1)} async-done(((bf16[1,6,2304]{2,0,1:T(2,128)(2,1)}), bf16[1,768,2304]{2,0,1:T(2,128)(2,1)}) %all-gather.30.cloned.1.call-update) | async-done | bytes 3538960 | tf_op jit(solution)/shard_map/all_gather | solution.py:113
  95.2 9.2 all-gather.1
  106.5 520.8 %gather_fusion = s32[131072]{0:T(1024)S(1)} fusion(s32[1024]{0:T(1024)S(1)} %copy-done, s32[131072]{0:T(1024)S(1)} %broadcast_clamp_fusion), kind=kCustom, calls=%fused_computation.clone | custom fusion | bytes 1572864 | tf_op jit(solution)/shard_map/jit(_take)/gather | solution.py:39
  627.8 5.8 fusion.7
  633.7 8.3 copy.113
  647.3 4.9 fusion.175
  661.2 5.2 all-to-all-start
  666.4 11.5 all-to-all-done
  677.9 6.7 fusion.46
  684.6 7.4 fusion.80
  696.3 10.1 all-to-all-done.1
  717.2 5.8 fusion.6
  723.0 8.3 copy.122
  731.5 5.2 all-gather.28.cloned.1.call-done
  738.4 25.2 %all-gather.26.cloned.1.call-done = bf16[1024,768]{1,0:T(8,128)(2,1)} async-done(((bf16[128,768]{1,0:T(8,128)(2,1)}), bf16[1024,768]{1,0:T(8,128)(2,1)}) %all-gather.26.cloned.1.call-update) | async-done | bytes 1572880 | tf_op jit(solution)/shard_map/all_gather | solution.py:129
  766.2 4.3 fusion.177
  774.9 57.5 %all-gather.40.cloned.1.call-done = bf16[1,768,768]{2,0,1:T(2,128)(2,1)} async-done(((bf16[1,6,768]{2,0,1:T(2,128)(2,1)}), bf16[1,768,768]{2,0,1:T(2,128)(2,1)}) %all-gather.40.cloned.1.call-update) | async-done | bytes 1179664 | tf_op jit(solution)/shard_map/all_gather | solution.py:114
  837.2 4.7 all-to-all-start.2
  842.8 23.2 %all-gather.42.cloned.1.call-done = bf16[1,1,768,3072]{3,2,1,0:T(8,128)(2,1)} async-done(((bf16[1,1,96,3072]{3,2,1,0:T(8,128)(2,1)}), bf16[1,1,768,3072]{3,2,1,0:T(8,128)(2,1)}) %all-gather.42.cloned.1.call-update) | async-done | bytes 4718608 | tf_op jit(solution)/shard_map/all_gather | solution.py:120
  866.0 6.7 fusion.40
  872.7 29.8 %all-gather.44.cloned.1.call-done = bf16[1,1,3072,768]{3,2,1,0:T(8,128)(2,1)} async-done(((bf16[1,1,384,768]{3,2,1,0:T(8,128)(2,1)}), bf16[1,1,3072,768]{3,2,1,0:T(8,128)(2,1)}) %all-gather.44.cloned.1.call-update) | async-done | bytes 4718608 | tf_op jit(solution)/shard_map/all_gather | solution.py:121
  902.5 7.4 fusion.83
  910.0 6.7 all-to-all-start.3
  916.9 11.3 all-to-all-done.3
  930.7 14.6 all_to_all.40
  945.3 8.1 fusion.31
  965.3 7.3 all-to-all-done.5
  990.0 4.6 multiply_reduce_fusion.1
  1007.6 10.6 reduce-scatter.35.cloned.1.call-done
  1019.9 32.1 %reduce-scatter.33.cloned.1.call-done = bf16[128,768]{1,0:T(8,128)(2,1)} async-done(((bf16[1024,768]{1,0:T(8,128)(2,1)}), bf16[128,768]{1,0:T(8,128)(2,1)}) %reduce-scatter.33.cloned.1.call-update) | async-done | bytes 196624
  1053.8 5.4 multiply_reduce_fusion.8
  1066.0 15.7 all_to_all.41
  1081.8 8.1 fusion.24
  1091.2 5.3 fusion.89
  1102.0 8.2 all-to-all-done.7
  1136.5 5.2 fusion.73
  1144.4 4.9 multiply_reduce_fusion
  1158.9 6.7 fusion.49
  1165.9 6.7 fusion.48
  1172.7 7.6 fusion.51
  1180.4 7.6 fusion.50
  1191.2 5.4 fusion.132
  1201.6 11.4 reduce-scatter.37.cloned.1.call-done
  1214.7 5.2 fusion.131
  1219.9 371.1 %fusion.167 = (f32[8,2304]{1,0:T(8,128)}, f32[8,2304]{1,0:T(8,128)}, f32[8,768]{1,0:T(8,128)}, f32[8,768]{1,0:T(8,128)}) fusion(f32[768,2304]{1,0:T(8,128)} %fusion.132, f32[768,2304]{1,0:T(8,128)} %fusion.131, f32[768,768]{1,0:T(8,128)} %fusion.140, f32[768,768]{1,0:T(8,128)} %fusion.137), kind=kCustom, calls=%all-reduce-scatter.4 | all-reduce-scatter fusion | flops 6291457 | bytes 19070976
  1616.3 5.9 collective-permute-start.117
  1660.4 4.4 collective-permute-start.101
  1720.1 4.4 collective-permute-start.74
  1749.0 7.7 copy.131
  1768.0 5.5 fusion.109
  1773.6 7.7 copy.130
  1789.0 4.9 fusion.108
  1805.4 4.6 collective-permute-start.50
  1822.5 6.6 collective-permute-start.43
  1843.3 5.1 collective-permute-start.36
  1848.5 4.5 fusion.128
  1880.3 6.4 collective-permute-start.22
  1892.4 63.5 %all-reduce.8 = (f32[2,768]{1,0:T(2,128)}, f32[2,32,12]{1,2,0:T(8,128)S(1)}, f32[2,768]{1,0:T(2,128)}) all-reduce(f32[2,768]{1,0:T(2,128)S(1)} %get-tuple-element.132, f32[2,32,12]{1,2,0:T(8,128)S(1)} %pad_maximum_fusion.9, f32[2,768]{1,0:T(2,128)S(1)} %get-tuple-element.133), channel_id=1, replica_groups=mesh['grp'=16,'seq'=8] {'grp','seq'}, use_global_device_ids=true, to_apply=%region_39.43 | all-reduce | flops 3840 | bytes 30720 | tf_op jit(solution)/shard_map/psum | solution.py:368
  1956.5 26.5 %concatenate.13 = f32[262,768]{1,0:T(8,128)S(1)} concatenate(f32[6,768]{1,0:T(8,128)S(1)} %copy-done.129, f32[8,768]{1,0:T(8,128)} %collective-permute-done.126, f32[8,768]{1,0:T(8,128)} %collective-permute-done.125, f32[8,768]{1,0:T(8,128)} %collective-permute-done.124, f32[8,768]{1,0:T(8,128)} %collective-permute-done.123, f32[8,768]{1,0:T(8,128)} %collective-permute-done.122, ...), dimensions={0} | concatenate | bytes 1609728
  1983.0 25.7 %concatenate.12 = f32[262,768]{1,0:T(8,128)S(1)} concatenate(f32[6,768]{1,0:T(8,128)S(1)} %copy-done.127, f32[8,768]{1,0:T(8,128)} %collective-permute-done.94, f32[8,768]{1,0:T(8,128)} %collective-permute-done.93, f32[8,768]{1,0:T(8,128)} %collective-permute-done.92, f32[8,768]{1,0:T(8,128)} %collective-permute-done.91, f32[8,768]{1,0:T(8,128)} %collective-permute-done.90, ...), dimensions={0} | concatenate | bytes 1609728
  2017.3 6.5 collective-permute-start.17
  2029.3 6.0 collective-permute-start.14
  2063.2 24.7 %concatenate.11 = f32[262,2304]{1,0:T(8,128)S(1)} concatenate(f32[6,2304]{1,0:T(8,128)} %collective-permute-done.63, f32[8,2304]{1,0:T(8,128)} %collective-permute-done.62, f32[8,2304]{1,0:T(8,128)} %collective-permute-done.61, f32[8,2304]{1,0:T(8,128)S(1)} %collective-permute-done.60, f32[8,2304]{1,0:T(8,128)S(1)} %collective-permute-done.59, ...), dimensions={0} | concatenate | bytes 4829184
  2102.8 25.6 %concatenate.10 = f32[262,2304]{1,0:T(8,128)S(1)} concatenate(f32[6,2304]{1,0:T(8,128)} %collective-permute-done.31, f32[8,2304]{1,0:T(8,128)S(1)} %copy-done.91, f32[8,2304]{1,0:T(8,128)S(1)} %copy-done.94, f32[8,2304]{1,0:T(8,128)S(1)} %copy-done.97, f32[8,2304]{1,0:T(8,128)} %copy-done.99, f32[8,2304]{1,0:T(8,128)} %copy-done.100, f32[8,2304]{1,0:T(8,128)} %copy-done.102, ...), dimensions={0} | concatenate | bytes 4829184
  (803 shorter events, 469.1 us)
Async XLA Ops:
  7.2 77.0 %all-gather.30.cloned.1.call-start = ((), (), s32[]{:S(2)}) async-start(), calls=%async_computation.25 | async-start | bytes 7133184 | tf_op jit(solution)/shard_map/all_gather | solution.py:113
  9.0 634.3 %all-gather.24.cloned.1.call-start = ((), (), s32[]{:S(2)}) async-start(), calls=%async_computation.17 | async-start | bytes 1769472 | tf_op jit(solution)/shard_map/all_gather | solution.py:128
  89.0 556.0 %all-gather.22.cloned.1.call-start = ((), (), s32[]{:S(2)}) async-start(), calls=%async_computation.16 | async-start | bytes 1769472 | tf_op jit(solution)/shard_map/all_gather | solution.py:129
  89.8 567.0 %all-gather.32.cloned.1.call-start = ((), (), s32[]{:S(2)}) async-start(), calls=%async_computation.26 | async-start | bytes 2377728 | tf_op jit(solution)/shard_map/all_gather | solution.py:114
  90.5 576.0 %all-gather.34.cloned.1.call-start = ((), (), s32[]{:S(2)}) async-start(), calls=%async_computation.27 | async-start | bytes 5308416 | tf_op jit(solution)/shard_map/all_gather | solution.py:120
  91.7 592.9 %all-gather.36.cloned.1.call-start = ((), (), s32[]{:S(2)}) async-start(), calls=%async_computation.28 | async-start | bytes 5308416 | tf_op jit(solution)/shard_map/all_gather | solution.py:121
  92.9 617.1 %all-gather.38.cloned.1.call-start = ((), (), s32[]{:S(2)}) async-start(), calls=%async_computation.29 | async-start | bytes 7133184 | tf_op jit(solution)/shard_map/all_gather | solution.py:113
  661.2 16.8 all-to-all-start
  695.8 40.9 %all-gather.28.cloned.1.call-start = ((), (), s32[]{:S(2)}) async-start(), calls=%async_computation.19 | async-start | bytes 1769472 | tf_op jit(solution)/shard_map/all_gather | solution.py:128
  714.6 49.1 %all-gather.26.cloned.1.call-start = ((), (), s32[]{:S(2)}) async-start(), calls=%async_computation.18 | async-start | bytes 1769472 | tf_op jit(solution)/shard_map/all_gather | solution.py:129
  715.3 117.1 %all-gather.40.cloned.1.call-start = ((), (), s32[]{:S(2)}) async-start(), calls=%async_computation.30 | async-start | bytes 2377728 | tf_op jit(solution)/shard_map/all_gather | solution.py:114
  715.9 150.1 %all-gather.42.cloned.1.call-start = ((), (), s32[]{:S(2)}) async-start(), calls=%async_computation.31 | async-start | bytes 5308416 | tf_op jit(solution)/shard_map/all_gather | solution.py:120
  716.6 185.9 %all-gather.44.cloned.1.call-start = ((), (), s32[]{:S(2)}) async-start(), calls=%async_computation.32 | async-start | bytes 5308416 | tf_op jit(solution)/shard_map/all_gather | solution.py:121
  837.2 28.8 %all-to-all-start.2 = ((bf16[16,24,768]{2,1,0:T(8,128)(2,1)}), bf16[16,24,768]{2,1,0:T(8,128)(2,1)}, u32[]{:S(2)}, u32[]{:S(2)}) async-start(bf16[16,24,768]{2,1,0:T(8,128)(2,1)} %bitcast.26), calls=%async_computation.2 | async-start | bytes 1179648 | tf_op jit(solution)/shard_map/all_to_all | solution.py:135
  910.0 18.2 all-to-all-start.3
  962.1 56.1 %reduce-scatter.35.cloned.1.call-start = ((), (), s32[]{:S(2)}) async-start(), calls=%async_computation.34 | async-start | bytes 1769472
  989.9 62.1 %reduce-scatter.33.cloned.1.call-start = ((), (), s32[]{:S(2)}) async-start(), calls=%async_computation.33 | async-start | bytes 1769472
  1100.8 99.0 %reduce-scatter.39.cloned.1.call-start = ((), (), s32[]{:S(2)}) async-start(), calls=%async_computation.36 | async-start | bytes 1769472
  1144.3 68.6 %reduce-scatter.37.cloned.1.call-start = ((), (), s32[]{:S(2)}) async-start(), calls=%async_computation.35 | async-start | bytes 1769472
  1158.9 970.2 %reduce-scatter.27.cloned.1.call-start = ((), (), s32[]{:S(2)}) async-start(), calls=%async_computation.22 | async-start | bytes 5308416 | tf_op jit(solution)/shard_map/reduce_scatter | solution.py:297
  1165.7 963.4 %reduce-scatter.25.cloned.1.call-start = ((), (), s32[]{:S(2)}) async-start(), calls=%async_computation.21 | async-start | bytes 5308416 | tf_op jit(solution)/shard_map/reduce_scatter | solution.py:297
  1172.6 959.3 %reduce-scatter.31.cloned.1.call-start = ((), (), s32[]{:S(2)}) async-start(), calls=%async_computation.24 | async-start | bytes 5308416 | tf_op jit(solution)/shard_map/reduce_scatter | solution.py:300
  1180.3 951.6 %reduce-scatter.29.cloned.1.call-start = ((), (), s32[]{:S(2)}) async-start(), calls=%async_computation.23 | async-start | bytes 5308416 | tf_op jit(solution)/shard_map/reduce_scatter | solution.py:300
  1188.0 946.7 %all-reduce.12.cloned.1.call-start = ((), (), s32[]{:S(2)}) async-start(), calls=%async_computation.20 | async-start | bytes 196608 | tf_op jit(solution)/shard_map/psum | solution.py:368
  1608.4 17.3 collective-permute-start.120
  1610.3 17.4 collective-permute-start.119
  1612.2 19.1 collective-permute-start.118
  1616.3 17.8 collective-permute-start.117
  1732.4 25.6 %collective-permute-start.69 = (f32[8,768]{1,0:T(8,128)}, f32[8,768]{1,0:T(8,128)}, u32[]{:S(2)}, u32[]{:S(2)}) collective-permute-start(f32[8,768]{1,0:T(8,128)} %get-tuple-element.77), channel_id=1, source_target_pairs={{0,6},{1,7},{2,8},{3,9},{4,10},{5,11},{6,12},{7,13},{8,14},{9,15},... | collective-permute-start | bytes 73736
  1736.5 23.5 %collective-permute-start.68 = (f32[8,768]{1,0:T(8,128)}, f32[8,768]{1,0:T(8,128)}, u32[]{:S(2)}, u32[]{:S(2)}) collective-permute-start(f32[8,768]{1,0:T(8,128)} %get-tuple-element.77), channel_id=1, source_target_pairs={{0,5},{1,6},{2,7},{3,8},{4,9},{5,10},{6,11},{7,12},{8,13},{9,14},{... | collective-permute-start | bytes 73736
  1738.8 23.1 %collective-permute-start.67 = (f32[8,768]{1,0:T(8,128)}, f32[8,768]{1,0:T(8,128)}, u32[]{:S(2)}, u32[]{:S(2)}) collective-permute-start(f32[8,768]{1,0:T(8,128)} %get-tuple-element.77), channel_id=1, source_target_pairs={{0,4},{1,5},{2,6},{3,7},{4,8},{5,9},{6,10},{7,11},{8,12},{9,13},{1... | collective-permute-start | bytes 73736
  1741.9 21.9 %collective-permute-start.66 = (f32[8,768]{1,0:T(8,128)}, f32[8,768]{1,0:T(8,128)}, u32[]{:S(2)}, u32[]{:S(2)}) collective-permute-start(f32[8,768]{1,0:T(8,128)} %get-tuple-element.77), channel_id=1, source_target_pairs={{0,3},{1,4},{2,5},{3,6},{4,7},{5,8},{6,9},{7,10},{8,11},{9,12},{10... | collective-permute-start | bytes 73736
  1745.4 20.4 collective-permute-start.65
  1758.0 23.4 %collective-permute-start.64 = (f32[8,768]{1,0:T(8,128)S(1)}, f32[8,768]{1,0:T(8,128)S(1)}, u32[]{:S(2)}, u32[]{:S(2)}) collective-permute-start(f32[8,768]{1,0:T(8,128)S(1)} %copy-done.55), channel_id=1, source_target_pairs={{0,1},{1,2},{2,3},{3,4},{4,5},{5,6},{6,7},{7,8},{8,9},{9,10},{10,1... | collective-permute-start | bytes 73736
  1760.0 26.4 %collective-permute-start.62 = (f32[8,2304]{1,0:T(8,128)S(1)}, f32[8,2304]{1,0:T(8,128)}, u32[]{:S(2)}, u32[]{:S(2)}) collective-permute-start(f32[8,2304]{1,0:T(8,128)S(1)} %copy-done.50), channel_id=1, source_target_pairs={{0,31},{1,32},{2,33},{3,34},{4,35},{5,36},{6,37},{7,38},{8,39},{9,... | collective-permute-start | bytes 221192
  1761.9 25.8 %collective-permute-start.61 = (f32[8,2304]{1,0:T(8,128)S(1)}, f32[8,2304]{1,0:T(8,128)}, u32[]{:S(2)}, u32[]{:S(2)}) collective-permute-start(f32[8,2304]{1,0:T(8,128)S(1)} %copy-done.50), channel_id=1, source_target_pairs={{0,30},{1,31},{2,32},{3,33},{4,34},{5,35},{6,36},{7,37},{8,38},{9,... | collective-permute-start | bytes 221192
  1763.8 19.0 collective-permute-start.31
  1765.7 19.4 collective-permute-start.63
  1812.7 16.4 collective-permute-start.47
  1814.0 18.9 collective-permute-start.46
  1817.3 16.9 collective-permute-start.45
  1819.0 16.9 collective-permute-start.44
  1834.3 18.7 collective-permute-start.40
  1835.9 19.9 collective-permute-start.39
  1837.9 22.2 %collective-permute-start.38 = (f32[8,2304]{1,0:T(8,128)S(1)}, f32[8,2304]{1,0:T(8,128)S(1)}, u32[]{:S(2)}, u32[]{:S(2)}) collective-permute-start(f32[8,2304]{1,0:T(8,128)S(1)} %copy-done.50), channel_id=1, source_target_pairs={{0,7},{1,8},{2,9},{3,10},{4,11},{5,12},{6,13},{7,14},{8,15},{9,16}... | collective-permute-start | bytes 221192
  1840.3 22.6 %collective-permute-start.37 = (f32[8,2304]{1,0:T(8,128)S(1)}, f32[8,2304]{1,0:T(8,128)S(1)}, u32[]{:S(2)}, u32[]{:S(2)}) collective-permute-start(f32[8,2304]{1,0:T(8,128)S(1)} %copy-done.50), channel_id=1, source_target_pairs={{0,6},{1,7},{2,8},{3,9},{4,10},{5,11},{6,12},{7,13},{8,14},{9,15},... | collective-permute-start | bytes 221192
  1843.3 22.7 %collective-permute-start.36 = (f32[8,2304]{1,0:T(8,128)S(1)}, f32[8,2304]{1,0:T(8,128)S(1)}, u32[]{:S(2)}, u32[]{:S(2)}) collective-permute-start(f32[8,2304]{1,0:T(8,128)S(1)} %copy-done.50), channel_id=1, source_target_pairs={{0,5},{1,6},{2,7},{3,8},{4,9},{5,10},{6,11},{7,12},{8,13},{9,14},{... | collective-permute-start | bytes 221192
  1877.6 131.1 %collective-permute-start.24 = (f32[8,2304]{1,0:T(8,128)S(1)}, f32[8,2304]{1,0:T(8,128)S(1)}, u32[]{:S(2)}, u32[]{:S(2)}) collective-permute-start(f32[8,2304]{1,0:T(8,128)S(1)} %copy-done.49), channel_id=1, source_target_pairs={{0,25},{1,26},{2,27},{3,28},{4,29},{5,30},{6,31},{7,32},{8,33},{9,... | collective-permute-start | bytes 221192
  1878.9 134.0 %collective-permute-start.23 = (f32[8,2304]{1,0:T(8,128)S(1)}, f32[8,2304]{1,0:T(8,128)S(1)}, u32[]{:S(2)}, u32[]{:S(2)}) collective-permute-start(f32[8,2304]{1,0:T(8,128)S(1)} %copy-done.49), channel_id=1, source_target_pairs={{0,24},{1,25},{2,26},{3,27},{4,28},{5,29},{6,30},{7,31},{8,32},{9,... | collective-permute-start | bytes 221192
  1880.3 137.0 %collective-permute-start.22 = (f32[8,2304]{1,0:T(8,128)S(1)}, f32[8,2304]{1,0:T(8,128)S(1)}, u32[]{:S(2)}, u32[]{:S(2)}) collective-permute-start(f32[8,2304]{1,0:T(8,128)S(1)} %copy-done.49), channel_id=1, source_target_pairs={{0,23},{1,24},{2,25},{3,26},{4,27},{5,28},{6,29},{7,30},{8,31},{9,... | collective-permute-start | bytes 221192
  1886.7 137.1 %collective-permute-start.21 = (f32[8,2304]{1,0:T(8,128)S(1)}, f32[8,2304]{1,0:T(8,128)}, u32[]{:S(2)}, u32[]{:S(2)}) collective-permute-start(f32[8,2304]{1,0:T(8,128)S(1)} %copy-done.49), channel_id=1, source_target_pairs={{0,22},{1,23},{2,24},{3,25},{4,26},{5,27},{6,28},{7,29},{8,30},{9,... | collective-permute-start | bytes 221192
  1890.4 135.3 %collective-permute-start.20 = (f32[8,2304]{1,0:T(8,128)S(1)}, f32[8,2304]{1,0:T(8,128)}, u32[]{:S(2)}, u32[]{:S(2)}) collective-permute-start(f32[8,2304]{1,0:T(8,128)S(1)} %copy-done.49), channel_id=1, source_target_pairs={{0,21},{1,22},{2,23},{3,24},{4,25},{5,26},{6,27},{7,28},{8,29},{9,... | collective-permute-start | bytes 221192
  2008.7 20.6 collective-permute-start.19
  2013.0 22.3 %collective-permute-start.18 = (f32[8,2304]{1,0:T(8,128)S(1)}, f32[8,2304]{1,0:T(8,128)S(1)}, u32[]{:S(2)}, u32[]{:S(2)}) collective-permute-start(f32[8,2304]{1,0:T(8,128)S(1)} %copy-done.49), channel_id=1, source_target_pairs={{0,19},{1,20},{2,21},{3,22},{4,23},{5,24},{6,25},{7,26},{8,27},{9,... | collective-permute-start | bytes 221192
  2017.3 19.9 collective-permute-start.17
  2023.8 17.2 collective-permute-start.16
  2025.7 19.2 collective-permute-start.15
  2029.3 19.8 collective-permute-start.14
  2037.2 16.9 collective-permute-start.12
  2049.1 38.8 %collective-permute-start.9 = (f32[8,2304]{1,0:T(8,128)S(1)}, f32[8,2304]{1,0:T(8,128)}, u32[]{:S(2)}, u32[]{:S(2)}) collective-permute-start(f32[8,2304]{1,0:T(8,128)S(1)} %copy-done.49), channel_id=1, source_target_pairs={{0,10},{1,11},{2,12},{3,13},{4,14},{5,15},{6,16},{7,17},{8,18},{9,... | collective-permute-start | bytes 221192
  2051.0 38.8 %collective-permute-start.8 = (f32[8,2304]{1,0:T(8,128)S(1)}, f32[8,2304]{1,0:T(8,128)}, u32[]{:S(2)}, u32[]{:S(2)}) collective-permute-start(f32[8,2304]{1,0:T(8,128)S(1)} %copy-done.49), channel_id=1, source_target_pairs={{0,9},{1,10},{2,11},{3,12},{4,13},{5,14},{6,15},{7,16},{8,17},{9,1... | collective-permute-start | bytes 221192
  2054.1 39.2 %collective-permute-start.7 = (f32[8,2304]{1,0:T(8,128)S(1)}, f32[8,2304]{1,0:T(8,128)}, u32[]{:S(2)}, u32[]{:S(2)}) collective-permute-start(f32[8,2304]{1,0:T(8,128)S(1)} %copy-done.49), channel_id=1, source_target_pairs={{0,8},{1,9},{2,10},{3,11},{4,12},{5,13},{6,14},{7,15},{8,16},{9,17... | collective-permute-start | bytes 221192
  2056.0 40.3 %collective-permute-start.6 = (f32[8,2304]{1,0:T(8,128)S(1)}, f32[8,2304]{1,0:T(8,128)}, u32[]{:S(2)}, u32[]{:S(2)}) collective-permute-start(f32[8,2304]{1,0:T(8,128)S(1)} %copy-done.49), channel_id=1, source_target_pairs={{0,7},{1,8},{2,9},{3,10},{4,11},{5,12},{6,13},{7,14},{8,15},{9,16}... | collective-permute-start | bytes 221192
  2058.0 40.6 %collective-permute-start.5 = (f32[8,2304]{1,0:T(8,128)S(1)}, f32[8,2304]{1,0:T(8,128)}, u32[]{:S(2)}, u32[]{:S(2)}) collective-permute-start(f32[8,2304]{1,0:T(8,128)S(1)} %copy-done.49), channel_id=1, source_target_pairs={{0,6},{1,7},{2,8},{3,9},{4,10},{5,11},{6,12},{7,13},{8,14},{9,15},... | collective-permute-start | bytes 221192
  (259 other events, 9901.9 us)
Sparse Core Ops, SparseCore 0:
  11.6 72.6 all-gather.29
  89.1 21.9 all-gather.23
  112.9 24.5 all-gather.21
  140.9 65.3 all-gather.31
  207.9 31.8 all-gather.33
  241.9 34.3 all-gather.35
  279.8 68.8 all-gather.37
  714.7 21.9 all-gather.27
  739.0 24.5 all-gather.25
  767.0 65.3 all-gather.39
  834.1 31.8 all-gather.41
  868.1 34.3 all-gather.43
  990.0 28.1 reduce-scatter.34
  1020.5 31.5 reduce-scatter.32
  1144.5 34.5 reduce-scatter.38
  1181.3 31.5 reduce-scatter.36
  1215.2 55.0 reduce-scatter.26
  1272.6 54.5 reduce-scatter.24
  1329.5 55.9 reduce-scatter.30
  1387.8 55.9 reduce-scatter.28
  1817.4 138.3 all-reduce.11
where the time goes:
time: 2170 us; the launch traced here: 2140 us
  local copies, waits for them, and re-layouts  728 us (34%)
  blocking collectives  474 us (22%)
  starting transfers between devices  358 us (16%)
  waiting for transfers between devices  324 us (15%)
  matrix products  195 us (9%)
  other arithmetic  46.2 us (2%)
    gather x2, local copies, waits for them, and re-layouts, mask_tables(): bucket_ids = jnp.take(rel_bucket, jnp.maximum(distance, 0))  521 us
    unnamed x1, blocking collectives  371 us
    unnamed x132, starting transfers between devices  328 us
    unnamed x356, local copies, waits for them, and re-layouts  136 us
    all_gather x2, waiting for transfers between devices, attention_weights(): lax.all_gather(wqkv[layer_index], ('grp', 'seq'), axis=0, tiled=True)  72.3 us
    psum x1, blocking collectives, on_device(): lax.psum((jnp.stack(gain_a_grads), jnp.stack(gain_f_grads), jnp.stack(rou...  63.5 us
    unnamed x153, waiting for transfers between devices  62.3 us
    all_gather x2, waiting for transfers between devices, attention_weights(): lax.all_gather(wout[layer_index], ('grp', 'seq'), axis=0, tiled=True)  57.5 us
  transfers between devices with their start and end apart: 155, of which 16 were waited for; matrix products, arithmetic and copies ran while one was open for 57% of the time, Pallas kernels for 0%

commit v1 on v0

v1 whole, which is shorter than its diff:
```python
import jax
import jax.numpy as jnp
from jax import lax
from jax.experimental import pallas as pl
from jax.experimental.pallas import tpu as pltpu
from jax.sharding import PartitionSpec as P

D = 768
HEADS = 12
HEAD_DIM = 64
PAIRS = HEADS // 2
TOP = 2
BUCKETS = 32
LAYERS = 2
BACK = 4
EPS = 1e-06
MASKED = -1e30
SCALE = HEAD_DIM**-0.5
BF = jnp.bfloat16
F32 = jnp.float32
highest = lax.Precision.HIGHEST
VMEM = pltpu.VMEM


def dot(a, b, contract=((1,), (0,))):
    return lax.dot_general(a, b, (contract, ((), ())), preferred_element_type=F32)


def inv_root(values):
    return lax.rsqrt(jnp.mean(values * values, axis=-1, keepdims=True) + EPS)


def norm_backward(values, scale_rows, gain_row, grad_out):
    scaled = grad_out * gain_row
    grad_gain = jnp.sum(grad_out * values * scale_rows, axis=0)
    cubed = scale_rows * scale_rows * scale_rows
    input_gradient = scale_rows * scaled - values * cubed * jnp.mean(
        values * scaled, axis=-1, keepdims=True
    )
    return (input_gradient, grad_gain)


def head_scores(q2, k2, low_lanes, head, allowed, bias_ref, width, span):
    mine = low_lanes if head % 2 == 0 else jnp.logical_not(low_lanes)
    q_head = jnp.where(mine, q2, jnp.zeros_like(q2))
    scores = dot(q_head, k2, ((1,), (1,))) * SCALE
    row = jnp.broadcast_to(bias_ref[head : head + 1, :], (q2.shape[0], span))
    bias = pltpu.roll(row, 0, 1, stride=1, stride_axis=0)[:, :width]
    return q_head, mine, jnp.where(allowed, scores + bias, MASKED)


def allowed_pairs(off_ref, segq_ref, segk_ref, rows, width):
    i = lax.broadcasted_iota(jnp.int32, (rows, width), 0)
    j = lax.broadcasted_iota(jnp.int32, (rows, width), 1)
    return (off_ref[0] + i - j >= 0) & (segq_ref[...] == segk_ref[...])


def attention_kernel(off_ref, q_ref, kv_ref, segq_ref, segk_ref, bias_ref, out_ref, lse_ref):
    rows, width, span = q_ref.shape[0], kv_ref.shape[0], bias_ref.shape[1]
    allowed = allowed_pairs(off_ref, segq_ref, segk_ref, rows, width)
    low_lanes = lax.broadcasted_iota(jnp.int32, (rows, 128), 1) < HEAD_DIM
    lane = lax.broadcasted_iota(jnp.int32, (rows, 128), 1)
    totals = jnp.zeros((rows, 128), F32)
    for pair in range(PAIRS):
        at = slice(pair * 128, pair * 128 + 128)
        q2, k2 = q_ref[:, at], kv_ref[:, at]
        v2 = kv_ref[:, D + pair * 128 : D + pair * 128 + 128]
        both = []
        for head in (2 * pair, 2 * pair + 1):
            _, _, scores = head_scores(q2, k2, low_lanes, head, allowed, bias_ref, width, span)
            row_max = jnp.max(scores, axis=1, keepdims=True)
            exponent = jnp.exp(scores - row_max)
            row_total = jnp.sum(exponent, axis=1, keepdims=True)
            weights = (exponent / row_total).astype(BF)
            both.append(dot(weights, v2))
            totals = jnp.where(lane == head, row_max + jnp.log(row_total), totals)
        out_ref[:, at] = jnp.where(low_lanes, both[0], both[1]).astype(BF)
    lse_ref[...] = totals


def attention_back_kernel(
    off_ref, q_ref, kv_ref, segq_ref, segk_ref, bias_ref, lse_ref, grad_ref, dq_ref, dkv_ref, diag_ref
):
    rows, width, span = q_ref.shape[0], kv_ref.shape[0], bias_ref.shape[1]
    allowed = allowed_pairs(off_ref, segq_ref, segk_ref, rows, width)
    low_lanes = lax.broadcasted_iota(jnp.int32, (rows, 128), 1) < HEAD_DIM
    lane = lax.broadcasted_iota(jnp.int32, (rows, 128), 1)
    i = lax.broadcasted_iota(jnp.int32, (rows, rows), 0)
    j = lax.broadcasted_iota(jnp.int32, (rows, rows), 1)
    flip = (i + j == rows - 1).astype(BF)
    for pair in range(PAIRS):
        at = slice(pair * 128, pair * 128 + 128)
        at_v = slice(D + pair * 128, D + pair * 128 + 128)
        q2, k2, v2, g2 = q_ref[:, at], kv_ref[:, at], kv_ref[:, at_v], grad_ref[:, at]
        dq, dk, dv = [], None, None
        for head in (2 * pair, 2 * pair + 1):
            q_head, mine, scores = head_scores(q2, k2, low_lanes, head, allowed, bias_ref, width, span)
            log_total = jnp.sum(jnp.where(lane == head, lse_ref[...], 0.0), axis=1, keepdims=True)
            probs = jnp.exp(scores - log_total)
            g_head = jnp.where(mine, g2, jnp.zeros_like(g2))
            grad_probs = dot(g_head, v2, ((1,), (1,)))
            inner = jnp.sum(probs * grad_probs, axis=1, keepdims=True)
            grad_scores = (probs * (grad_probs - inner)).astype(BF)
            dq.append(dot(grad_scores, k2))
            dk_head = dot(grad_scores, q_head, ((0,), (0,)))
            dv_head = dot(probs.astype(BF), g_head, ((0,), (0,)))
            dk = dk_head if dk is None else dk + dk_head
            dv = dv_head if dv is None else dv + dv_head
            turned = jnp.concatenate(
                [dot(flip, grad_scores), jnp.zeros((rows, span - width), F32)], axis=1
            )
            turned = pltpu.roll(turned, span - (rows - 1), 1, stride=1, stride_axis=0)
            diag_ref[head : head + 1, :] = jnp.sum(turned, axis=0, keepdims=True)
        dq_ref[:, at] = (jnp.where(low_lanes, dq[0], dq[1]) * SCALE).astype(BF)
        dkv_ref[:, at] = (dk * SCALE).astype(BF)
        dkv_ref[:, at_v] = dv.astype(BF)


def vmem_specs(n):
    return [pl.BlockSpec(memory_space=VMEM) for _ in range(n)]


def attention(off, queries, kv, segq, segk, bias):
    return pl.pallas_call(
        attention_kernel,
        out_shape=(
            jax.ShapeDtypeStruct(queries.shape, BF),
            jax.ShapeDtypeStruct((queries.shape[0], 128), F32),
        ),
        in_specs=[pl.BlockSpec(memory_space=pltpu.SMEM)] + vmem_specs(5),
        out_specs=tuple(vmem_specs(2)),
        compiler_params=pltpu.CompilerParams(vmem_limit_bytes=32 * 2**20),
    )(off, queries, kv, segq, segk, bias)


def attention_back(off, queries, kv, segq, segk, bias, lse, grad):
    return pl.pallas_call(
        attention_back_kernel,
        out_shape=(
            jax.ShapeDtypeStruct(queries.shape, BF),
            jax.ShapeDtypeStruct(kv.shape, BF),
            jax.ShapeDtypeStruct(bias.shape, F32),
        ),
        in_specs=[pl.BlockSpec(memory_space=pltpu.SMEM)] + vmem_specs(7),
        out_specs=tuple(vmem_specs(3)),
        compiler_params=pltpu.CompilerParams(vmem_limit_bytes=32 * 2**20),
    )(off, queries, kv, segq, segk, bias, lse, grad)


def to_peers(rows):
    return lax.all_to_all(rows, "grp", split_axis=0, concat_axis=0, tiled=True)


def gather_attn(wqkv, wout, layer_index):
    own = jnp.concatenate([wqkv[layer_index], wout[layer_index]], axis=1)
    own = own.reshape(-1, 128)
    full = lax.all_gather(lax.all_gather(own, "seq", axis=0, tiled=True), "grp", axis=0, tiled=True)
    return full.reshape(D, -1)


def gather_experts(w_in, w_out, layer_index):
    first = lax.all_gather(w_in[layer_index, 0], "seq", axis=0, tiled=True)
    second = lax.all_gather(w_out[layer_index, 0], "seq", axis=0, tiled=True)
    return first, second


def on_device(
    tokens,
    segments,
    rel_bucket,
    routes,
    gain_attn,
    wqkv,
    wout,
    bucket_bias_table,
    gain_ffn,
    router,
    w_in,
    w_out,
    cotangent,
):
    count_q = tokens.shape[0]
    experts = lax.axis_size("grp")
    blocks = lax.axis_size("seq")
    capacity = max(2, 3 * count_q * TOP // (2 * experts))
    window = (BACK + 1) * count_q
    span = window + count_q
    me = lax.axis_index("seq")
    first_block = jnp.clip(me - BACK, 0, blocks - BACK - 1)
    start = first_block * count_q
    off = (me * count_q - start).astype(jnp.int32)

    place = jnp.arange(span, dtype=jnp.int32)
    distance = off - jnp.where(place < window, place, place - span)
    pick = (distance[:, None] == jnp.arange(rel_bucket.shape[0], dtype=jnp.int32)[None, :]).astype(BF)
    bucket_at = dot(pick, rel_bucket.astype(BF)[:, None])[:, 0].astype(jnp.int32)
    in_range = (distance >= 0) & (distance < rel_bucket.shape[0])
    bucket_hot = (
        (bucket_at[None, :] == jnp.arange(BUCKETS, dtype=jnp.int32)[:, None]) & in_range[None, :]
    ).astype(BF)
    bias_rows = [dot(bucket_bias_table[l], bucket_hot, ((0,), (0,))) for l in range(LAYERS)]

    expert_ids = jnp.arange(experts, dtype=jnp.int32)
    flat_routes = jnp.concatenate([routes[:, 0], routes[:, 1]])
    hot = (flat_routes[:, None] == expert_ids[None, :]).astype(BF)
    number = jnp.arange(TOP * count_q, dtype=jnp.int32)
    ranks = dot((number[:, None] > number[None, :]).astype(BF), hot)
    rank = jnp.sum(ranks * hot.astype(F32), axis=1).astype(jnp.int32)
    target = flat_routes * capacity + rank
    slots = jnp.arange(experts * capacity, dtype=jnp.int32)
    dispatch = (slots[:, None] == target[None, :]).astype(BF)
    dispatch_tokens = dispatch[:, :count_q] + dispatch[:, count_q:]
    route_hot = hot.astype(F32).reshape(TOP, count_q, experts)

    seg_own = segments[0].astype(F32)
    seg_col = seg_own[:, None]
    hidden_state = tokens.astype(F32)
    gains_a, gains_f = gain_attn.astype(F32), gain_ffn.astype(F32)
    stored = []
    seg_keys = None
    attn_full = [gather_attn(wqkv, wout, l) for l in range(LAYERS)]
    expert_full = [gather_experts(w_in, w_out, l) for l in range(LAYERS)]
    for l in range(LAYERS):
        qkv_mat, out_mat = attn_full[l][:, : 3 * D], attn_full[l][:, 3 * D :]
        first_mat, second_mat = expert_full[l]
        scale_one = inv_root(hidden_state)
        normed = (hidden_state * scale_one * gains_a[l]).astype(BF)
        projected = dot(normed, qkv_mat).astype(BF)
        queries = projected[:, :D]
        kv_own = projected[:, D:]
        if l == 0:
            tail = jnp.broadcast_to(seg_col, (count_q, 128)).astype(BF)
            kv_own = jnp.concatenate([kv_own, tail], axis=1)
        kv = lax.all_gather(kv_own, "seq", axis=0, tiled=True)
        kv = lax.dynamic_slice_in_dim(kv, start, window, axis=0)
        if l == 0:
            seg_keys = kv[:, 2 * D].astype(F32)[None, :]
            kv = kv[:, : 2 * D]
        off_arr = off.reshape(1)
        attended, lse = attention(off_arr, queries, kv, seg_col, seg_keys, bias_rows[l])
        middle = hidden_state + dot(attended, out_mat)
        scale_two = inv_root(middle)
        mixed_in = (middle * scale_two * gains_f[l]).astype(BF)
        router_probs = jax.nn.softmax(dot(mixed_in, router[l]), axis=-1)
        gate_values = jnp.sum(router_probs[None] * route_hot, axis=2)
        send_rows = dot(dispatch_tokens, mixed_in).astype(BF)
        expert_rows = to_peers(send_rows.reshape(experts, capacity, D)).reshape(-1, D)
        pre_act = dot(expert_rows, first_mat)
        activated = jax.nn.gelu(pre_act).astype(BF)
        expert_out = dot(activated, second_mat).astype(BF)
        returned = to_peers(expert_out.reshape(experts, capacity, D)).reshape(-1, D)
        pair_out = dot(dispatch, returned, ((0,), (0,))).reshape(TOP, count_q, D)
        new_state = middle + jnp.sum(gate_values[:, :, None] * pair_out, axis=0)
        stored.append(
            (hidden_state, scale_one, normed, queries, kv, lse, attended, middle, scale_two,
             mixed_in, router_probs, gate_values, pair_out, expert_rows, pre_act, activated)
        )
        hidden_state = new_state
    out_tokens = hidden_state.astype(BF)

    grad_state = cotangent
    small = [None] * LAYERS
    attn_grads = [None] * LAYERS
    first_grads = [None] * LAYERS
    second_grads = [None] * LAYERS
    for l in reversed(range(LAYERS)):
        (state_in, scale_one, normed, queries, kv, lse, attended, middle, scale_two,
         mixed_in, router_probs, gate_values, pair_out, expert_rows, pre_act, activated) = stored[l]
        qkv_mat, out_mat = attn_full[l][:, : 3 * D], attn_full[l][:, 3 * D :]
        first_mat, second_mat = expert_full[l]
        grad_gates = jnp.sum(grad_state[None] * pair_out, axis=2)
        grad_pairs = (gate_values[:, :, None] * grad_state[None]).astype(BF).reshape(-1, D)
        send_grads = dot(dispatch, grad_pairs).astype(BF)
        grad_rows = to_peers(send_grads.reshape(experts, capacity, D)).reshape(-1, D)
        grad_act = dot(grad_rows, second_mat, ((1,), (1,)))
        _, gelu_pull = jax.vjp(jax.nn.gelu, pre_act)
        grad_pre = gelu_pull(grad_act)[0].astype(BF)
        grad_inputs = dot(grad_pre, first_mat, ((1,), (1,))).astype(BF)
        grad_back = to_peers(grad_inputs.reshape(experts, capacity, D)).reshape(-1, D)
        grad_second = dot(activated, grad_rows, ((0,), (0,))).astype(BF)
        grad_first = dot(expert_rows, grad_pre, ((0,), (0,))).astype(BF)
        first_grads[l] = lax.psum_scatter(grad_first, "seq", scatter_dimension=0, tiled=True).astype(F32)
        second_grads[l] = lax.psum_scatter(grad_second, "seq", scatter_dimension=0, tiled=True).astype(F32)
        grad_mixed = dot(dispatch_tokens, grad_back, ((0,), (0,)))
        grad_probs = jnp.sum(grad_gates[:, :, None] * route_hot, axis=0)
        grad_logits = router_probs * (
            grad_probs - jnp.sum(router_probs * grad_probs, axis=-1, keepdims=True)
        )
        router_grad = jnp.dot(mixed_in.astype(F32).T, grad_logits, precision=highest)
        grad_mixed = grad_mixed + jnp.dot(grad_logits, router[l].astype(F32).T, precision=highest)
        grad_mid, gain_f_grad = norm_backward(middle, scale_two, gains_f[l], grad_mixed)
        grad_mid = grad_mid + grad_state
        branch_grad = grad_mid.astype(BF)
        grad_out_proj = dot(attended, branch_grad, ((0,), (0,))).astype(BF)
        grad_attended = dot(branch_grad, out_mat, ((1,), (1,))).astype(BF)
        dq, dkv, diag = attention_back(
            off_arr, queries, kv, seg_col, seg_keys, bias_rows[l], lse, grad_attended
        )
        table_grad = lax.dot_general(
            bucket_hot.astype(F32), diag, (((1,), (1,)), ((), ())), precision=highest
        )
        dkv_all = lax.dynamic_update_slice_in_dim(
            jnp.zeros((blocks * count_q, 2 * D), BF), dkv, start, axis=0
        )
        dkv_own = lax.psum_scatter(dkv_all, "seq", scatter_dimension=0, tiled=True)
        grad_proj = jnp.concatenate([dq, dkv_own], axis=1)
        grad_in_proj = dot(normed, grad_proj, ((0,), (0,))).astype(BF)
        grad_normed = dot(grad_proj, qkv_mat, ((1,), (1,)))
        grad_prev, gain_a_grad = norm_backward(state_in, scale_one, gains_a[l], grad_normed)
        grad_state = grad_mid + grad_prev
        both = jnp.concatenate([grad_in_proj, grad_out_proj], axis=1).reshape(-1, 128)
        both = lax.psum_scatter(both, "grp", scatter_dimension=0, tiled=True)
        both = lax.psum_scatter(both, "seq", scatter_dimension=0, tiled=True)
        attn_grads[l] = both.reshape(-1, 4 * D).astype(F32)
        small[l] = (gain_a_grad, gain_f_grad, router_grad, table_grad)
    sizes = [D, D, D * experts, BUCKETS * HEADS]
    flat = jnp.concatenate([part.reshape(-1) for l in range(LAYERS) for part in small[l]])
    flat = lax.psum(flat.reshape(-1, 128), ("grp", "seq")).reshape(LAYERS, -1)
    sums, at = [], 0
    for size in sizes:
        sums.append(flat[:, at : at + size])
        at += size
    attn = jnp.stack(attn_grads)
    return (
        out_tokens,
        grad_state,
        sums[0],
        attn[:, :, : 3 * D],
        attn[:, :, 3 * D :],
        sums[3].reshape(LAYERS, BUCKETS, HEADS),
        sums[1],
        sums[2].reshape(LAYERS, D, experts),
        jnp.stack(first_grads)[:, None],
        jnp.stack(second_grads)[:, None],
    )


def solution(mesh):
    rows = P(("grp", "seq"), None)
    slab = P(None, ("grp", "seq"), None)
    expert = P(None, "grp", "seq", None)
    return jax.shard_map(
        on_device,
        mesh=mesh,
        in_specs=(
            rows, P("grp", "seq"), P(), rows, P(), slab, slab, P(), P(), P(), expert, expert, rows,
        ),
        out_specs=(rows, rows, P(), slab, slab, P(), P(), P(), expert, expert),
        check_vma=False,
    )
```

time: 2170 us -> 1140 us (0.53)
  local copies, waits for them, and re-layouts: 728 us -> 70.7 us
  waiting for transfers between devices: 324 us -> 774 us
  blocking collectives: 474 us -> 47.5 us
  starting transfers between devices: 358 us -> 41.4 us
  matrix products: 195 us -> 122 us
  Pallas kernels: 0 us -> 26.7 us
    gather x6 -> x0, local copies, waits for them, and re-layouts: 528 us -> none  [the longest x2 521 us: mask_tables(): bucket_ids = jnp.take(rel_bucket, jnp.maximum(distance, 0))]
    reduce_scatter x4 -> x10, waiting for transfers between devices: 0.01 us -> 376 us  [the longest x2 112 us: on_device(): both = lax.psum_scatter(both, 'grp', scatter_dimension=0, tiled=True)]
    unnamed x1 -> x0, blocking collectives: 371 us -> none
    unnamed x132 -> x0, starting transfers between devices: 328 us -> none
    psum x1, waiting for transfers between devices: 0.01 us -> 145 us  [on_device(): flat = lax.psum(flat.reshape(-1, 128), ('grp', 'seq')).reshape(LAYERS, -1)]
    unnamed x356 -> x161, local copies, waits for them, and re-layouts: 136 us -> 10.8 us
    dot_general x50 -> x44, matrix products: 195 us -> 122 us  [the longest x38 118 us: dot(): lax.dot_general(a, b, (contract, ((), ())), preferred_element_type=F32)]
    psum x1 -> x0, blocking collectives: 63.5 us -> none  [on_device(): lax.psum((jnp.stack(gain_a_grads), jnp.stack(gain_f_grads), jnp.stack(rou...]
  transfers between devices with their start and end apart: 155 -> 26, of which waited for: 16 -> 23; matrix products, arithmetic and copies ran while one was open for 57% -> 12% of each run, Pallas kernels for 0% -> 1%
where the time goes in v1:
time: 1140 us; the launch traced here: 1120 us
  waiting for transfers between devices  774 us (68%)
  matrix products  122 us (11%)
  local copies, waits for them, and re-layouts  70.7 us (6%)
  blocking collectives  47.5 us (4%)
  starting transfers between devices  41.4 us (4%)
  Pallas kernels  26.7 us (2%)
  other arithmetic  26.4 us (2%)
  between operations  15.6 us (1%)
    psum x1, waiting for transfers between devices, on_device(): flat = lax.psum(flat.reshape(-1, 128), ('grp', 'seq')).reshape(LAYERS, -1)  145 us
    dot_general x38, matrix products, dot(): lax.dot_general(a, b, (contract, ((), ())), preferred_element_type=F32)  118 us
    reduce_scatter x2, waiting for transfers between devices, on_device(): both = lax.psum_scatter(both, 'grp', scatter_dimension=0, tiled=True)  112 us
    all_gather x2, waiting for transfers between devices, gather_attn(): lax.all_gather(lax.all_gather(own, 'seq', axis=0, tiled=True), 'grp', axi...  94.1 us
    reduce_scatter x2, waiting for transfers between devices, on_device(): lax.psum_scatter(grad_first, 'seq', scatter_dimension=0, tiled=True)  78.6 us
    reduce_scatter x2, waiting for transfers between devices, on_device(): lax.psum_scatter(grad_second, 'seq', scatter_dimension=0, tiled=True)  71.7 us
    reduce_scatter x2, waiting for transfers between devices, on_device(): both = lax.psum_scatter(both, 'seq', scatter_dimension=0, tiled=True)  60.5 us
    all_gather x2, waiting for transfers between devices, gather_experts(): second = lax.all_gather(w_out[layer_index, 0], 'seq', axis=0, tiled=True)  59.1 us
  transfers between devices with their start and end apart: 26, of which 23 were waited for; matrix products, arithmetic and copies ran while one was open for 12% of the time, Pallas kernels for 1%

profile of v1, /device:TPU:1, one launch (start us, length us, event | category | flops | bytes accessed | tf_op | source)
XLA Modules:
  0.0 1123.9 jit_solution(2487775537268472293)
XLA Ops:
  9.2 16.5 %all_gather.30 = bf16[1152,128]{1,0:T(8,128)(2,1)} all-gather(bf16[144,128]{1,0:T(8,128)(2,1)S(1)} %reshape.358), channel_id=1, replica_groups=mesh['grp'=16,'seq'=8] {'seq'}, dimensions={0}, use_global_device_ids=true | all-gather | bytes 331776 | tf_op jit(solution)/shard_map/all_gather | solution.py:157
  28.8 51.6 %all-gather.13.cloned.1.call-done = bf16[18432,128]{1,0:T(8,128)(2,1)} async-done(((bf16[1152,128]{1,0:T(8,128)(2,1)}), bf16[18432,128]{1,0:T(8,128)(2,1)}) %all-gather.13.cloned.1.call-update) | async-done | bytes 4718608 | tf_op jit(solution)/shard_map/all_gather | solution.py:157
  80.4 8.2 reshape.359
  88.7 2.8 convolution_convert_fusion.7
  93.5 14.9 %all_gather.35 = bf16[1152,128]{1,0:T(8,128)(2,1)} all-gather(bf16[144,128]{1,0:T(8,128)(2,1)S(1)} %reshape.364), channel_id=1, replica_groups=mesh['grp'=16,'seq'=8] {'seq'}, dimensions={0}, use_global_device_ids=true | all-gather | bytes 331776 | tf_op jit(solution)/shard_map/all_gather | solution.py:157
  113.8 8.8 all-gather.15.cloned.1.call-done
  125.4 5.2 shard_map.204
  134.2 6.8 all-to-all-start
  141.1 42.4 %all-gather.17.cloned.1.call-done = bf16[18432,128]{1,0:T(8,128)(2,1)} async-done(((bf16[1152,128]{1,0:T(8,128)(2,1)}), bf16[18432,128]{1,0:T(8,128)(2,1)}) %all-gather.17.cloned.1.call-update) | async-done | bytes 4718608 | tf_op jit(solution)/shard_map/all_gather | solution.py:157
  183.5 8.2 reshape.365
  191.7 28.0 %all-gather.21.cloned.1.call-done = bf16[1,1,768,3072]{3,2,1,0:T(8,128)(2,1)} async-done(((bf16[1,1,96,3072]{3,2,1,0:T(8,128)(2,1)}), bf16[1,1,768,3072]{3,2,1,0:T(8,128)(2,1)}) %all-gather.21.cloned.1.call-update) | async-done | bytes 4718608 | tf_op jit(solution)/shard_map/all_gather | solution.py:162
  219.7 6.7 fusion.28
  226.4 29.8 %all-gather.23.cloned.1.call-done = bf16[1,1,3072,768]{3,2,1,0:T(8,128)(2,1)} async-done(((bf16[1,1,384,768]{3,2,1,0:T(8,128)(2,1)}), bf16[1,1,3072,768]{3,2,1,0:T(8,128)(2,1)}) %all-gather.23.cloned.1.call-update) | async-done | bytes 4718608 | tf_op jit(solution)/shard_map/all_gather | solution.py:163
  256.2 7.4 fusion.45
  263.7 6.6 all-to-all-start.1
  271.1 10.8 all-to-all-done.1
  281.8 2.4 multiply_reduce_fusion.3
  285.1 2.7 convolution_convert_fusion.6
  292.0 22.9 %all-gather.19.cloned.1.call-done = bf16[1024,1536]{1,0:T(8,128)(2,1)} async-done(((bf16[128,1536]{1,0:T(8,128)(2,1)}), bf16[1024,1536]{1,0:T(8,128)(2,1)}) %all-gather.19.cloned.1.call-update) | async-done | bytes 3145744 | tf_op jit(solution)/shard_map/all_gather | solution.py:234
  316.7 5.2 shard_map.205
  328.2 6.6 all-to-all-start.2
  338.3 8.1 all-to-all-done.2
  346.4 4.7 all-to-all-start.4
  351.1 6.8 fusion.20
  357.9 29.3 %all-gather.27.cloned.1.call-done = bf16[1,1,3072,768]{3,2,1,0:T(8,128)(2,1)} async-done(((bf16[1,1,384,768]{3,2,1,0:T(8,128)(2,1)}), bf16[1,1,3072,768]{3,2,1,0:T(8,128)(2,1)}) %all-gather.27.cloned.1.call-update) | async-done | bytes 4718608 | tf_op jit(solution)/shard_map/all_gather | solution.py:163
  387.2 8.2 fusion.13
  395.4 2.9 fusion.48
  398.3 6.6 all-to-all-start.5
  404.8 7.5 fusion.51
  412.3 4.1 all-to-all-done.5
  416.4 4.2 all-to-all-start.3
  420.9 2.2 fusion.130
  423.1 8.3 all-to-all-done.3
  439.1 8.1 shard_map.206
  451.3 30.2 %reduce-scatter.11.cloned.1.call-done = bf16[128,1536]{1,0:T(8,128)(2,1)} async-done(((bf16[1024,1536]{1,0:T(8,128)(2,1)}), bf16[128,1536]{1,0:T(8,128)(2,1)}) %reduce-scatter.11.cloned.1.call-update) | async-done | bytes 393232 | tf_op jit(solution)/shard_map/reduce_scatter | solution.py:305
  483.3 3.6 multiply_reduce_fusion.5
  489.4 16.1 %all_to_all.40 = bf16[16,24,768]{2,1,0:T(8,128)(2,1)S(1)} all-to-all(bf16[16,24,768]{2,1,0:T(8,128)(2,1)S(1)} %bitcast.174), channel_id=1, replica_groups=mesh['grp'=16,'seq'=8] {'grp'}, dimensions={0} | all-to-all | bytes 1179648 | tf_op jit(solution)/shard_map/all_to_all | solution.py:151
  505.5 8.1 fusion.6
  513.8 2.9 fusion.42
  516.6 4.3 all-to-all-start.7
  522.6 7.7 all-to-all-done.7
  535.3 8.2 shard_map.207
  547.5 2.2 convolution_convert_fusion.4
  549.7 2.8 pad_maximum_fusion.1
  552.5 8.3 reshape.385
  561.8 22.9 %reduce-scatter.13.cloned.1.call-done = bf16[128,1536]{1,0:T(8,128)(2,1)} async-done(((bf16[1024,1536]{1,0:T(8,128)(2,1)}), bf16[128,1536]{1,0:T(8,128)(2,1)}) %reduce-scatter.13.cloned.1.call-update) | async-done | bytes 393232 | tf_op jit(solution)/shard_map/reduce_scatter | solution.py:305
  587.0 2.8 pad_maximum_fusion
  589.8 8.3 reshape.384
  600.7 3.4 fusion.72
  605.0 7.6 convolution_convert_fusion
  613.6 7.6 convolution_convert_fusion.1
  621.5 6.7 convolution_convert_fusion.2
  628.2 6.8 convolution_convert_fusion.3
  635.1 31.7 %reduce-scatter.19.cloned.1.call-done = bf16[1152,128]{1,0:T(8,128)(2,1)} async-done(((bf16[18432,128]{1,0:T(8,128)(2,1)}), bf16[1152,128]{1,0:T(8,128)(2,1)}) %reduce-scatter.19.cloned.1.call-update) | async-done | bytes 294928 | tf_op jit(solution)/shard_map/reduce_scatter | solution.py:312
  667.9 80.0 %reduce-scatter.15.cloned.1.call-done = bf16[1152,128]{1,0:T(8,128)(2,1)} async-done(((bf16[18432,128]{1,0:T(8,128)(2,1)}), bf16[1152,128]{1,0:T(8,128)(2,1)}) %reduce-scatter.15.cloned.1.call-update) | async-done | bytes 294928 | tf_op jit(solution)/shard_map/reduce_scatter | solution.py:312
  747.8 145.1 %all-reduce.2.cloned.1.call-done = f32[2,14208]{1,0:T(2,128)} async-done(((f32[2,14208]{1,0:T(2,128)}), f32[2,14208]{1,0:T(2,128)}) %all-reduce.2.cloned.1.call-update) | async-done | bytes 113680 | tf_op jit(solution)/shard_map/psum | solution.py:318
  897.7 31.2 %reduce-scatter.29.cloned.1.call-done = bf16[384,768]{1,0:T(8,128)(2,1)} async-done(((bf16[3072,768]{1,0:T(8,128)(2,1)}), bf16[384,768]{1,0:T(8,128)(2,1)}) %reduce-scatter.29.cloned.1.call-update) | async-done | bytes 589840 | tf_op jit(solution)/shard_map/reduce_scatter | solution.py:283
  928.9 40.5 %reduce-scatter.27.cloned.1.call-done = bf16[384,768]{1,0:T(8,128)(2,1)} async-done(((bf16[3072,768]{1,0:T(8,128)(2,1)}), bf16[384,768]{1,0:T(8,128)(2,1)}) %reduce-scatter.27.cloned.1.call-update) | async-done | bytes 589840 | tf_op jit(solution)/shard_map/reduce_scatter | solution.py:283
  969.5 2.8 fusion.55
  972.3 37.9 %reduce-scatter.25.cloned.1.call-done = bf16[96,3072]{1,0:T(8,128)(2,1)} async-done(((bf16[768,3072]{1,0:T(8,128)(2,1)}), bf16[96,3072]{1,0:T(8,128)(2,1)}) %reduce-scatter.25.cloned.1.call-update) | async-done | bytes 589840 | tf_op jit(solution)/shard_map/reduce_scatter | solution.py:282
  1010.2 40.7 %reduce-scatter.23.cloned.1.call-done = bf16[96,3072]{1,0:T(8,128)(2,1)} async-done(((bf16[768,3072]{1,0:T(8,128)(2,1)}), bf16[96,3072]{1,0:T(8,128)(2,1)}) %reduce-scatter.23.cloned.1.call-update) | async-done | bytes 589840 | tf_op jit(solution)/shard_map/reduce_scatter | solution.py:282
  1050.8 2.8 fusion.54
  1053.6 29.4 %reduce-scatter.21.cloned.1.call-done = bf16[144,128]{1,0:T(8,128)(2,1)} async-done(((bf16[1152,128]{1,0:T(8,128)(2,1)}), bf16[144,128]{1,0:T(8,128)(2,1)}) %reduce-scatter.21.cloned.1.call-update) | async-done | bytes 36880 | tf_op jit(solution)/shard_map/reduce_scatter | solution.py:313
  1083.9 31.1 %reduce-scatter.17.cloned.1.call-done = bf16[144,128]{1,0:T(8,128)(2,1)} async-done(((bf16[1152,128]{1,0:T(8,128)(2,1)}), bf16[144,128]{1,0:T(8,128)(2,1)}) %reduce-scatter.17.cloned.1.call-update) | async-done | bytes 36880 | tf_op jit(solution)/shard_map/reduce_scatter | solution.py:313
  (318 shorter events, 79.5 us)
Async XLA Ops:
  7.2 73.3 %all-gather.13.cloned.1.call-start = ((), (), s32[]{:S(2)}) async-start(), calls=%async_computation.18 | async-start | bytes 5013504 | tf_op jit(solution)/shard_map/all_gather | solution.py:157
  25.7 97.0 %all-gather.15.cloned.1.call-start = ((), (), s32[]{:S(2)}) async-start(), calls=%async_computation.19 | async-start | bytes 3833856 | tf_op jit(solution)/shard_map/all_gather | solution.py:234
  26.5 62.2 %copy-start.35 = (f32[768]{0:T(1024)}, f32[768]{0:T(1024)S(1)}, u32[]{:S(2)}) copy-start(f32[768]{0:T(1024)S(1)} %get-tuple-element.73) | copy-start | bytes 9220
  26.5 258.4 %copy-start.37 = (f32[768]{0:T(1024)}, f32[768]{0:T(1024)S(1)}, u32[]{:S(2)}) copy-start(f32[768]{0:T(1024)S(1)} %get-tuple-element.72) | copy-start | bytes 9220
  28.8 59.9 %copy-start.63 = (f32[128]{0:T(128)}, f32[128]{0:T(128)S(1)}, u32[]{:S(2)}) copy-start(f32[128]{0:T(128)S(1)} %get-tuple-element.95) | copy-start | bytes 1540
  28.8 59.9 %copy-start.16 = (bf16[128,768]{1,0:T(8,128)(2,1)S(1)}, bf16[128,768]{1,0:T(8,128)(2,1)}, u32[]{:S(2)}) copy-start(bf16[128,768]{1,0:T(8,128)(2,1)} %param.13) | copy-start | bytes 589828
  88.7 19.8 %copy-start.18 = (bf16[2,1,96,3072]{3,2,1,0:T(8,128)(2,1)S(1)}, bf16[2,1,96,3072]{3,2,1,0:T(8,128)(2,1)}, u32[]{:S(2)}) copy-start(bf16[2,1,96,3072]{3,2,1,0:T(8,128)(2,1)} %param.23) | copy-start | bytes 3538948
  88.7 21.0 %copy-start.19 = (bf16[2,1,384,768]{3,2,1,0:T(8,128)(2,1)S(1)}, bf16[2,1,384,768]{3,2,1,0:T(8,128)(2,1)}, u32[]{:S(2)}) copy-start(bf16[2,1,384,768]{3,2,1,0:T(8,128)(2,1)} %param.24) | copy-start | bytes 3538948
  92.4 18.5 %copy-start.59 = (s32[1024]{0:T(1024)S(1)}, s32[1024]{0:T(1024)}, u32[]{:S(2)}) copy-start(s32[1024]{0:T(1024)} %param.15) | copy-start | bytes 12292
  92.4 19.3 %copy-start.60 = (bf16[2,768]{1,0:T(2,128)(2,1)S(1)}, bf16[2,768]{1,0:T(2,128)(2,1)}, u32[]{:S(2)}) copy-start(bf16[2,768]{1,0:T(2,128)(2,1)} %param.21) | copy-start | bytes 9220
  92.4 19.4 %copy-start.65 = (s32[128,2]{0,1:T(2,128)S(1)}, s32[128,2]{0,1:T(2,128)}, u32[]{:S(2)}) copy-start(s32[128,2]{0,1:T(2,128)} %param.16) | copy-start | bytes 3076
  92.4 20.2 %copy-start.45 = (bf16[2,32,12]{1,0,2:T(2,128)(2,1)S(1)}, bf16[2,32,12]{1,0,2:T(2,128)(2,1)}, u32[]{:S(2)}) copy-start(bf16[2,32,12]{1,0,2:T(2,128)(2,1)} %param.20) | copy-start | bytes 4612
  93.3 90.2 %all-gather.17.cloned.1.call-start = ((), (), s32[]{:S(2)}) async-start(), calls=%async_computation.20 | async-start | bytes 5013504 | tf_op jit(solution)/shard_map/all_gather | solution.py:157
  108.4 111.3 %all-gather.21.cloned.1.call-start = ((), (), s32[]{:S(2)}) async-start(), calls=%async_computation.33 | async-start | bytes 5308416 | tf_op jit(solution)/shard_map/all_gather | solution.py:162
  109.6 146.6 %all-gather.23.cloned.1.call-start = ((), (), s32[]{:S(2)}) async-start(), calls=%async_computation.34 | async-start | bytes 5308416 | tf_op jit(solution)/shard_map/all_gather | solution.py:163
  111.7 179.2 %copy-start.46 = (pred[768]{0:T(1024)(128)(4,1)}, pred[768]{0:T(1024)(128)(4,1)S(1)}, u32[]{:S(2)}) copy-start(pred[768]{0:T(1024)(128)(4,1)S(1)} %compare_and_fusion) | copy-start | bytes 2308
  112.4 20.5 %copy-start.32 = (f32[768]{0:T(1024)}, f32[768]{0:T(1024)S(1)}, u32[]{:S(2)}) copy-start(f32[768]{0:T(1024)S(1)} %get-tuple-element.71) | copy-start | bytes 9220
  112.6 28.3 %copy-start.39 = (s32[256]{0:T(256)}, s32[256]{0:T(256)S(1)}, u32[]{:S(2)}) copy-start(s32[256]{0:T(256)S(1)} %get-tuple-element.91) | copy-start | bytes 3076
  112.6 158.4 %copy-start.42 = (s32[2,128]{1,0:T(2,128)}, s32[2,128]{1,0:T(2,128)S(1)}, u32[]{:S(2)}) copy-start(s32[2,128]{1,0:T(2,128)S(1)} %get-tuple-element.90) | copy-start | bytes 3076
  112.9 20.2 %copy-start.14 = (bf16[384,128]{1,0:T(8,128)(2,1)}, bf16[384,128]{1,0:T(8,128)(2,1)S(1)}, u32[]{:S(2)}) copy-start(bf16[384,128]{1,0:T(8,128)(2,1)S(1)} %slice_add_fusion) | copy-start | bytes 294916
  132.3 151.9 %copy-start.4 = (f32[128,768]{1,0:T(8,128)}, f32[128,768]{1,0:T(8,128)S(1)}, u32[]{:S(2)}) copy-start(f32[128,768]{1,0:T(8,128)S(1)} %get-tuple-element.105) | copy-start | bytes 1179652
  132.9 58.8 %copy-start.53 = (f32[128]{0:T(128)}, f32[128]{0:T(128)S(1)}, u32[]{:S(2)}) copy-start(f32[128]{0:T(128)S(1)} %get-tuple-element.97) | copy-start | bytes 1540
  133.0 137.3 %copy-start.10 = (bf16[128,768]{1,0:T(8,128)(2,1)}, bf16[128,768]{1,0:T(8,128)(2,1)S(1)}, u32[]{:S(2)}) copy-start(bf16[128,768]{1,0:T(8,128)(2,1)S(1)} %multiply_convert_fusion.4) | copy-start | bytes 589828
  134.2 85.6 %all-to-all-start = ((bf16[16,24,768]{2,1,0:T(8,128)(2,1)}), bf16[16,24,768]{2,1,0:T(8,128)(2,1)}, u32[]{:S(2)}, u32[]{:S(2)}) async-start(bf16[16,24,768]{2,1,0:T(8,128)(2,1)} %bitcast.172), calls=%async_computation | async-start | bytes 1179648 | tf_op jit(solution)/shard_map/all_to_all | solution.py:151
  141.1 140.8 %copy-start.20 = (pred[256,384]{1,0:T(32,128)(4,1)}, pred[256,384]{1,0:T(32,128)(4,1)S(1)}, u32[]{:S(2)}) copy-start(pred[256,384]{1,0:T(32,128)(4,1)S(1)} %iota_compare_fusion.7) | copy-start | bytes 294916
  226.4 43.9 %copy-start.25 = (bf16[2,768,16]{1,2,0:T(8,128)(2,1)S(1)}, bf16[2,768,16]{1,2,0:T(8,128)(2,1)}, u32[]{:S(2)}) copy-start(bf16[2,768,16]{1,2,0:T(8,128)(2,1)} %param.22) | copy-start | bytes 147460
  263.7 18.2 %all-to-all-start.1 = ((bf16[16,24,768]{2,1,0:T(8,128)(2,1)}), bf16[16,24,768]{2,1,0:T(8,128)(2,1)}, u32[]{:S(2)}, u32[]{:S(2)}) async-start(bf16[16,24,768]{2,1,0:T(8,128)(2,1)} %bitcast.184), calls=%async_computation.1 | async-start | bytes 1179648 | tf_op jit(solution)/shard_map/all_to_all | solution.py:151
  270.2 44.7 %all-gather.19.cloned.1.call-start = ((), (), s32[]{:S(2)}) async-start(), calls=%async_computation.21 | async-start | bytes 3538944 | tf_op jit(solution)/shard_map/all_gather | solution.py:234
  270.5 19.6 %copy-start.55 = (f32[128]{0:T(128)}, f32[128]{0:T(128)S(1)}, u32[]{:S(2)}) copy-start(f32[128]{0:T(128)S(1)} %fusion.115) | copy-start | bytes 1540
  271.0 19.1 %copy-start.26 = (f32[128,16]{0,1:T(8,128)}, f32[128,16]{0,1:T(8,128)S(1)}, u32[]{:S(2)}) copy-start(f32[128,16]{0,1:T(8,128)S(1)} %fusion.114) | copy-start | bytes 24580
  271.1 19.1 %copy-start.49 = (f32[2,128]{1,0:T(2,128)}, f32[2,128]{1,0:T(2,128)S(1)}, u32[]{:S(2)}) copy-start(f32[2,128]{1,0:T(2,128)S(1)} %fusion.107) | copy-start | bytes 3076
  284.8 31.8 %copy-start.61 = (f32[128]{0:T(128)}, f32[128]{0:T(128)S(1)}, u32[]{:S(2)}) copy-start(f32[128]{0:T(128)S(1)} %get-tuple-element.99) | copy-start | bytes 1540
  289.4 61.7 %all-gather.25.cloned.1.call-start = ((), (), s32[]{:S(2)}) async-start(), calls=%async_computation.35 | async-start | bytes 5308416 | tf_op jit(solution)/shard_map/all_gather | solution.py:162
  290.2 35.3 %copy-start.34 = (f32[768]{0:T(1024)S(1)}, f32[768]{0:T(1024)}, u32[]{:S(2)}) copy-start(f32[768]{0:T(1024)} %get-tuple-element.70) | copy-start | bytes 9220
  290.2 97.0 %all-gather.27.cloned.1.call-start = ((), (), s32[]{:S(2)}) async-start(), calls=%async_computation.36 | async-start | bytes 5308416 | tf_op jit(solution)/shard_map/all_gather | solution.py:163
  292.0 44.0 %copy-start.43 = (s32[2,128]{1,0:T(2,128)S(1)}, s32[2,128]{1,0:T(2,128)}, u32[]{:S(2)}) copy-start(s32[2,128]{1,0:T(2,128)} %copy-done.42) | copy-start | bytes 3076
  316.7 20.5 %copy-start.40 = (s32[256]{0:T(256)S(1)}, s32[256]{0:T(256)}, u32[]{:S(2)}) copy-start(s32[256]{0:T(256)} %copy-done.39) | copy-start | bytes 3076
  328.2 18.2 %all-to-all-start.2 = ((bf16[16,24,768]{2,1,0:T(8,128)(2,1)}), bf16[16,24,768]{2,1,0:T(8,128)(2,1)}, u32[]{:S(2)}, u32[]{:S(2)}) async-start(bf16[16,24,768]{2,1,0:T(8,128)(2,1)} %bitcast.173), calls=%async_computation.2 | async-start | bytes 1179648 | tf_op jit(solution)/shard_map/all_to_all | solution.py:151
  336.0 97.2 %copy-start.28 = (f32[128,16]{0,1:T(8,128)}, f32[128,16]{0,1:T(8,128)S(1)}, u32[]{:S(2)}) copy-start(f32[128,16]{0,1:T(8,128)S(1)} %fusion.116) | copy-start | bytes 24580
  346.4 40.7 %all-to-all-start.4 = ((bf16[16,24,768]{2,1,0:T(8,128)(2,1)}), bf16[16,24,768]{2,1,0:T(8,128)(2,1)}, u32[]{:S(2)}, u32[]{:S(2)}) async-start(bf16[16,24,768]{2,1,0:T(8,128)(2,1)} %bitcast.171), calls=%async_computation.4 | async-start | bytes 1179648 | tf_op jit(solution)/shard_map/all_to_all | solution.py:151
  398.3 18.2 %all-to-all-start.5 = ((bf16[16,24,768]{2,1,0:T(8,128)(2,1)}), bf16[16,24,768]{2,1,0:T(8,128)(2,1)}, u32[]{:S(2)}, u32[]{:S(2)}) async-start(bf16[16,24,768]{2,1,0:T(8,128)(2,1)} %bitcast.186), calls=%async_computation.5 | async-start | bytes 1179648 | tf_op jit(solution)/shard_map/all_to_all | solution.py:151
  416.4 14.9 %all-to-all-start.3 = ((bf16[16,24,768]{2,1,0:T(8,128)(2,1)}), bf16[16,24,768]{2,1,0:T(8,128)(2,1)}, u32[]{:S(2)}, u32[]{:S(2)}) async-start(bf16[16,24,768]{2,1,0:T(8,128)(2,1)} %bitcast.185), calls=%async_computation.3 | async-start | bytes 1179648 | tf_op jit(solution)/shard_map/all_to_all | solution.py:151
  420.7 60.8 %reduce-scatter.11.cloned.1.call-start = ((), (), s32[]{:S(2)}) async-start(), calls=%async_computation.22 | async-start | bytes 3538944 | tf_op jit(solution)/shard_map/reduce_scatter | solution.py:305
  449.1 34.2 %copy-start.38 = (f32[768]{0:T(1024)S(1)}, f32[768]{0:T(1024)}, u32[]{:S(2)}) copy-start(f32[768]{0:T(1024)} %copy-done.37) | copy-start | bytes 9220
  449.1 34.2 %copy-start.62 = (f32[128]{0:T(128)S(1)}, f32[128]{0:T(128)}, u32[]{:S(2)}) copy-start(f32[128]{0:T(128)} %copy-done.61) | copy-start | bytes 1540
  450.5 36.4 %copy-start.67 = (f32[128]{0:T(128)S(1)}, f32[128]{0:T(128)}, u32[]{:S(2)}) copy-start(f32[128]{0:T(128)} %get-tuple-element.98) | copy-start | bytes 1540
  450.6 38.4 %copy-start.50 = (f32[2,128]{1,0:T(2,128)S(1)}, f32[2,128]{1,0:T(2,128)}, u32[]{:S(2)}) copy-start(f32[2,128]{1,0:T(2,128)} %copy-done.49) | copy-start | bytes 3076
  450.6 38.5 %copy-start.41 = (s32[256]{0:T(256)S(1)}, s32[256]{0:T(256)}, u32[]{:S(2)}) copy-start(s32[256]{0:T(256)} %copy-done.39) | copy-start | bytes 3076
  489.0 24.7 %slice-start = ((s8[4718592]{0:T(1024)(128)(4,1)}), s8[4194304]{0:T(1024)(128)(4,1)S(1)}, s32[]{:S(2)}) async-start(s8[4718592]{0:T(1024)(128)(4,1)} %bitcast.189), calls=%async_computation.37 | async-start | bytes 8388608
  516.6 13.6 %all-to-all-start.7 = ((bf16[16,24,768]{2,1,0:T(8,128)(2,1)}), bf16[16,24,768]{2,1,0:T(8,128)(2,1)}, u32[]{:S(2)}, u32[]{:S(2)}) async-start(bf16[16,24,768]{2,1,0:T(8,128)(2,1)} %bitcast.183), calls=%async_computation.8 | async-start | bytes 1179648 | tf_op jit(solution)/shard_map/all_to_all | solution.py:151
  520.9 63.8 %reduce-scatter.13.cloned.1.call-start = ((), (), s32[]{:S(2)}) async-start(), calls=%async_computation.23 | async-start | bytes 3538944 | tf_op jit(solution)/shard_map/reduce_scatter | solution.py:305
  546.9 119.9 %reduce-scatter.19.cloned.1.call-start = ((), (), s32[]{:S(2)}) async-start(), calls=%async_computation.27 | async-start | bytes 5013504 | tf_op jit(solution)/shard_map/reduce_scatter | solution.py:312
  560.8 24.9 %copy-start.17 = (bf16[128,768]{1,0:T(8,128)(2,1)S(1)}, bf16[128,768]{1,0:T(8,128)(2,1)}, u32[]{:S(2)}) copy-start(bf16[128,768]{1,0:T(8,128)(2,1)} %param.13) | copy-start | bytes 589828
  560.8 25.0 %copy-start.36 = (f32[768]{0:T(1024)S(1)}, f32[768]{0:T(1024)}, u32[]{:S(2)}) copy-start(f32[768]{0:T(1024)} %copy-done.35) | copy-start | bytes 9220
  560.8 25.0 %copy-start.64 = (f32[128]{0:T(128)S(1)}, f32[128]{0:T(128)}, u32[]{:S(2)}) copy-start(f32[128]{0:T(128)} %copy-done.63) | copy-start | bytes 1540
  560.8 187.0 %reduce-scatter.15.cloned.1.call-start = ((), (), s32[]{:S(2)}) async-start(), calls=%async_computation.25 | async-start | bytes 5013504 | tf_op jit(solution)/shard_map/reduce_scatter | solution.py:312
  598.1 294.8 %all-reduce.2.cloned.1.call-start = ((), (), s32[]{:S(2)}) async-start(), calls=%async_computation.24 | async-start | bytes 227328 | tf_op jit(solution)/shard_map/psum | solution.py:318
  604.9 324.0 %reduce-scatter.29.cloned.1.call-start = ((), (), s32[]{:S(2)}) async-start(), calls=%async_computation.32 | async-start | bytes 5308416 | tf_op jit(solution)/shard_map/reduce_scatter | solution.py:283
  612.6 356.9 %reduce-scatter.27.cloned.1.call-start = ((), (), s32[]{:S(2)}) async-start(), calls=%async_computation.31 | async-start | bytes 5308416 | tf_op jit(solution)/shard_map/reduce_scatter | solution.py:283
  621.3 388.9 %reduce-scatter.25.cloned.1.call-start = ((), (), s32[]{:S(2)}) async-start(), calls=%async_computation.30 | async-start | bytes 5308416 | tf_op jit(solution)/shard_map/reduce_scatter | solution.py:282
  628.2 422.6 %reduce-scatter.23.cloned.1.call-start = ((), (), s32[]{:S(2)}) async-start(), calls=%async_computation.29 | async-start | bytes 5308416 | tf_op jit(solution)/shard_map/reduce_scatter | solution.py:282
  635.0 31.9 %copy-start.68 = (f32[128]{0:T(128)S(1)}, f32[128]{0:T(128)}, u32[]{:S(2)}) copy-start(f32[128]{0:T(128)} %get-tuple-element.94) | copy-start | bytes 1540
  635.1 448.0 %reduce-scatter.21.cloned.1.call-start = ((), (), s32[]{:S(2)}) async-start(), calls=%async_computation.28 | async-start | bytes 331776 | tf_op jit(solution)/shard_map/reduce_scatter | solution.py:313
  666.9 448.1 %reduce-scatter.17.cloned.1.call-start = ((), (), s32[]{:S(2)}) async-start(), calls=%async_computation.26 | async-start | bytes 331776 | tf_op jit(solution)/shard_map/reduce_scatter | solution.py:313
  (36 other events, 218.4 us)
Sparse Core Ops, SparseCore 0:
  25.8 54.5 all-gather.12
  93.4 29.1 all-gather.14
  124.8 58.6 all-gather.16
  185.0 34.6 all-gather.20
  221.8 34.3 all-gather.22
  289.5 25.3 all-gather.18
  316.6 34.4 all-gather.24
  352.8 34.3 all-gather.26
  450.7 30.7 reduce-scatter.10
  547.0 37.6 reduce-scatter.12
  588.1 78.7 reduce-scatter.18
  670.0 77.7 reduce-scatter.14
  752.6 140.2 all-reduce.1
  895.3 33.5 reduce-scatter.28
  931.3 38.0 reduce-scatter.26
  971.9 38.2 reduce-scatter.24
  1012.5 38.2 reduce-scatter.22
  1053.2 29.8 reduce-scatter.20
  1085.4 29.4 reduce-scatter.16

commit v2 on v1

--- a/solution.py
+++ b/solution.py
@@ -49,6 +49,11 @@
     return q_head, mine, jnp.where(allowed, scores + bias, MASKED)
 
 
+def first_key_block():
+    me = lax.axis_index("seq")
+    return me // BACK * (me % BACK)
+
+
 def allowed_pairs(off_ref, segq_ref, segk_ref, rows, width):
     i = lax.broadcasted_iota(jnp.int32, (rows, width), 0)
     j = lax.broadcasted_iota(jnp.int32, (rows, width), 1)
@@ -56,15 +61,17 @@
 
 
 def attention_kernel(off_ref, q_ref, kv_ref, segq_ref, segk_ref, bias_ref, out_ref, lse_ref):
-    rows, width, span = q_ref.shape[0], kv_ref.shape[0], bias_ref.shape[1]
+    rows, width, span = q_ref.shape[0], segk_ref.shape[1], bias_ref.shape[1]
+    first = first_key_block()
+    window = pl.ds(pl.multiple_of(first * rows, rows), width)
     allowed = allowed_pairs(off_ref, segq_ref, segk_ref, rows, width)
     low_lanes = lax.broadcasted_iota(jnp.int32, (rows, 128), 1) < HEAD_DIM
     lane = lax.broadcasted_iota(jnp.int32, (rows, 128), 1)
     totals = jnp.zeros((rows, 128), F32)
     for pair in range(PAIRS):
         at = slice(pair * 128, pair * 128 + 128)
-        q2, k2 = q_ref[:, at], kv_ref[:, at]
-        v2 = kv_ref[:, D + pair * 128 : D + pair * 128 + 128]
+        q2, k2 = q_ref[:, at], kv_ref[window, at]
+        v2 = kv_ref[window, D + pair * 128 : D + pair * 128 + 128]
         both = []
         for head in (2 * pair, 2 * pair + 1):
             _, _, scores = head_scores(q2, k2, low_lanes, head, allowed, bias_ref, width, span)
@@ -81,17 +88,20 @@
 def attention_back_kernel(
     off_ref, q_ref, kv_ref, segq_ref, segk_ref, bias_ref, lse_ref, grad_ref, dq_ref, dkv_ref, diag_ref
 ):
-    rows, width, span = q_ref.shape[0], kv_ref.shape[0], bias_ref.shape[1]
+    rows, width, span = q_ref.shape[0], segk_ref.shape[1], bias_ref.shape[1]
+    first = first_key_block()
+    window = pl.ds(pl.multiple_of(first * rows, rows), width)
     allowed = allowed_pairs(off_ref, segq_ref, segk_ref, rows, width)
     low_lanes = lax.broadcasted_iota(jnp.int32, (rows, 128), 1) < HEAD_DIM
     lane = lax.broadcasted_iota(jnp.int32, (rows, 128), 1)
     i = lax.broadcasted_iota(jnp.int32, (rows, rows), 0)
     j = lax.broadcasted_iota(jnp.int32, (rows, rows), 1)
     flip = (i + j == rows - 1).astype(BF)
+    dkv_ref[...] = jnp.zeros_like(dkv_ref)
     for pair in range(PAIRS):
         at = slice(pair * 128, pair * 128 + 128)
         at_v = slice(D + pair * 128, D + pair * 128 + 128)
-        q2, k2, v2, g2 = q_ref[:, at], kv_ref[:, at], kv_ref[:, at_v], grad_ref[:, at]
+        q2, k2, v2, g2 = q_ref[:, at], kv_ref[window, at], kv_ref[window, at_v], grad_ref[:, at]
         dq, dk, dv = [], None, None
         for head in (2 * pair, 2 * pair + 1):
             q_head, mine, scores = head_scores(q2, k2, low_lanes, head, allowed, bias_ref, width, span)
@@ -112,8 +122,9 @@
             turned = pltpu.roll(turned, span - (rows - 1), 1, stride=1, stride_axis=0)
             diag_ref[head : head + 1, :] = jnp.sum(turned, axis=0, keepdims=True)
         dq_ref[:, at] = (jnp.where(low_lanes, dq[0], dq[1]) * SCALE).astype(BF)
-        dkv_ref[:, at] = (dk * SCALE).astype(BF)
-        dkv_ref[:, at_v] = dv.astype(BF)
+        blocks = pl.ds(first, width // rows)
+        dkv_ref[blocks, :, at] = (dk * SCALE).astype(BF).reshape(-1, rows, 128)
+        dkv_ref[blocks, :, at_v] = dv.astype(BF).reshape(-1, rows, 128)
 
 
 def vmem_specs(n):
@@ -138,7 +149,7 @@
         attention_back_kernel,
         out_shape=(
             jax.ShapeDtypeStruct(queries.shape, BF),
-            jax.ShapeDtypeStruct(kv.shape, BF),
+            jax.ShapeDtypeStruct((kv.shape[0] // queries.shape[0], queries.shape[0], kv.shape[1]), BF),
             jax.ShapeDtypeStruct(bias.shape, F32),
         ),
         in_specs=[pl.BlockSpec(memory_space=pltpu.SMEM)] + vmem_specs(7),
@@ -147,15 +158,397 @@
     )(off, queries, kv, segq, segk, bias, lse, grad)
 
 
+MESH_ID = pl.DeviceIdType.MESH
+SIDE = 4
+
+
+def place_of_device():
+    grp, seq = lax.axis_index("grp"), lax.axis_index("seq")
+    return [grp // SIDE, grp % SIDE, seq // 2], seq % 2
+
+
+def device_at(coords, core):
+    return (coords[0] * SIDE + coords[1], coords[2] * 2 + core)
+
+
+def moved(coords, axis, delta):
+    return [(c + delta) % SIDE if a == axis else c for a, c in enumerate(coords)]
+
+
+def remote(src, dst, send_sem, recv_sem, device):
+    return pltpu.make_async_remote_copy(
+        src_ref=src, dst_ref=dst, send_sem=send_sem, recv_sem=recv_sem, device_id=device, device_id_type=MESH_ID
+    )
+
+
+def greet(devices):
+    barrier = pltpu.get_barrier_semaphore()
+    for device in devices:
+        pl.semaphore_signal(barrier, inc=1, device_id=device, device_id_type=MESH_ID)
+    pl.semaphore_wait(barrier, len(devices))
+
+
+def all_partners(coords, core):
+    partners = [device_at(moved(coords, a, d), core) for a in range(3) for d in range(1, SIDE)]
+    return partners + [device_at(coords, 1 - core)]
+
+
+def attn_gather_kernel(own_ref, seg_ref, full_ref, segs_ref, send_sem, recv_sem, core_send, core_recv, seg_send, seg_recv):
+    coords, core = place_of_device()
+    sibling = device_at(coords, 1 - core)
+    y, x, z = coords
+    for p in range(3):
+        full_ref[p, y, x, z, core] = own_ref[p]
+    segs_ref[z, core] = seg_ref[...]
+    greet(all_partners(coords, core))
+
+    def region(p, free, fixed=None):
+        index = [slice(None) if a in free else coords[a] for a in range(3)]
+        if fixed is not None:
+            index[fixed[0]] = fixed[1]
+        return full_ref.at[(p, *index, core)]
+
+    seg_copies = []
+    for d in range(1, SIDE):
+        one = segs_ref.at[z, core]
+        seg_copies.append(remote(one, one, seg_send.at[d - 1], seg_recv.at[d - 1], device_at(moved(coords, 2, d), core)))
+        seg_copies[-1].start()
+    copies = {}
+    core_copies = []
+
+    def to_sibling(part, number):
+        core_copies.append(remote(part, part, core_send.at[number], core_recv.at[number], sibling))
+        core_copies[-1].start()
+
+    for k in range(3):
+        for p in range(3):
+            if k:
+                for d in (1, 3, 2):
+                    copies[k - 1, p, d].wait_recv()
+            axis, free = (p + k) % 3, [(p + i) % 3 for i in range(k)]
+            part = region(p, free)
+            for d in (1, 3, 2):
+                copies[k, p, d] = remote(
+                    part, part, send_sem.at[k, p, d - 1], recv_sem.at[k, p, d - 1],
+                    device_at(moved(coords, axis, d), core),
+                )
+                copies[k, p, d].start()
+            if k == 2:
+                to_sibling(part, 4 * p)
+    for copy in seg_copies:
+        copy.wait_recv()
+    part = segs_ref.at[:, core]
+    seg_last = remote(part, part, seg_send.at[3], seg_recv.at[3], sibling)
+    seg_last.start()
+    for d in (1, 3, 2):
+        for p in range(3):
+            axis = (p + 2) % 3
+            copies[2, p, d].wait_recv()
+            came = (coords[axis] + SIDE - d) % SIDE
+            to_sibling(region(p, [a for a in range(3) if a != axis], (axis, came)), 4 * p + d)
+    for copy in copies.values():
+        copy.wait_send()
+    for copy in seg_copies:
+        copy.wait_send()
+    seg_last.wait()
+    for copy in core_copies:
+        copy.wait()
+
+
+def attn_gather(own, seg):
+    sems = [pltpu.SemaphoreType.DMA((3, 3, 3))] * 2 + [pltpu.SemaphoreType.DMA((12,))] * 2
+    sems += [pltpu.SemaphoreType.DMA((4,))] * 2
+    return pl.pallas_call(
+        attn_gather_kernel,
+        out_shape=(
+            jax.ShapeDtypeStruct((3, SIDE, SIDE, SIDE, 2) + own.shape[1:], BF),
+            jax.ShapeDtypeStruct((SIDE, 2) + seg.shape, F32),
+        ),
+        in_specs=vmem_specs(2),
+        out_specs=tuple(vmem_specs(2)),
+        scratch_shapes=sems,
+        compiler_params=pltpu.CompilerParams(
+            collective_id=0, has_side_effects=True, vmem_limit_bytes=40 * 2**20
+        ),
+    )(own, seg)
+
+
+def reduce_kernel(
+    x_ref, small_ref, out_ref, small_out, got_core, y_ref, got_one, z_ref, got_two, w_ref, got_three,
+    s_core, s_got, core_send, core_recv, send_sem, recv_sem, s_core_send, s_core_recv, s_send, s_recv,
+):
+    coords, core = place_of_device()
+    sibling = device_at(coords, 1 - core)
+    greet(all_partners(coords, core))
+    first = []
+    for p in range(3):
+        copy = remote(
+            x_ref.at[p, :, :, :, 1 - core], got_core.at[p], core_send.at[p], core_recv.at[p], sibling
+        )
+        copy.start()
+        first.append(copy)
+    s_first = remote(small_ref, s_core, s_core_send, s_core_recv, sibling)
+    s_first.start()
+
+    def spread(p, k, source, target):
+        axis = (p + k) % 3
+        left = [a for a in range(3) if a not in [(p + i) % 3 for i in range(k)]]
+        out = []
+        for d in (1, 3, 2):
+            to = moved(coords, axis, d)
+            index = tuple(to[axis] if a == axis else slice(None) for a in left)
+            copy = remote(
+                source.at[(p, *index)], target.at[p, d - 1], send_sem.at[k, p, d - 1], recv_sem.at[k, p, d - 1],
+                device_at(to, core),
+            )
+            copy.start()
+            out.append(copy)
+        return out
+
+    def spread_small(p, k):
+        axis, out = (p + k) % 3, []
+        for d in (1, 3, 2):
+            copy = remote(
+                s_got.at[k, p, 0], s_got.at[k, p, d], s_send.at[k, p, d - 1], s_recv.at[k, p, d - 1],
+                device_at(moved(coords, axis, d), core),
+            )
+            copy.start()
+            out.append(copy)
+        return out
+
+    def small_sum(p, k):
+        axis = (p + k) % 3
+        total = s_got[k, p, coords[axis]]
+        for v in range(1, SIDE):
+            total = total + s_got[k, p, (coords[axis] + SIDE - v) % SIDE]
+        return total
+
+    sent, s_sent = {}, {}
+    s_first.wait()
+    for p in range(3):
+        s_got[0, p, 0] = small_ref[p] + s_core[p]
+        s_sent[0, p] = spread_small(p, 0)
+    for p in range(3):
+        first[p].wait()
+
+        def add_core(i, carry, p=p):
+            a, b, c = i // (SIDE * SIDE), i // SIDE % SIDE, i % SIDE
+            total = x_ref[p, a, b, c, core].astype(F32) + got_core[p, a, b, c].astype(F32)
+            y_ref[p, a, b, c] = total.astype(BF)
+            return carry
+
+        lax.fori_loop(0, SIDE**3, add_core, 0)
+        sent[0, p] = spread(p, 0, y_ref, got_one)
+    for p in range(3):
+        for copy in s_sent[0, p]:
+            copy.wait()
+        s_got[1, p, 0] = small_sum(p, 0)
+        s_sent[1, p] = spread_small(p, 1)
+    for p in range(3):
+        for copy in sent[0, p]:
+            copy.wait()
+        axis = p
+
+        def add_one(i, carry, p=p, axis=axis):
+            a, b = i // SIDE, i % SIDE
+            index = [a, b]
+            index.insert(axis, coords[axis])
+            total = y_ref[(p, *index)].astype(F32)
+            for d in range(3):
+                total = total + got_one[p, d, a, b].astype(F32)
+            z_ref[p, a, b] = total.astype(BF)
+            return carry
+
+        lax.fori_loop(0, SIDE**2, add_one, 0)
+        sent[1, p] = spread(p, 1, z_ref, got_two)
+    for p in range(3):
+        for copy in s_sent[1, p]:
+            copy.wait()
+        s_got[2, p, 0] = small_sum(p, 1)
+        s_sent[2, p] = spread_small(p, 2)
+    for p in range(3):
+        for copy in sent[1, p]:
+            copy.wait()
+        axis = (p + 1) % 3
+        left = [a for a in range(3) if a != p]
+
+        def add_two(i, carry, p=p, axis=axis, left=left):
+            index = tuple(coords[axis] if a == axis else i for a in left)
+            total = z_ref[(p, *index)].astype(F32)
+            for d in range(3):
+                total = total + got_two[p, d, i].astype(F32)
+            w_ref[p, i] = total.astype(BF)
+            return carry
+
+        lax.fori_loop(0, SIDE, add_two, 0)
+        sent[2, p] = spread(p, 2, w_ref, got_three)
+    for p in range(3):
+        for copy in s_sent[2, p]:
+            copy.wait()
+        small_out[p] = small_sum(p, 2)
+    for p in range(3):
+        for copy in sent[2, p]:
+            copy.wait()
+        total = w_ref[p, coords[(p + 2) % 3]].astype(F32)
+        for d in range(3):
+            total = total + got_three[p, d].astype(F32)
+        out_ref[p] = total
+
+
+def reduce_all(x, small):
+    block, part = x.shape[-2:], small.shape[1:]
+    dma = pltpu.SemaphoreType.DMA
+    return pl.pallas_call(
+        reduce_kernel,
+        out_shape=(jax.ShapeDtypeStruct((3,) + block, F32), jax.ShapeDtypeStruct(small.shape, F32)),
+        in_specs=vmem_specs(2),
+        out_specs=tuple(vmem_specs(2)),
+        scratch_shapes=[
+            VMEM((3, SIDE, SIDE, SIDE) + block, BF),
+            VMEM((3, SIDE, SIDE, SIDE) + block, BF),
+            VMEM((3, 3, SIDE, SIDE) + block, BF),
+            VMEM((3, SIDE, SIDE) + block, BF),
+            VMEM((3, 3, SIDE) + block, BF),
+            VMEM((3, SIDE) + block, BF),
+            VMEM((3, 3) + block, BF),
+            VMEM(small.shape, F32),
+            VMEM((3, 3, SIDE) + part, F32),
+            dma((3,)), dma((3,)), dma((3, 3, 3)), dma((3, 3, 3)), dma(()), dma(()), dma((3, 3, 3)), dma((3, 3, 3)),
+        ],
+        compiler_params=pltpu.CompilerParams(
+            collective_id=1, has_side_effects=True, vmem_limit_bytes=50 * 2**20
+        ),
+    )(x, small)
+
+
+def kv_gather(own_ref, kv_ref, send_sem, recv_sem):
+    coords, core = place_of_device()
+    z, rows = coords[2], own_ref.shape[0]
+    half = rows // 2
+    up, down = moved(coords, 2, 1), moved(coords, 2, 3)
+    up_z, down_z, far_z = (z + 1) % SIDE, (z + 3) % SIDE, (z + 2) % SIDE
+    sibling = device_at(coords, 1 - core)
+
+    def block(at, start=0, size=rows):
+        return kv_ref.at[pl.ds(pl.multiple_of((at * 2 + core) * rows + start, half), size)]
+
+    copies = []
+
+    def send(part, number, device):
+        copy = remote(part, part, send_sem.at[number], recv_sem.at[number], device)
+        copy.start()
+        copies.append(copy)
+        return copy
+
+    kv_ref[pl.ds(pl.multiple_of((z * 2 + core) * rows, rows), rows), :] = own_ref[...]
+    greet([device_at(up, core), device_at(down, core), sibling])
+    went_up = send(block(z), 0, device_at(up, core))
+    went_down = send(block(z), 1, device_at(down, core))
+    from_core = [send(block(z), 2, sibling)]
+    went_up.wait_recv()
+    far_up = send(block(down_z, 0, half), 3, device_at(up, core))
+    from_core.append(send(block(down_z), 4, sibling))
+    went_down.wait_recv()
+    far_down = send(block(up_z, half, half), 5, device_at(down, core))
+    from_core.append(send(block(up_z), 6, sibling))
+    far_up.wait_recv()
+    from_core.append(send(block(far_z, 0, half), 7, sibling))
+    far_down.wait_recv()
+    from_core.append(send(block(far_z, half, half), 8, sibling))
+    for copy in from_core:
+        copy.wait_recv()
+    for copy in copies:
+        copy.wait_send()
+
+
+def kv_scatter(grads_ref, out_ref, got_core, sums, got_far, got_near, send_sem, recv_sem):
+    coords, core = place_of_device()
+    z, rows = coords[2], out_ref.shape[0]
+    half = rows // 2
+    up, down = device_at(moved(coords, 2, 1), core), device_at(moved(coords, 2, 3), core)
+    up_z, down_z, far_z = (z + 1) % SIDE, (z + 3) % SIDE, (z + 2) % SIDE
+    sibling = device_at(coords, 1 - core)
+    greet([up, down, sibling])
+    copies = []
+
+    def send(src, dst, number, device):
+        copy = remote(src, dst, send_sem.at[number], recv_sem.at[number], device)
+        copy.start()
+        copies.append(copy)
+        return copy
+
+    order = [far_z, up_z, down_z, z]
+    cross = [send(grads_ref.at[at * 2 + 1 - core], got_core.at[n], n, sibling) for n, at in enumerate(order)]
+
+    def total(n):
+        cross[n].wait_recv()
+        return grads_ref[order[n] * 2 + core].astype(F32) + got_core[n].astype(F32)
+
+    sums[0] = total(0).astype(BF)
+    far_up = send(sums.at[0, pl.ds(0, half)], got_far.at[0], 4, up)
+    far_down = send(sums.at[0, pl.ds(half, half)], got_far.at[1], 5, down)
+    up_sum, down_sum = total(1), total(2)
+    sums[1, half:] = up_sum[half:].astype(BF)
+    sums[2, :half] = down_sum[:half].astype(BF)
+    far_up.wait_recv()
+    sums[1, :half] = (up_sum[:half] + got_far[0].astype(F32)).astype(BF)
+    near_up = send(sums.at[1], got_near.at[0], 6, up)
+    far_down.wait_recv()
+    sums[2, half:] = (down_sum[half:] + got_far[1].astype(F32)).astype(BF)
+    near_down = send(sums.at[2], got_near.at[1], 7, down)
+    own = total(3)
+    near_up.wait_recv()
+    near_down.wait_recv()
+    out_ref[...] = (own + got_near[0].astype(F32) + got_near[1].astype(F32)).astype(BF)
+    for copy in copies:
+        copy.wait_send()
+
+def gather_keys(own):
+    return pl.pallas_call(
+        kv_gather,
+        out_shape=jax.ShapeDtypeStruct((2 * SIDE * own.shape[0], own.shape[1]), BF),
+        in_specs=vmem_specs(1),
+        out_specs=vmem_specs(1)[0],
+        scratch_shapes=[pltpu.SemaphoreType.DMA((9,))] * 2,
+        compiler_params=pltpu.CompilerParams(
+            collective_id=2, has_side_effects=True, vmem_limit_bytes=20 * 2**20
+        ),
+    )(own)
+
+
+def scatter_key_grads(grads):
+    block = grads.shape[1:]
+    return pl.pallas_call(
+        kv_scatter,
+        out_shape=jax.ShapeDtypeStruct(block, BF),
+        in_specs=vmem_specs(1),
+        out_specs=vmem_specs(1)[0],
+        scratch_shapes=[
+            VMEM((SIDE,) + block, BF),
+            VMEM((3,) + block, BF),
+            VMEM((2, block[0] // 2, block[1]), BF),
+            VMEM((2,) + block, BF),
+            pltpu.SemaphoreType.DMA((8,)),
+            pltpu.SemaphoreType.DMA((8,)),
+        ],
+        compiler_params=pltpu.CompilerParams(
+            collective_id=3, has_side_effects=True, vmem_limit_bytes=20 * 2**20
+        ),
+    )(grads)
+
+
 def to_peers(rows):
     return lax.all_to_all(rows, "grp", split_axis=0, concat_axis=0, tiled=True)
 
 
-def gather_attn(wqkv, wout, layer_index):
-    own = jnp.concatenate([wqkv[layer_index], wout[layer_index]], axis=1)
-    own = own.reshape(-1, 128)
-    full = lax.all_gather(lax.all_gather(own, "seq", axis=0, tiled=True), "grp", axis=0, tiled=True)
-    return full.reshape(D, -1)
+def gather_attn(wqkv, wout, segments):
+    layers, shard = wqkv.shape[0], wqkv.shape[1]
+    own = jnp.concatenate([wqkv, wout], axis=2).reshape(3, -1, 128)
+    seg = jnp.broadcast_to(segments.astype(F32), (8, segments.shape[1]))
+    full, segs = attn_gather(own, seg)
+    full = full.reshape(3, 2 * SIDE**3, -1, 128).transpose(1, 0, 2, 3)
+    full = full.reshape(2 * SIDE**3, layers, shard, -1).transpose(1, 0, 2, 3)
+    return full.reshape(layers, 2 * SIDE**3 * shard, -1), segs[:, :, 0].reshape(1, -1)
 
 
 def gather_experts(w_in, w_out, layer_index):
@@ -181,13 +574,11 @@
 ):
     count_q = tokens.shape[0]
     experts = lax.axis_size("grp")
-    blocks = lax.axis_size("seq")
     capacity = max(2, 3 * count_q * TOP // (2 * experts))
     window = (BACK + 1) * count_q
     span = window + count_q
     me = lax.axis_index("seq")
-    first_block = jnp.clip(me - BACK, 0, blocks - BACK - 1)
-    start = first_block * count_q
+    start = first_key_block() * count_q
     off = (me * count_q - start).astype(jnp.int32)
 
     place = jnp.arange(span, dtype=jnp.int32)
@@ -217,8 +608,8 @@
     hidden_state = tokens.astype(F32)
     gains_a, gains_f = gain_attn.astype(F32), gain_ffn.astype(F32)
     stored = []
-    seg_keys = None
-    attn_full = [gather_attn(wqkv, wout, l) for l in range(LAYERS)]
+    attn_full, segs = gather_attn(wqkv, wout, segments)
+    seg_keys = lax.dynamic_slice_in_dim(segs, start, window, axis=1)
     expert_full = [gather_experts(w_in, w_out, l) for l in range(LAYERS)]
     for l in range(LAYERS):
         qkv_mat, out_mat = attn_full[l][:, : 3 * D], attn_full[l][:, 3 * D :]
@@ -228,14 +619,7 @@
         projected = dot(normed, qkv_mat).astype(BF)
         queries = projected[:, :D]
         kv_own = projected[:, D:]
-        if l == 0:
-            tail = jnp.broadcast_to(seg_col, (count_q, 128)).astype(BF)
-            kv_own = jnp.concatenate([kv_own, tail], axis=1)
-        kv = lax.all_gather(kv_own, "seq", axis=0, tiled=True)
-        kv = lax.dynamic_slice_in_dim(kv, start, window, axis=0)
-        if l == 0:
-            seg_keys = kv[:, 2 * D].astype(F32)[None, :]
-            kv = kv[:, : 2 * D]
+        kv = gather_keys(kv_own)
         off_arr = off.reshape(1)
         attended, lse = attention(off_arr, queries, kv, seg_col, seg_keys, bias_rows[l])
         middle = hidden_state + dot(attended, out_mat)
@@ -299,28 +683,29 @@
         table_grad = lax.dot_general(
             bucket_hot.astype(F32), diag, (((1,), (1,)), ((), ())), precision=highest
         )
-        dkv_all = lax.dynamic_update_slice_in_dim(
-            jnp.zeros((blocks * count_q, 2 * D), BF), dkv, start, axis=0
-        )
-        dkv_own = lax.psum_scatter(dkv_all, "seq", scatter_dimension=0, tiled=True)
+        dkv_own = scatter_key_grads(dkv)
         grad_proj = jnp.concatenate([dq, dkv_own], axis=1)
         grad_in_proj = dot(normed, grad_proj, ((0,), (0,))).astype(BF)
         grad_normed = dot(grad_proj, qkv_mat, ((1,), (1,)))
         grad_prev, gain_a_grad = norm_backward(state_in, scale_one, gains_a[l], grad_normed)
         grad_state = grad_mid + grad_prev
-        both = jnp.concatenate([grad_in_proj, grad_out_proj], axis=1).reshape(-1, 128)
-        both = lax.psum_scatter(both, "grp", scatter_dimension=0, tiled=True)
-        both = lax.psum_scatter(both, "seq", scatter_dimension=0, tiled=True)
-        attn_grads[l] = both.reshape(-1, 4 * D).astype(F32)
+        attn_grads[l] = jnp.concatenate([grad_in_proj, grad_out_proj], axis=1)
         small[l] = (gain_a_grad, gain_f_grad, router_grad, table_grad)
     sizes = [D, D, D * experts, BUCKETS * HEADS]
     flat = jnp.concatenate([part.reshape(-1) for l in range(LAYERS) for part in small[l]])
-    flat = lax.psum(flat.reshape(-1, 128), ("grp", "seq")).reshape(LAYERS, -1)
+    used = flat.size
+    padded = -(-used // (3 * 8 * 128)) * 3 * 8 * 128
+    devices = 2 * SIDE**3
+    whole = jnp.stack(attn_grads).reshape(LAYERS, devices, -1, 128).transpose(1, 0, 2, 3)
+    whole = whole.reshape(devices, 3, -1, 128).transpose(1, 0, 2, 3)
+    whole = whole.reshape(3, SIDE, SIDE, SIDE, 2, -1, 128)
+    attn, flat = reduce_all(whole, jnp.pad(flat, (0, padded - used)).reshape(3, -1, 128))
+    attn = attn.reshape(LAYERS, -1, 4 * D)
+    flat = flat.reshape(-1)[:used].reshape(LAYERS, -1)
     sums, at = [], 0
     for size in sizes:
         sums.append(flat[:, at : at + size])
         at += size
-    attn = jnp.stack(attn_grads)
     return (
         out_tokens,
         grad_state,

time: 1140 us -> 618 us (0.54)
  waiting for transfers between devices: 774 us -> 31.3 us
  Pallas kernels: 26.7 us -> 236 us
  local copies, waits for them, and re-layouts: 70.7 us -> 112 us
  blocking collectives: 47.5 us -> 14.6 us
    reduce_scatter x6 -> x0, waiting for transfers between devices: 225 us -> none  [the longest x2 112 us: on_device(): both = lax.psum_scatter(both, 'grp', scatter_dimension=0, tiled=True)]
    pallas_call x0 -> x6, Pallas kernels: none -> 208 us  [the longest x1 56.8 us: attn_gather(): pl.pallas_call(attn_gather_kernel, out_shape=(jax.ShapeDtypeStruct((3, SI...]
    psum x1 -> x0, waiting for transfers between devices: 145 us -> none  [on_device(): flat = lax.psum(flat.reshape(-1, 128), ('grp', 'seq')).reshape(LAYERS, -1)]
    all_gather x4 -> x0, waiting for transfers between devices: 126 us -> none  [the longest x2 94.1 us: gather_attn(): lax.all_gather(lax.all_gather(own, 'seq', axis=0, tiled=True), 'grp', axi...]
    reduce_scatter x2, waiting for transfers between devices: 78.6 us -> 0.01 us  [on_device(): lax.psum_scatter(grad_first, 'seq', scatter_dimension=0, tiled=True)]
    reduce_scatter x2, waiting for transfers between devices: 71.7 us -> 0.01 us  [on_device(): lax.psum_scatter(grad_second, 'seq', scatter_dimension=0, tiled=True)]
    all_gather x2, waiting for transfers between devices: 59.1 us -> 0.02 us  [gather_experts(): second = lax.all_gather(w_out[layer_index, 0], 'seq', axis=0, tiled=True)]
    all_gather x2 -> x0, blocking collectives: 31.4 us -> none  [gather_attn(): lax.all_gather(own, 'seq', axis=0, tiled=True)]
  transfers between devices with their start and end apart: 26 -> 15, of which waited for: 23 -> 5; matrix products, arithmetic and copies ran while one was open for 12% -> 40% of each run, Pallas kernels for 1% -> 39%
where the time goes in v2:
time: 618 us; the launch traced here: 605 us
  Pallas kernels  236 us (38%)
  matrix products  127 us (21%)
  local copies, waits for them, and re-layouts  112 us (18%)
  other arithmetic  35.4 us (6%)
  starting transfers between devices  33.3 us (5%)
  waiting for transfers between devices  31.3 us (5%)
  between operations  16.1 us (3%)
  blocking collectives  14.6 us (2%)
    dot_general x38, matrix products, dot(): lax.dot_general(a, b, (contract, ((), ())), preferred_element_type=F32)  118 us
    pallas_call x1, Pallas kernels, attn_gather(): pl.pallas_call(attn_gather_kernel, out_shape=(jax.ShapeDtypeStruct((3, SI...  56.8 us
    pallas_call x2, Pallas kernels, gather_keys(): pl.pallas_call(kv_gather, out_shape=jax.ShapeDtypeStruct((2 * SIDE * own....  53.1 us
    pallas_call x1, Pallas kernels, reduce_all(): pl.pallas_call(reduce_kernel, out_shape=(jax.ShapeDtypeStruct((3,) + bloc...  51.3 us
    pallas_call x2, Pallas kernels, scatter_key_grads(): pl.pallas_call(kv_scatter, out_shape=jax.ShapeDtypeStruct(block, BF), in_...  46.8 us
    all_to_all x7, starting transfers between devices, to_peers(): return lax.all_to_all(rows, 'grp', split_axis=0, concat_axis=0, tiled=True)  32.8 us
    all_to_all x7, waiting for transfers between devices, to_peers(): return lax.all_to_all(rows, 'grp', split_axis=0, concat_axis=0, tiled=True)  29.9 us
    slice x3, local copies, waits for them, and re-layouts, on_device(): qkv_mat, out_mat = (attn_full[l][:, :3 * D], attn_full[l][:, 3 * D:])  25.7 us
  transfers between devices with their start and end apart: 15, of which 5 were waited for; matrix products, arithmetic and copies ran while one was open for 40% of the time, Pallas kernels for 39%

profile of v2, /device:TPU:1, one launch (start us, length us, event | category | flops | bytes accessed | tf_op | source)
XLA Modules:
  0.0 605.4 jit_solution(12196165597300403413)
XLA Ops:
  7.3 2.4 fusion.127
  9.7 2.3 fusion.128
  13.7 56.8 %shard_map.204 = (bf16[3,4,4,4,2,96,128]{6,5,4,3,2,1,0:T(8,128)(2,1)S(1)}, f32[4,2,8,128]{3,2,1,0:T(8,128)S(1)}) custom-call(bf16[3,96,128]{2,1,0:T(8,128)(2,1)S(1)} %reshape.330.own_ref, f32[8,128]{1,0:T(8,128)S(1)} %broadcast_in_dim.15.seg_ref), custom_call_target="tpu_custom_call" | custom-call | tf_op jit(solution)/shard_map/pallas_call | solution.py:261
  70.4 3.6 copy-done.2
  74.0 12.9 %copy.64 = bf16[3,128,96,128]{1,3,2,0:T(8,128)(2,1)} copy(bf16[3,128,96,128]{3,2,1,0:T(8,128)(2,1)} %bitcast.176) | data formatting | bytes 18874368 | tf_op jit(solution)/shard_map/reshape | solution.py:549
  87.0 8.3 %fusion.126 = (bf16[1,128,6,3072]{1,3,2,0:T(8,128)(2,1)}, bf16[1,128,6,3072]{1,3,2,0:T(8,128)(2,1)}) fusion(bf16[2,128,6,3072]{1,3,2,0:T(8,128)(2,1)} %bitcast.180), kind=kLoop, calls=%fused_computation.225 | loop fusion | bytes 18874368 | tf_op jit(solution)/shard_map/slice | solution.py:615
  95.3 8.7 %copy.65 = bf16[1,128,6,3072]{3,2,1,0:T(8,128)(2,1)} copy(bf16[1,128,6,3072]{1,3,2,0:T(8,128)(2,1)} %get-tuple-element.85) | data formatting | bytes 9437184 | tf_op jit(solution)/shard_map/slice | solution.py:615
  104.0 7.8 %squeeze.46 = bf16[768,3072]{1,0:T(8,128)(2,1)} reshape(bf16[1,128,6,3072]{3,2,1,0:T(8,128)(2,1)} %copy.65) | data formatting | bytes 9437184 | tf_op jit(solution)/shard_map/squeeze | solution.py:615
  112.5 3.0 convolution_convert_fusion.7
  117.4 33.3 %shard_map.205.kv_ref = bf16[1024,1536]{1,0:T(8,128)(2,1)S(1)} custom-call(bf16[128,1536]{1,0:T(8,128)(2,1)S(1)} %copy-done.7), custom_call_target="tpu_custom_call" | custom-call | tf_op jit(solution)/shard_map/pallas_call | solution.py:507
  152.3 5.2 shard_map.206
  164.0 4.5 all-to-all-start
  168.5 8.7 %copy.68 = bf16[1,128,6,3072]{3,2,1,0:T(8,128)(2,1)} copy(bf16[1,128,6,3072]{1,3,2,0:T(8,128)(2,1)} %get-tuple-element.84) | data formatting | bytes 9437184 | tf_op jit(solution)/shard_map/slice | solution.py:615
  177.2 7.9 %squeeze.53 = bf16[768,3072]{1,0:T(8,128)(2,1)} reshape(bf16[1,128,6,3072]{3,2,1,0:T(8,128)(2,1)} %copy.68) | data formatting | bytes 9437184 | tf_op jit(solution)/shard_map/squeeze | solution.py:615
  187.2 6.7 %fusion.28 = f32[384,3072]{1,0:T(8,128)} fusion(bf16[384,768]{1,0:T(8,128)(2,1)} %bitcast.16, bf16[1,1,768,3072]{3,2,1,0:T(8,128)(2,1)} %all-gather.9.cloned.1.call-done), kind=kOutput, calls=%fused_computation.41 | convolution fusion | flops 1811939328 | bytes 10027008 | tf_op jit(solution)/shard_map/dot_general | solution.py:26
  193.9 7.4 %fusion.45 = bf16[384,768]{1,0:T(8,128)(2,1)} fusion(bf16[1,1,3072,768]{3,2,1,0:T(8,128)(2,1)} %all-gather.11.cloned.1.call-done, f32[384,3072]{1,0:T(8,128)} %fusion.28), kind=kOutput, calls=%fused_computation.63 | convolution fusion | flops 1822851072 | bytes 10027008 | tf_op jit(solution)/shard_map/dot_general | solution.py:26
  201.3 6.7 %all-to-all-start.1 = ((bf16[16,24,768]{2,1,0:T(8,128)(2,1)}), bf16[16,24,768]{2,1,0:T(8,128)(2,1)}, u32[]{:S(2)}, u32[]{:S(2)}) async-start(bf16[16,24,768]{2,1,0:T(8,128)(2,1)} %bitcast.198), calls=%async_computation.1 | async-start | bytes 1179648 | tf_op jit(solution)/shard_map/all_to_all | solution.py:541
  209.0 10.2 %all-to-all-done.1 = bf16[16,24,768]{2,1,0:T(8,128)(2,1)} async-done(((bf16[16,24,768]{2,1,0:T(8,128)(2,1)}), bf16[16,24,768]{2,1,0:T(8,128)(2,1)}, u32[]{:S(2)}, u32[]{:S(2)}) %all-to-all-start.1) | async-done | bytes 589856 | tf_op jit(solution)/shard_map/all_to_all | solution.py:541
  219.2 2.3 multiply_reduce_fusion.3
  223.9 2.7 convolution_convert_fusion.6
  226.7 19.8 %shard_map.207.kv_ref = bf16[1024,1536]{1,0:T(8,128)(2,1)S(1)} custom-call(bf16[128,1536]{1,0:T(8,128)(2,1)S(1)} %slice.167.own_ref), custom_call_target="tpu_custom_call" | custom-call | tf_op jit(solution)/shard_map/pallas_call | solution.py:507
  246.5 5.2 shard_map.208
  258.5 4.2 all-to-all-start.2
  268.2 6.5 %all-to-all-done.2 = bf16[16,24,768]{2,1,0:T(8,128)(2,1)} async-done(((bf16[16,24,768]{2,1,0:T(8,128)(2,1)}), bf16[16,24,768]{2,1,0:T(8,128)(2,1)}, u32[]{:S(2)}, u32[]{:S(2)}) %all-to-all-start.2) | async-done | bytes 589856 | tf_op jit(solution)/shard_map/all_to_all | solution.py:541
  274.7 4.7 all-to-all-start.4
  279.4 6.6 %fusion.20 = f32[384,3072]{1,0:T(8,128)} fusion(bf16[384,768]{1,0:T(8,128)(2,1)} %bitcast.28, bf16[1,1,768,3072]{3,2,1,0:T(8,128)(2,1)} %all-gather.13.cloned.1.call-done), kind=kOutput, calls=%fused_computation.33 | convolution fusion | flops 1811939328 | bytes 10027008 | tf_op jit(solution)/shard_map/dot_general | solution.py:26
  286.0 4.4 all-to-all-done.4
  290.4 8.0 %fusion.13 = bf16[384,3072]{1,0:T(8,128)(2,1)S(1)} fusion(f32[384,3072]{1,0:T(8,128)} %fusion.20, bf16[384,768]{1,0:T(8,128)(2,1)} %bitcast.38, bf16[1,1,3072,768]{3,2,1,0:T(8,128)(2,1)} %all-gather.15.cloned.1.call-done), kind=kOutput, calls=%fused_computation.24 | convolution fusion | flops 1835532288 | bytes 12386304 | tf_op jit(solution)/shard_map/dot_general | solution.py:26
  299.9 5.3 convolution_convert_fusion.2
  305.2 7.5 %fusion.51 = bf16[384,768]{1,0:T(8,128)(2,1)} fusion(bf16[1,1,3072,768]{3,2,1,0:T(8,128)(2,1)} %all-gather.15.cloned.1.call-done, f32[384,3072]{1,0:T(8,128)} %fusion.20), kind=kOutput, calls=%fused_computation.65 | convolution fusion | flops 1822851072 | bytes 10027008 | tf_op jit(solution)/shard_map/dot_general | solution.py:26
  312.7 4.3 all-to-all-start.3
  317.0 6.0 fusion.48
  323.0 4.4 all-to-all-done.3
  327.4 4.3 all-to-all-start.5
  331.9 2.5 multiply_reduce_fusion.1
  336.9 4.4 all-to-all-done.5
  342.8 2.2 multiply_reduce_fusion.4
  345.0 2.0 subtract_add_fusion.2
  347.0 2.0 convolution_convert_fusion.15.grad_ref
  349.0 8.7 %shard_map.209 = (bf16[128,768]{1,0:T(8,128)(2,1)S(1)}, bf16[8,128,1536]{2,1,0:T(8,128)(2,1)S(1)}, f32[12,768]{1,0:T(8,128)S(1)}) custom-call(s32[1]{0:T(128)} %bitcast.off_ref, bf16[128,768]{1,0:T(8,128)(2,1)S(1)} %slice.166.q_ref, bf16[1024,1536]{1,0:T(8,128)(2,1)S(1)} %copy-done.1, f32[128,1]{1,0:T(8,128)S(1)} %copy-done.5, ...), custom_call_target="tpu_custom_call" | custom-call | tf_op jit(solution)/shard_map/pallas_call | solution.py:148
  357.8 23.3 %shard_map.210 = bf16[128,1536]{1,0:T(8,128)(2,1)S(1)} custom-call(bf16[8,128,1536]{2,1,0:T(8,128)(2,1)S(1)} %get-tuple-element.30.grads_ref), custom_call_target="tpu_custom_call" | custom-call | tf_op jit(solution)/shard_map/pallas_call | solution.py:521
  381.2 4.1 multiply_reduce_fusion.5
  386.3 14.6 %all_to_all.40 = bf16[16,24,768]{2,1,0:T(8,128)(2,1)S(1)} all-to-all(bf16[16,24,768]{2,1,0:T(8,128)(2,1)S(1)} %bitcast.187), channel_id=1, replica_groups=mesh['grp'=16,'seq'=8] {'grp'}, dimensions={0} | all-to-all | bytes 1179648 | tf_op jit(solution)/shard_map/all_to_all | solution.py:541
  400.9 4.4 fusion.6
  406.8 5.4 convolution_convert_fusion.3
  412.2 7.6 %convolution_convert_fusion = bf16[3072,768]{1,0:T(8,128)(2,1)} fusion(bf16[384,768]{1,0:T(8,128)(2,1)} %bitcast.38, f32[384,3072]{1,0:T(8,128)} %fusion.20), kind=kOutput, calls=%fused_computation.5 | convolution fusion | flops 1824915456 | bytes 10027008 | tf_op jit(solution)/shard_map/dot_general | solution.py:26
  419.9 7.7 %convolution_convert_fusion.1 = bf16[3072,768]{1,0:T(8,128)(2,1)} fusion(bf16[384,768]{1,0:T(8,128)(2,1)} %bitcast.195, f32[384,3072]{1,0:T(8,128)} %fusion.28), kind=kOutput, calls=%fused_computation.6 | convolution fusion | flops 1824915456 | bytes 10027008 | tf_op jit(solution)/shard_map/dot_general | solution.py:26
  432.5 2.5 convolution_convert_fusion.4
  435.1 2.8 pad_maximum_fusion.2
  437.9 2.9 fusion.42
  440.8 4.2 all-to-all-start.7
  446.9 8.5 %stack.34 = bf16[1,128,144,128]{3,2,1,0:T(8,128)(2,1)} reshape(bf16[768,3072]{1,0:T(8,128)(2,1)} %pad_maximum_fusion.2) | data formatting | bytes 9437184 | tf_op jit(solution)/shard_map/stack | solution.py:699
  457.2 2.0 fusion.119
  467.0 2.0 convolution_convert_fusion.14.grad_ref
  469.1 8.7 %shard_map.211 = (bf16[128,768]{1,0:T(8,128)(2,1)S(1)}, bf16[8,128,1536]{2,1,0:T(8,128)(2,1)S(1)}, f32[12,768]{1,0:T(8,128)S(1)}) custom-call(s32[1]{0:T(128)} %bitcast.off_ref, bf16[128,768]{1,0:T(8,128)(2,1)S(1)} %slice.157.q_ref, bf16[1024,1536]{1,0:T(8,128)(2,1)S(1)} %shard_map.205.kv_ref, f32[128,1]{1,0:T(8,128)S(1)} %copy-done.6, ...), custom_call_target="tpu_custom_call" | custom-call | tf_op jit(solution)/shard_map/pallas_call | solution.py:148
  477.8 23.5 %shard_map.212 = bf16[128,1536]{1,0:T(8,128)(2,1)S(1)} custom-call(bf16[8,128,1536]{2,1,0:T(8,128)(2,1)S(1)} %get-tuple-element.33.grads_ref), custom_call_target="tpu_custom_call" | custom-call | tf_op jit(solution)/shard_map/pallas_call | solution.py:521
  503.0 2.8 pad_maximum_fusion.1
  505.9 8.5 %stack.33 = bf16[1,128,144,128]{3,2,1,0:T(8,128)(2,1)} reshape(bf16[768,3072]{1,0:T(8,128)(2,1)} %pad_maximum_fusion.1) | data formatting | bytes 9437184 | tf_op jit(solution)/shard_map/stack | solution.py:699
  514.4 8.3 %pad_maximum_fusion = bf16[2,128,144,128]{3,2,0,1:T(8,128)(2,1)} fusion(bf16[1,128,144,128]{3,2,0,1:T(8,128)(2,1)} %bitcast.182, bf16[1,128,144,128]{3,2,0,1:T(8,128)(2,1)} %bitcast.183), kind=kLoop, calls=%fused_computation | loop fusion | flops 4718592 | bytes 18874368 | tf_op jit(solution)/shard_map/stack | solution.py:699
  522.8 9.6 %copy.77 = bf16[3,128,96,128]{3,2,1,0:T(8,128)(2,1)} copy(bf16[3,128,96,128]{3,2,0,1:T(8,128)(2,1)} %bitcast.181) | data formatting | bytes 18874368 | tf_op jit(solution)/shard_map/transpose | solution.py:700
  532.7 3.4 fusion.72
  536.3 51.3 %shard_map.213 = (f32[3,96,128]{2,1,0:T(8,128)S(1)}, f32[3,80,128]{2,1,0:T(8,128)S(1)}) custom-call(bf16[3,4,4,4,2,96,128]{6,5,4,3,2,1,0:T(8,128)(2,1)} %bitcast.179, f32[3,80,128]{2,1,0:T(8,128)S(1)} %bitcast.177), custom_call_target="tpu_custom_call" | custom-call | tf_op jit(solution)/shard_map/pallas_call | solution.py:401
  592.7 2.8 fusion.54
  595.5 2.8 fusion.55
  (345 shorter events, 61.0 us)
Async XLA Ops:
  7.2 179.4 %all-gather.9.cloned.1.call-start = ((), (), s32[]{:S(2)}) async-start(), calls=%async_computation.16 | async-start | bytes 5308416 | tf_op jit(solution)/shard_map/all_gather | solution.py:555
  9.7 184.2 %all-gather.11.cloned.1.call-start = ((), (), s32[]{:S(2)}) async-start(), calls=%async_computation.17 | async-start | bytes 5308416 | tf_op jit(solution)/shard_map/all_gather | solution.py:556
  12.1 267.3 %all-gather.13.cloned.1.call-start = ((), (), s32[]{:S(2)}) async-start(), calls=%async_computation.18 | async-start | bytes 5308416 | tf_op jit(solution)/shard_map/all_gather | solution.py:555
  12.8 273.2 %all-gather.15.cloned.1.call-start = ((), (), s32[]{:S(2)}) async-start(), calls=%async_computation.19 | async-start | bytes 5308416 | tf_op jit(solution)/shard_map/all_gather | solution.py:556
  112.5 38.2 %copy-start.89 = (s32[1024]{0:T(1024)S(1)}, s32[1024]{0:T(1024)}, u32[]{:S(2)}) copy-start(s32[1024]{0:T(1024)} %param.15) | copy-start | bytes 12292
  112.5 39.0 %copy-start.68 = (bf16[2,32,12]{1,0,2:T(2,128)(2,1)S(1)}, bf16[2,32,12]{1,0,2:T(2,128)(2,1)}, u32[]{:S(2)}) copy-start(bf16[2,32,12]{1,0,2:T(2,128)(2,1)} %param.20) | copy-start | bytes 4612
  112.5 39.6 %copy-start.92 = (bf16[2,768]{1,0:T(2,128)(2,1)S(1)}, bf16[2,768]{1,0:T(2,128)(2,1)}, u32[]{:S(2)}) copy-start(bf16[2,768]{1,0:T(2,128)(2,1)} %param.21) | copy-start | bytes 9220
  115.5 42.6 %copy-start.93 = (s32[128,2]{0,1:T(2,128)S(1)}, s32[128,2]{0,1:T(2,128)}, u32[]{:S(2)}) copy-start(s32[128,2]{0,1:T(2,128)} %param.16) | copy-start | bytes 3076
  117.4 43.4 %copy-start.71 = (pred[768]{0:T(1024)(128)(4,1)}, pred[768]{0:T(1024)(128)(4,1)S(1)}, u32[]{:S(2)}) copy-start(pred[768]{0:T(1024)(128)(4,1)S(1)} %compare_and_fusion) | copy-start | bytes 2308
  150.8 13.2 %copy-start.3 = (f32[128,1]{1,0:T(8,128)}, f32[128,1]{1,0:T(8,128)S(1)}, u32[]{:S(2)}) copy-start(f32[128,1]{1,0:T(8,128)S(1)} %copy.67.segq_ref) | copy-start | bytes 1540
  151.6 56.5 %copy-start.58 = (s32[768]{0:T(1024)}, s32[768]{0:T(1024)S(1)}, u32[]{:S(2)}) copy-start(s32[768]{0:T(1024)S(1)} %convert_element_type.177) | copy-start | bytes 9220
  158.8 9.6 %copy-start.60 = (f32[768]{0:T(1024)}, f32[768]{0:T(1024)S(1)}, u32[]{:S(2)}) copy-start(f32[768]{0:T(1024)S(1)} %get-tuple-element.79) | copy-start | bytes 9220
  164.0 22.6 %all-to-all-start = ((bf16[16,24,768]{2,1,0:T(8,128)(2,1)}), bf16[16,24,768]{2,1,0:T(8,128)(2,1)}, u32[]{:S(2)}, u32[]{:S(2)}) async-start(bf16[16,24,768]{2,1,0:T(8,128)(2,1)} %bitcast.185), calls=%async_computation | async-start | bytes 1179648 | tf_op jit(solution)/shard_map/all_to_all | solution.py:541
  177.1 7.9 %copy-start.36 = (bf16[128,768]{1,0:T(8,128)(2,1)S(1)}, bf16[128,768]{1,0:T(8,128)(2,1)}, u32[]{:S(2)}) copy-start(bf16[128,768]{1,0:T(8,128)(2,1)} %copy-done.35) | copy-start | bytes 589828
  186.6 21.4 %copy-start.50 = (f32[128,16]{0,1:T(8,128)}, f32[128,16]{0,1:T(8,128)S(1)}, u32[]{:S(2)}) copy-start(f32[128,16]{0,1:T(8,128)S(1)} %fusion.114) | copy-start | bytes 24580
  193.9 14.2 %copy-start.66 = (s32[2,128]{1,0:T(2,128)S(1)}, s32[2,128]{1,0:T(2,128)}, u32[]{:S(2)}) copy-start(s32[2,128]{1,0:T(2,128)} %get-tuple-element.96) | copy-start | bytes 3076
  193.9 14.2 %copy-start.70 = (bf16[1,32,12]{1,0,2:T(2,128)(2,1)S(1)}, bf16[1,32,12]{1,0,2:T(2,128)(2,1)}, u32[]{:S(2)}) copy-start(bf16[1,32,12]{1,0,2:T(2,128)(2,1)} %get-tuple-element.94) | copy-start | bytes 2308
  193.9 14.2 %copy-start.72 = (pred[768]{0:T(1024)(128)(4,1)S(1)}, pred[768]{0:T(1024)(128)(4,1)}, u32[]{:S(2)}) copy-start(pred[768]{0:T(1024)(128)(4,1)} %copy-done.71) | copy-start | bytes 2308
  193.9 15.0 %copy-start.64 = (s32[256]{0:T(256)S(1)}, s32[256]{0:T(256)}, u32[]{:S(2)}) copy-start(s32[256]{0:T(256)} %copy-done.63) | copy-start | bytes 3076
  201.3 17.9 %all-to-all-start.1 = ((bf16[16,24,768]{2,1,0:T(8,128)(2,1)}), bf16[16,24,768]{2,1,0:T(8,128)(2,1)}, u32[]{:S(2)}, u32[]{:S(2)}) async-start(bf16[16,24,768]{2,1,0:T(8,128)(2,1)} %bitcast.198), calls=%async_computation.1 | async-start | bytes 1179648 | tf_op jit(solution)/shard_map/all_to_all | solution.py:541
  208.0 15.3 %copy-start.75 = (f32[2,128]{1,0:T(2,128)}, f32[2,128]{1,0:T(2,128)S(1)}, u32[]{:S(2)}) copy-start(f32[2,128]{1,0:T(2,128)S(1)} %fusion.107) | copy-start | bytes 3076
  209.0 14.4 %copy-start.44 = (pred[256,384]{1,0:T(32,128)(4,1)}, pred[256,384]{1,0:T(32,128)(4,1)S(1)}, u32[]{:S(2)}) copy-start(pred[256,384]{1,0:T(32,128)(4,1)S(1)} %iota_compare_fusion.7) | copy-start | bytes 294916
  222.7 30.7 %copy-start.27 = (f32[128,768]{1,0:T(8,128)}, f32[128,768]{1,0:T(8,128)S(1)}, u32[]{:S(2)}) copy-start(f32[128,768]{1,0:T(8,128)S(1)} %get-tuple-element.83) | copy-start | bytes 1179652
  223.9 22.7 %copy-start.4 = (f32[128,1]{1,0:T(8,128)S(1)}, f32[128,1]{1,0:T(8,128)}, u32[]{:S(2)}) copy-start(f32[128,1]{1,0:T(8,128)} %copy-done.3) | copy-start | bytes 1540
  223.9 22.7 %copy-start.13 = (f32[12,768]{1,0:T(8,128)S(1)}, f32[12,768]{1,0:T(8,128)}, u32[]{:S(2)}) copy-start(f32[12,768]{1,0:T(8,128)} %convolution_bitcast_fusion.bias_ref) | copy-start | bytes 110596
  226.6 29.9 %copy-start.61 = (f32[768]{0:T(1024)S(1)}, f32[768]{0:T(1024)}, u32[]{:S(2)}) copy-start(f32[768]{0:T(1024)} %get-tuple-element.78) | copy-start | bytes 9220
  226.7 30.7 %copy-start.43 = (bf16[384,128]{1,0:T(8,128)(2,1)S(1)}, bf16[384,128]{1,0:T(8,128)(2,1)}, u32[]{:S(2)}) copy-start(bf16[384,128]{1,0:T(8,128)(2,1)} %copy-done.42) | copy-start | bytes 294916
  258.5 16.2 %all-to-all-start.2 = ((bf16[16,24,768]{2,1,0:T(8,128)(2,1)}), bf16[16,24,768]{2,1,0:T(8,128)(2,1)}, u32[]{:S(2)}, u32[]{:S(2)}) async-start(bf16[16,24,768]{2,1,0:T(8,128)(2,1)} %bitcast.186), calls=%async_computation.2 | async-start | bytes 1179648 | tf_op jit(solution)/shard_map/all_to_all | solution.py:541
  274.7 15.7 %all-to-all-start.4 = ((bf16[16,24,768]{2,1,0:T(8,128)(2,1)}), bf16[16,24,768]{2,1,0:T(8,128)(2,1)}, u32[]{:S(2)}, u32[]{:S(2)}) async-start(bf16[16,24,768]{2,1,0:T(8,128)(2,1)} %bitcast.184), calls=%async_computation.4 | async-start | bytes 1179648 | tf_op jit(solution)/shard_map/all_to_all | solution.py:541
  279.3 313.4 %reduce-scatter.7.cloned.1.call-start = ((), (), s32[]{:S(2)}) async-start(), calls=%async_computation.13 | async-start | bytes 5308416 | tf_op jit(solution)/shard_map/reduce_scatter | solution.py:666
  312.7 14.7 %all-to-all-start.3 = ((bf16[16,24,768]{2,1,0:T(8,128)(2,1)}), bf16[16,24,768]{2,1,0:T(8,128)(2,1)}, u32[]{:S(2)}, u32[]{:S(2)}) async-start(bf16[16,24,768]{2,1,0:T(8,128)(2,1)} %bitcast.199), calls=%async_computation.3 | async-start | bytes 1179648 | tf_op jit(solution)/shard_map/all_to_all | solution.py:541
  327.4 13.9 %all-to-all-start.5 = ((bf16[16,24,768]{2,1,0:T(8,128)(2,1)}), bf16[16,24,768]{2,1,0:T(8,128)(2,1)}, u32[]{:S(2)}, u32[]{:S(2)}) async-start(bf16[16,24,768]{2,1,0:T(8,128)(2,1)} %bitcast.196), calls=%async_computation.5 | async-start | bytes 1179648 | tf_op jit(solution)/shard_map/all_to_all | solution.py:541
  331.6 261.0 %reduce-scatter.5.cloned.1.call-start = ((), (), s32[]{:S(2)}) async-start(), calls=%async_computation.12 | async-start | bytes 5308416 | tf_op jit(solution)/shard_map/reduce_scatter | solution.py:666
  347.0 38.3 %copy-start.31 = (f32[128,768]{1,0:T(8,128)}, f32[128,768]{1,0:T(8,128)S(1)}, u32[]{:S(2)}) copy-start(f32[128,768]{1,0:T(8,128)S(1)} %get-tuple-element.90) | copy-start | bytes 1179652
  347.0 34.2 %copy-start.28 = (f32[128,768]{1,0:T(8,128)S(1)}, f32[128,768]{1,0:T(8,128)}, u32[]{:S(2)}) copy-start(f32[128,768]{1,0:T(8,128)} %copy-done.27) | copy-start | bytes 1179652
  347.0 34.2 %copy-start.88 = (f32[128]{0:T(128)S(1)}, f32[128]{0:T(128)}, u32[]{:S(2)}) copy-start(f32[128]{0:T(128)} %copy-done.87) | copy-start | bytes 1540
  349.0 51.9 %slice-start.4 = ((s8[4718592]{0:T(1024)(128)(4,1)}), s8[4194304]{0:T(1024)(128)(4,1)S(1)}, s32[]{:S(2)}) async-start(s8[4718592]{0:T(1024)(128)(4,1)} %bitcast.207), calls=%async_computation.24 | async-start | bytes 8388608
  357.8 27.6 %copy-start.19 = (bf16[128,768]{1,0:T(8,128)(2,1)}, bf16[128,768]{1,0:T(8,128)(2,1)S(1)}, u32[]{:S(2)}) copy-start(bf16[128,768]{1,0:T(8,128)(2,1)S(1)} %get-tuple-element.29) | copy-start | bytes 589828
  357.8 27.5 %copy-start.24 = (f32[12,768]{1,0:T(8,128)}, f32[12,768]{1,0:T(8,128)S(1)}, u32[]{:S(2)}) copy-start(f32[12,768]{1,0:T(8,128)S(1)} %get-tuple-element.35) | copy-start | bytes 110596
  357.8 27.5 %copy-start.94 = (f32[128]{0:T(128)S(1)}, f32[128]{0:T(128)}, u32[]{:S(2)}) copy-start(f32[128]{0:T(128)} %get-tuple-element.104) | copy-start | bytes 1540
  357.8 43.1 %slice-start.2 = ((s8[4718592]{0:T(1024)(128)(4,1)}), s8[4194304]{0:T(1024)(128)(4,1)S(1)}, s32[]{:S(2)}) async-start(s8[4718592]{0:T(1024)(128)(4,1)} %bitcast.205), calls=%async_computation.22 | async-start | bytes 8388608
  381.2 19.7 %slice-start.3 = ((s8[4718592]{0:T(1024)(128)(4,1)}), s8[524288]{0:T(1024)(128)(4,1)S(1)}, s32[]{:S(2)}) async-start(s8[4718592]{0:T(1024)(128)(4,1)} %bitcast.205), calls=%async_computation.23 | async-start | bytes 1048576
  381.2 19.7 %slice-start.5 = ((s8[4718592]{0:T(1024)(128)(4,1)}), s8[524288]{0:T(1024)(128)(4,1)S(1)}, s32[]{:S(2)}) async-start(s8[4718592]{0:T(1024)(128)(4,1)} %bitcast.207), calls=%async_computation.25 | async-start | bytes 1048576
  412.2 183.3 %reduce-scatter.11.cloned.1.call-start = ((), (), s32[]{:S(2)}) async-start(), calls=%async_computation.15 | async-start | bytes 5308416 | tf_op jit(solution)/shard_map/reduce_scatter | solution.py:667
  419.8 175.7 %reduce-scatter.9.cloned.1.call-start = ((), (), s32[]{:S(2)}) async-start(), calls=%async_computation.14 | async-start | bytes 5308416 | tf_op jit(solution)/shard_map/reduce_scatter | solution.py:667
  440.8 22.0 %all-to-all-start.7 = ((bf16[16,24,768]{2,1,0:T(8,128)(2,1)}), bf16[16,24,768]{2,1,0:T(8,128)(2,1)}, u32[]{:S(2)}, u32[]{:S(2)}) async-start(bf16[16,24,768]{2,1,0:T(8,128)(2,1)} %bitcast.197), calls=%async_computation.7 | async-start | bytes 1179648 | tf_op jit(solution)/shard_map/all_to_all | solution.py:541
  446.9 10.3 %copy-start.53 = (f32[128,16]{0,1:T(8,128)S(1)}, f32[128,16]{0,1:T(8,128)}, u32[]{:S(2)}) copy-start(f32[128,16]{0,1:T(8,128)} %copy-done.52) | copy-start | bytes 24580
  446.9 10.3 %copy-start.55 = (f32[128,16]{0,1:T(8,128)S(1)}, f32[128,16]{0,1:T(8,128)}, u32[]{:S(2)}) copy-start(f32[128,16]{0,1:T(8,128)} %copy-done.54) | copy-start | bytes 24580
  455.4 13.7 %copy-start.6 = (f32[128,1]{1,0:T(8,128)S(1)}, f32[128,1]{1,0:T(8,128)}, u32[]{:S(2)}) copy-start(f32[128,1]{1,0:T(8,128)} %copy-done.3) | copy-start | bytes 1540
  455.4 13.7 %copy-start.12 = (f32[12,768]{1,0:T(8,128)S(1)}, f32[12,768]{1,0:T(8,128)}, u32[]{:S(2)}) copy-start(f32[12,768]{1,0:T(8,128)} %copy-done.11) | copy-start | bytes 110596
  455.4 13.7 %copy-start.21 = (f32[128,128]{1,0:T(8,128)S(1)}, f32[128,128]{1,0:T(8,128)}, u32[]{:S(2)}) copy-start(f32[128,128]{1,0:T(8,128)} %copy-done.20) | copy-start | bytes 196612
  467.0 34.8 %copy-start.29 = (f32[128,768]{1,0:T(8,128)}, f32[128,768]{1,0:T(8,128)S(1)}, u32[]{:S(2)}) copy-start(f32[128,768]{1,0:T(8,128)S(1)} %subtract_add_fusion) | copy-start | bytes 1179652
  467.0 34.3 %copy-start.18 = (bf16[128,768]{1,0:T(8,128)(2,1)S(1)}, bf16[128,768]{1,0:T(8,128)(2,1)}, u32[]{:S(2)}) copy-start(bf16[128,768]{1,0:T(8,128)(2,1)} %copy-done.17) | copy-start | bytes 589828
  469.0 32.8 %copy-start.40 = (bf16[128,768]{1,0:T(8,128)(2,1)S(1)}, bf16[128,768]{1,0:T(8,128)(2,1)}, u32[]{:S(2)}) copy-start(bf16[128,768]{1,0:T(8,128)(2,1)} %param.13) | copy-start | bytes 589828
  469.0 32.8 %copy-start.83 = (f32[128]{0:T(128)S(1)}, f32[128]{0:T(128)}, u32[]{:S(2)}) copy-start(f32[128]{0:T(128)} %copy-done.82) | copy-start | bytes 1540
  477.8 24.0 %copy-start.25 = (f32[12,768]{1,0:T(8,128)}, f32[12,768]{1,0:T(8,128)S(1)}, u32[]{:S(2)}) copy-start(f32[12,768]{1,0:T(8,128)S(1)} %get-tuple-element.34) | copy-start | bytes 110596
  477.8 24.0 %copy-start.15 = (bf16[128,768]{1,0:T(8,128)(2,1)}, bf16[128,768]{1,0:T(8,128)(2,1)S(1)}, u32[]{:S(2)}) copy-start(bf16[128,768]{1,0:T(8,128)(2,1)S(1)} %get-tuple-element.32) | copy-start | bytes 589828
  522.8 9.6 %copy-start.26 = (f32[12,768]{1,0:T(8,128)S(1)}, f32[12,768]{1,0:T(8,128)}, u32[]{:S(2)}) copy-start(f32[12,768]{1,0:T(8,128)} %copy-done.25) | copy-start | bytes 110596
  522.8 9.6 %copy-start.59 = (s32[768]{0:T(1024)S(1)}, s32[768]{0:T(1024)}, u32[]{:S(2)}) copy-start(s32[768]{0:T(1024)} %copy-done.58) | copy-start | bytes 9220
  522.8 9.6 %copy-start.73 = (pred[768]{0:T(1024)(128)(4,1)S(1)}, pred[768]{0:T(1024)(128)(4,1)}, u32[]{:S(2)}) copy-start(pred[768]{0:T(1024)(128)(4,1)} %copy-done.71) | copy-start | bytes 2308
  522.8 9.9 %copy-start.16 = (bf16[128,768]{1,0:T(8,128)(2,1)S(1)}, bf16[128,768]{1,0:T(8,128)(2,1)}, u32[]{:S(2)}) copy-start(bf16[128,768]{1,0:T(8,128)(2,1)} %copy-done.15) | copy-start | bytes 589828
  522.8 9.9 %copy-start.41 = (bf16[128,768]{1,0:T(8,128)(2,1)S(1)}, bf16[128,768]{1,0:T(8,128)(2,1)}, u32[]{:S(2)}) copy-start(bf16[128,768]{1,0:T(8,128)(2,1)} %param.13) | copy-start | bytes 589828
  536.3 55.5 %copy-start.30 = (f32[128,768]{1,0:T(8,128)S(1)}, f32[128,768]{1,0:T(8,128)}, u32[]{:S(2)}) copy-start(f32[128,768]{1,0:T(8,128)} %copy-done.29) | copy-start | bytes 1179652
  536.3 55.5 %copy-start.95 = (f32[128]{0:T(128)S(1)}, f32[128]{0:T(128)}, u32[]{:S(2)}) copy-start(f32[128]{0:T(128)} %get-tuple-element.100) | copy-start | bytes 1540
  (57 other events, 185.7 us)
Sparse Core Ops, SparseCore 0:
  9.8 59.0 all-gather.8
  71.2 31.6 all-gather.10
  104.5 47.0 all-gather.12
  153.8 34.2 all-gather.14
  305.3 35.6 reduce-scatter.6
  412.3 34.7 reduce-scatter.4
  449.5 41.2 reduce-scatter.10
  493.2 39.2 reduce-scatter.8

commit v3 on v2

--- a/solution.py
+++ b/solution.py
@@ -1,3 +1,5 @@
+import functools
+
 import jax
 import jax.numpy as jnp
 from jax import lax
@@ -20,6 +22,7 @@
 F32 = jnp.float32
 highest = lax.Precision.HIGHEST
 VMEM = pltpu.VMEM
+LITTLE = pl.CostEstimate(flops=1024, bytes_accessed=1024, transcendentals=0)
 
 
 def dot(a, b, contract=((1,), (0,))):
@@ -140,6 +143,7 @@
         ),
         in_specs=[pl.BlockSpec(memory_space=pltpu.SMEM)] + vmem_specs(5),
         out_specs=tuple(vmem_specs(2)),
+        cost_estimate=LITTLE,
         compiler_params=pltpu.CompilerParams(vmem_limit_bytes=32 * 2**20),
     )(off, queries, kv, segq, segk, bias)
 
@@ -154,11 +158,13 @@
         ),
         in_specs=[pl.BlockSpec(memory_space=pltpu.SMEM)] + vmem_specs(7),
         out_specs=tuple(vmem_specs(3)),
+        cost_estimate=LITTLE,
         compiler_params=pltpu.CompilerParams(vmem_limit_bytes=32 * 2**20),
     )(off, queries, kv, segq, segk, bias, lse, grad)
 
 
 MESH_ID = pl.DeviceIdType.MESH
+QKV_BLOCKS = 6
 SIDE = 4
 
 
@@ -188,31 +194,52 @@
     pl.semaphore_wait(barrier, len(devices))
 
 
+def sequence_partners(coords, core):
+    seq = coords[2] * 2 + core
+    others = [(seq + d) % (2 * SIDE) for d in range(1, 2 * SIDE)]
+    return [(coords[0] * SIDE + coords[1], s) for s in others], others
+
+
 def all_partners(coords, core):
-    partners = [device_at(moved(coords, a, d), core) for a in range(3) for d in range(1, SIDE)]
-    return partners + [device_at(coords, 1 - core)]
-
-
-def attn_gather_kernel(own_ref, seg_ref, full_ref, segs_ref, send_sem, recv_sem, core_send, core_recv, seg_send, seg_recv):
+    partners = [device_at(moved(coords, a, d), core) for a in range(2) for d in range(1, SIDE)]
+    return partners + sequence_partners(coords, core)[0]
+
+
+def attn_gather_kernel(
+    own_ref, seg_ref, pick_ref, full_ref, segs_ref, rows_ref,
+    row_send, row_recv, send_sem, recv_sem, core_send, core_recv, seg_send, seg_recv,
+):
     coords, core = place_of_device()
     sibling = device_at(coords, 1 - core)
     y, x, z = coords
-    for p in range(3):
-        full_ref[p, y, x, z, core] = own_ref[p]
+    seq = z * 2 + core
+    greet(all_partners(coords, core))
+    rows_ref[seq] = own_ref[seq]
     segs_ref[z, core] = seg_ref[...]
-    greet(all_partners(coords, core))
-
-    def region(p, free, fixed=None):
-        index = [slice(None) if a in free else coords[a] for a in range(3)]
-        if fixed is not None:
-            index[fixed[0]] = fixed[1]
-        return full_ref.at[(p, *index, core)]
-
+    devices, numbers = sequence_partners(coords, core)
+    row_copies = []
+    for n, (device, s) in enumerate(zip(devices, numbers)):
+        row_copies.append(remote(own_ref.at[s], rows_ref.at[seq], row_send.at[n], row_recv.at[n], device))
+        row_copies[-1].start()
     seg_copies = []
     for d in range(1, SIDE):
         one = segs_ref.at[z, core]
         seg_copies.append(remote(one, one, seg_send.at[d - 1], seg_recv.at[d - 1], device_at(moved(coords, 2, d), core)))
         seg_copies[-1].start()
+    for copy in row_copies:
+        copy.wait()
+    for l in range(LAYERS):
+        flat = rows_ref[:, l].reshape(-1, own_ref.shape[-1])
+        block = dot(pick_ref[...], flat).astype(BF)
+        for p in range(3):
+            full_ref[z, core, l, y, x, p] = block[16 * p : 16 * p + 16]
+
+    def region(p, free, fixed=None):
+        at = [slice(None) if a in free else coords[a] for a in range(3)]
+        if fixed is not None:
+            at[fixed[0]] = fixed[1]
+        return full_ref.at[at[2], core, :, at[0], at[1], p]
+
     copies = {}
     core_copies = []
 
@@ -255,48 +282,55 @@
         copy.wait()
 
 
-def attn_gather(own, seg):
-    sems = [pltpu.SemaphoreType.DMA((3, 3, 3))] * 2 + [pltpu.SemaphoreType.DMA((12,))] * 2
-    sems += [pltpu.SemaphoreType.DMA((4,))] * 2
+def attn_gather(own, seg, pick):
+    dma = pltpu.SemaphoreType.DMA
+    width = own.shape[-1]
     return pl.pallas_call(
         attn_gather_kernel,
         out_shape=(
-            jax.ShapeDtypeStruct((3, SIDE, SIDE, SIDE, 2) + own.shape[1:], BF),
+            jax.ShapeDtypeStruct((SIDE, 2, LAYERS, SIDE, SIDE, 3, 16, width), BF),
             jax.ShapeDtypeStruct((SIDE, 2) + seg.shape, F32),
         ),
-        in_specs=vmem_specs(2),
+        in_specs=vmem_specs(3),
         out_specs=tuple(vmem_specs(2)),
-        scratch_shapes=sems,
+        scratch_shapes=[VMEM(own.shape, BF), dma((7,)), dma((7,)), dma((3, 3, 3)), dma((3, 3, 3)),
+                        dma((12,)), dma((12,)), dma((4,)), dma((4,))],
+        cost_estimate=LITTLE,
         compiler_params=pltpu.CompilerParams(
             collective_id=0, has_side_effects=True, vmem_limit_bytes=40 * 2**20
         ),
-    )(own, seg)
+    )(own, seg, pick)
 
 
 def reduce_kernel(
-    x_ref, small_ref, out_ref, small_out, got_core, y_ref, got_one, z_ref, got_two, w_ref, got_three,
-    s_core, s_got, core_send, core_recv, send_sem, recv_sem, s_core_send, s_core_recv, s_send, s_recv,
+    x0_ref, x1_ref, small_ref, pick_ref, out_ref, small_out, got_core, y_ref, got_one, z_ref, got_two, w_ref, got_three,
+    rows_ref, s_core, s_got, core_send, core_recv, send_sem, recv_sem, s_core_send, s_core_recv, s_send, s_recv,
+    row_send, row_recv,
 ):
     coords, core = place_of_device()
     sibling = device_at(coords, 1 - core)
     greet(all_partners(coords, core))
-    first = []
+    x_refs = (x0_ref, x1_ref)
+    order = (2, 0, 1)
+    first = {}
     for p in range(3):
-        copy = remote(
-            x_ref.at[p, :, :, :, 1 - core], got_core.at[p], core_send.at[p], core_recv.at[p], sibling
-        )
-        copy.start()
-        first.append(copy)
+        for l in range(LAYERS):
+            first[p, l] = remote(
+                x_refs[l].at[:, 1 - core, :, :, p], got_core.at[p, l], core_send.at[p, l], core_recv.at[p, l], sibling
+            )
+            first[p, l].start()
     s_first = remote(small_ref, s_core, s_core_send, s_core_recv, sibling)
     s_first.start()
 
+    def axes_left(p, k):
+        gone = [(p + i) % 3 for i in range(k)]
+        return [a for a in order if a not in gone]
+
     def spread(p, k, source, target):
-        axis = (p + k) % 3
-        left = [a for a in range(3) if a not in [(p + i) % 3 for i in range(k)]]
-        out = []
+        axis, out = (p + k) % 3, []
         for d in (1, 3, 2):
             to = moved(coords, axis, d)
-            index = tuple(to[axis] if a == axis else slice(None) for a in left)
+            index = tuple(to[axis] if a == axis else slice(None) for a in axes_left(p, k))
             copy = remote(
                 source.at[(p, *index)], target.at[p, d - 1], send_sem.at[k, p, d - 1], recv_sem.at[k, p, d - 1],
                 device_at(to, core),
@@ -329,12 +363,14 @@
         s_got[0, p, 0] = small_ref[p] + s_core[p]
         s_sent[0, p] = spread_small(p, 0)
     for p in range(3):
-        first[p].wait()
+        for l in range(LAYERS):
+            first[p, l].wait()
 
         def add_core(i, carry, p=p):
             a, b, c = i // (SIDE * SIDE), i // SIDE % SIDE, i % SIDE
-            total = x_ref[p, a, b, c, core].astype(F32) + got_core[p, a, b, c].astype(F32)
-            y_ref[p, a, b, c] = total.astype(BF)
+            for l in range(LAYERS):
+                total = x_refs[l][a, core, b, c, p].astype(F32) + got_core[p, l, a, b, c].astype(F32)
+                y_ref[p, a, b, c, l] = total.astype(BF)
             return carry
 
         lax.fori_loop(0, SIDE**3, add_core, 0)
@@ -347,12 +383,12 @@
     for p in range(3):
         for copy in sent[0, p]:
             copy.wait()
-        axis = p
-
-        def add_one(i, carry, p=p, axis=axis):
+        at = order.index(p)
+
+        def add_one(i, carry, p=p, at=at):
             a, b = i // SIDE, i % SIDE
             index = [a, b]
-            index.insert(axis, coords[axis])
+            index.insert(at, coords[p])
             total = y_ref[(p, *index)].astype(F32)
             for d in range(3):
                 total = total + got_one[p, d, a, b].astype(F32)
@@ -370,10 +406,9 @@
         for copy in sent[1, p]:
             copy.wait()
         axis = (p + 1) % 3
-        left = [a for a in range(3) if a != p]
-
-        def add_two(i, carry, p=p, axis=axis, left=left):
-            index = tuple(coords[axis] if a == axis else i for a in left)
+
+        def add_two(i, carry, p=p, axis=axis):
+            index = tuple(coords[axis] if a == axis else i for a in axes_left(p, 1))
             total = z_ref[(p, *index)].astype(F32)
             for d in range(3):
                 total = total + got_two[p, d, i].astype(F32)
@@ -386,39 +421,143 @@
         for copy in s_sent[2, p]:
             copy.wait()
         small_out[p] = small_sum(p, 2)
+    blocks = []
     for p in range(3):
         for copy in sent[2, p]:
             copy.wait()
         total = w_ref[p, coords[(p + 2) % 3]].astype(F32)
         for d in range(3):
             total = total + got_three[p, d].astype(F32)
-        out_ref[p] = total
-
-
-def reduce_all(x, small):
-    block, part = x.shape[-2:], small.shape[1:]
+        blocks.append(total.astype(BF))
+    for l in range(LAYERS):
+        block = jnp.concatenate([part[l] for part in blocks], axis=0)
+        spread_rows = dot(pick_ref[...], block, ((0,), (0,))).astype(BF)
+        rows_ref[:, l] = spread_rows.reshape(2 * SIDE, 16, -1)
+    seq = coords[2] * 2 + core
+    out_ref[seq] = rows_ref[seq]
+    devices, numbers = sequence_partners(coords, core)
+    last = []
+    for n, (device, s) in enumerate(zip(devices, numbers)):
+        last.append(remote(rows_ref.at[s], out_ref.at[seq], row_send.at[n], row_recv.at[n], device))
+        last[-1].start()
+    for copy in last:
+        copy.wait()
+
+
+def reduce_all(x0, x1, small, pick):
+    width, part = x0.shape[-1], small.shape[1:]
+    block = (LAYERS, 16, width)
+    rows = (2 * SIDE, LAYERS, 16, width)
     dma = pltpu.SemaphoreType.DMA
     return pl.pallas_call(
         reduce_kernel,
-        out_shape=(jax.ShapeDtypeStruct((3,) + block, F32), jax.ShapeDtypeStruct(small.shape, F32)),
-        in_specs=vmem_specs(2),
+        out_shape=(jax.ShapeDtypeStruct(rows, BF), jax.ShapeDtypeStruct(small.shape, F32)),
+        in_specs=vmem_specs(4),
         out_specs=tuple(vmem_specs(2)),
         scratch_shapes=[
-            VMEM((3, SIDE, SIDE, SIDE) + block, BF),
+            VMEM((3, LAYERS, SIDE, SIDE, SIDE, 16, width), BF),
             VMEM((3, SIDE, SIDE, SIDE) + block, BF),
             VMEM((3, 3, SIDE, SIDE) + block, BF),
             VMEM((3, SIDE, SIDE) + block, BF),
             VMEM((3, 3, SIDE) + block, BF),
             VMEM((3, SIDE) + block, BF),
             VMEM((3, 3) + block, BF),
+            VMEM(rows, BF),
             VMEM(small.shape, F32),
             VMEM((3, 3, SIDE) + part, F32),
-            dma((3,)), dma((3,)), dma((3, 3, 3)), dma((3, 3, 3)), dma(()), dma(()), dma((3, 3, 3)), dma((3, 3, 3)),
+            dma((3, LAYERS)), dma((3, LAYERS)), dma((3, 3, 3)), dma((3, 3, 3)), dma(()), dma(()),
+            dma((3, 3, 3)), dma((3, 3, 3)), dma((7,)), dma((7,)),
         ],
+        cost_estimate=LITTLE,
         compiler_params=pltpu.CompilerParams(
             collective_id=1, has_side_effects=True, vmem_limit_bytes=50 * 2**20
         ),
-    )(x, small)
+    )(x0, x1, small, pick)
+
+
+def project_kernel(x_ref, w_ref, out_ref):
+    width = w_ref.shape[3]
+    for s in range(w_ref.shape[0]):
+        out_ref[:, s * width : (s + 1) * width] = dot(x_ref[...], w_ref[s, 0]).astype(out_ref.dtype)
+
+
+def project(x, full, layer, first, count, dtype):
+    depth, width = full.shape[2:]
+    some = 3 if count % 3 == 0 else count
+    return pl.pallas_call(
+        project_kernel,
+        grid=(count // some,),
+        out_shape=jax.ShapeDtypeStruct((x.shape[0], count * width), dtype),
+        in_specs=[
+            pl.BlockSpec(x.shape, lambda s: (0, 0)),
+            pl.BlockSpec((some, 1, depth, width), lambda s: (first // some + s, layer, 0, 0)),
+        ],
+        out_specs=pl.BlockSpec((x.shape[0], some * width), lambda s: (0, s)),
+        cost_estimate=LITTLE,
+        compiler_params=pltpu.CompilerParams(vmem_limit_bytes=56 * 2**20),
+    )(x, full)
+
+
+def project_back_kernel(x_ref, w_ref, out_ref):
+    @pl.when(pl.program_id(0) == 0)
+    def _():
+        out_ref[...] = jnp.zeros_like(out_ref)
+
+    width = w_ref.shape[3]
+    for s in range(w_ref.shape[0]):
+        out_ref[...] += dot(x_ref[:, s * width : (s + 1) * width], w_ref[s, 0], ((1,), (1,)))
+
+
+def project_back(x, full, layer, first, count):
+    depth, width = full.shape[2:]
+    some = 3 if count % 3 == 0 else count
+    return pl.pallas_call(
+        project_back_kernel,
+        grid=(count // some,),
+        out_shape=jax.ShapeDtypeStruct((x.shape[0], depth), F32),
+        in_specs=[
+            pl.BlockSpec((x.shape[0], some * width), lambda s: (0, s)),
+            pl.BlockSpec((some, 1, depth, width), lambda s: (first // some + s, layer, 0, 0)),
+        ],
+        out_specs=pl.BlockSpec((x.shape[0], depth), lambda s: (0, 0)),
+        cost_estimate=LITTLE,
+        compiler_params=pltpu.CompilerParams(vmem_limit_bytes=56 * 2**20),
+    )(x, full)
+
+
+def weight_grad_kernel(normed_ref, attended_ref, proj_ref, branch_ref, out_ref):
+    step, width = pl.program_id(0), out_ref.shape[2]
+
+    def fill(left, right):
+        for s in range(out_ref.shape[0]):
+            out_ref[s] = dot(left[...], right[:, s * width : (s + 1) * width], ((0,), (0,))).astype(BF)
+
+    @pl.when(step < QKV_BLOCKS // 2)
+    def _():
+        fill(normed_ref, proj_ref)
+
+    @pl.when(step >= QKV_BLOCKS // 2)
+    def _():
+        fill(attended_ref, branch_ref)
+
+
+def weight_grads(normed, attended, grad_proj, branch_grad):
+    rows, width = normed.shape[0], grad_proj.shape[1] // QKV_BLOCKS
+    last = QKV_BLOCKS // 2 - 1
+    return pl.pallas_call(
+        weight_grad_kernel,
+        grid=(SIDE,),
+        out_shape=jax.ShapeDtypeStruct((2 * SIDE, D, width), BF),
+        in_specs=[
+            pl.BlockSpec((rows, D), lambda s: (0, 0)),
+            pl.BlockSpec((rows, D), lambda s: (0, 0)),
+            pl.BlockSpec((rows, 2 * width), lambda s: (0, jnp.minimum(s, last))),
+            pl.BlockSpec((rows, 2 * width), lambda s: (0, 0)),
+        ],
+        out_specs=pl.BlockSpec((2, D, width), lambda s: (s, 0, 0)),
+        cost_estimate=LITTLE,
+        compiler_params=pltpu.CompilerParams(vmem_limit_bytes=56 * 2**20),
+    )(normed, attended, grad_proj, branch_grad)
 
 
 def kv_gather(own_ref, kv_ref, send_sem, recv_sem):
@@ -510,6 +649,7 @@
         in_specs=vmem_specs(1),
         out_specs=vmem_specs(1)[0],
         scratch_shapes=[pltpu.SemaphoreType.DMA((9,))] * 2,
+        cost_estimate=LITTLE,
         compiler_params=pltpu.CompilerParams(
             collective_id=2, has_side_effects=True, vmem_limit_bytes=20 * 2**20
         ),
@@ -531,24 +671,164 @@
             pltpu.SemaphoreType.DMA((8,)),
             pltpu.SemaphoreType.DMA((8,)),
         ],
+        cost_estimate=LITTLE,
         compiler_params=pltpu.CompilerParams(
             collective_id=3, has_side_effects=True, vmem_limit_bytes=20 * 2**20
         ),
     )(grads)
 
 
-def to_peers(rows):
-    return lax.all_to_all(rows, "grp", split_axis=0, concat_axis=0, tiled=True)
-
-
-def gather_attn(wqkv, wout, segments):
+def exchange_kernel(n, *refs):
+    loads, outs = refs[: 5 * n], refs[5 * n : 6 * n]
+    to_send, got, send_sem, recv_sem = refs[6 * n :]
+    grp, seq = lax.axis_index("grp"), lax.axis_index("seq")
+    peers, half = got.shape[1], got.shape[3]
+    others = [(grp + d) % peers for d in range(1, peers)]
+    greet([(other, seq) for other in others])
+    for i in range(n):
+        x_ref, put_left, put_right = loads[5 * i : 5 * i + 3]
+        rows = dot(put_left[...], x_ref[:, :half]) + dot(put_right[...], x_ref[:, half:])
+        to_send[i] = rows.astype(BF).reshape(to_send.shape[1:])
+    copies = []
+    for k, other in enumerate(others):
+        copies.append(
+            remote(to_send.at[:, other], got.at[:, grp], send_sem.at[k], recv_sem.at[k], (other, seq))
+        )
+        copies[-1].start()
+    got[:, grp] = to_send[:, grp]
+    for copy in copies:
+        copy.wait()
+    for i in range(n):
+        take_left, take_right = loads[5 * i + 3 : 5 * i + 5]
+        came = got[i].reshape(-1, half)
+        outs[i][:, :half] = dot(take_left[...], came, ((0,), (0,))).astype(outs[i].dtype)
+        outs[i][:, half:] = dot(take_right[...], came, ((0,), (0,))).astype(outs[i].dtype)
+
+
+def exchange(number, *loads):
+    peers, n = lax.axis_size("grp"), len(loads)
+    x, put = loads[0][:2]
+    slots = (n, peers, put[0].shape[0] // peers, x.shape[1] // 2)
+    dma = pltpu.SemaphoreType.DMA
+    return pl.pallas_call(
+        functools.partial(exchange_kernel, n),
+        out_shape=tuple(
+            jax.ShapeDtypeStruct((take[0].shape[1], x.shape[1]), dtype) for x, _, take, dtype in loads
+        ),
+        in_specs=vmem_specs(5 * n),
+        out_specs=tuple(vmem_specs(n)),
+        scratch_shapes=[VMEM(slots, BF), VMEM(slots, BF), dma((peers - 1,)), dma((peers - 1,))],
+        cost_estimate=LITTLE,
+        compiler_params=pltpu.CompilerParams(
+            collective_id=4 + number, has_side_effects=True, vmem_limit_bytes=24 * 2**20
+        ),
+    )(*[part for x, put, take, _ in loads for part in (x, *put, *take)])
+
+
+FF_BLOCK = 1024
+GELU_A, GELU_B = 0.7978845608028654, 0.044715
+
+
+def expert_kernel(x_ref, in_ref, out_w_ref, out_ref, pre_ref, total):
+    step = pl.program_id(0)
+
+    @pl.when(step == 0)
+    def _():
+        total[...] = jnp.zeros_like(total)
+
+    pre = dot(x_ref[...], in_ref[...])
+    pre_ref[...] = pre
+    act = 0.5 * pre * (1.0 + jnp.tanh(GELU_A * (pre + GELU_B * pre * pre * pre)))
+    total[...] += dot(act.astype(BF), out_w_ref[...])
+
+    @pl.when(step == pl.num_programs(0) - 1)
+    def _():
+        out_ref[...] = total[...].astype(BF)
+
+
+def expert_forward(rows, first_mat, second_mat):
+    width, hidden = first_mat.shape
+    count = rows.shape[0]
+    return pl.pallas_call(
+        expert_kernel,
+        grid=(hidden // FF_BLOCK,),
+        out_shape=(jax.ShapeDtypeStruct(rows.shape, BF), jax.ShapeDtypeStruct((count, hidden), F32)),
+        in_specs=[
+            pl.BlockSpec((count, width), lambda j: (0, 0)),
+            pl.BlockSpec((width, FF_BLOCK), lambda j: (0, j)),
+            pl.BlockSpec((FF_BLOCK, width), lambda j: (j, 0)),
+        ],
+        out_specs=(
+            pl.BlockSpec((count, width), lambda j: (0, 0)),
+            pl.BlockSpec((count, FF_BLOCK), lambda j: (0, j)),
+        ),
+        scratch_shapes=[VMEM((count, width), F32)],
+        cost_estimate=LITTLE,
+        compiler_params=pltpu.CompilerParams(vmem_limit_bytes=50 * 2**20),
+    )(rows, first_mat, second_mat)
+
+
+def expert_back_kernel(again, x_ref, grad_ref, *refs):
+    pre_ref, in_ref, out_w_ref, out_ref, gx_ref, gin_ref, gout_ref, total, out_total = (
+        (None, *refs) if again else (*refs[:3], None, *refs[3:], None)
+    )
+    step = pl.program_id(0)
+
+    @pl.when(step == 0)
+    def _():
+        total[...] = jnp.zeros_like(total)
+        if again:
+            out_total[...] = jnp.zeros_like(out_total)
+
+    pre = dot(x_ref[...], in_ref[...]) if again else pre_ref[...]
+    grad = grad_ref[...]
+    square = pre * pre
+    curve = jnp.tanh(GELU_A * (pre + GELU_B * pre * square))
+    act = (0.5 * pre * (1.0 + curve)).astype(BF)
+    slope = 0.5 * (1.0 + curve) + 0.5 * pre * (1.0 - curve * curve) * (GELU_A * (1.0 + 3.0 * GELU_B * square))
+    grad_pre = (dot(grad, out_w_ref[...], ((1,), (1,))) * slope).astype(BF)
+    total[...] += dot(grad_pre, in_ref[...], ((1,), (1,)))
+    if again:
+        out_total[...] += dot(act, out_w_ref[...])
+    gin_ref[...] = dot(x_ref[...], grad_pre, ((0,), (0,))).astype(BF)
+    gout_ref[...] = dot(act, grad, ((0,), (0,))).astype(BF)
+
+    @pl.when(step == pl.num_programs(0) - 1)
+    def _():
+        gx_ref[...] = total[...].astype(BF)
+        if again:
+            out_ref[...] = out_total[...].astype(BF)
+
+
+def expert_back(rows, grads, pre, first_mat, second_mat):
+    width, hidden = first_mat.shape
+    count, again = rows.shape[0], pre is None
+    whole = pl.BlockSpec((count, width), lambda j: (0, 0))
+    columns = pl.BlockSpec((width, FF_BLOCK), lambda j: (0, j))
+    lines = pl.BlockSpec((FF_BLOCK, width), lambda j: (j, 0))
+    row_like = jax.ShapeDtypeStruct(rows.shape, BF)
+    return pl.pallas_call(
+        functools.partial(expert_back_kernel, again),
+        grid=(hidden // FF_BLOCK,),
+        out_shape=(row_like,) * (1 + again)
+        + (jax.ShapeDtypeStruct(first_mat.shape, BF), jax.ShapeDtypeStruct(second_mat.shape, BF)),
+        in_specs=[whole, whole]
+        + ([] if again else [pl.BlockSpec((count, FF_BLOCK), lambda j: (0, j))])
+        + [columns, lines],
+        out_specs=(whole,) * (1 + again) + (columns, lines),
+        scratch_shapes=[VMEM((count, width), F32)] * (1 + again),
+        cost_estimate=LITTLE,
+        compiler_params=pltpu.CompilerParams(vmem_limit_bytes=50 * 2**20),
+    )(rows, grads, *(() if again else (pre,)), first_mat, second_mat)
+
+
+def gather_attn(wqkv, wout, segments, pick):
     layers, shard = wqkv.shape[0], wqkv.shape[1]
-    own = jnp.concatenate([wqkv, wout], axis=2).reshape(3, -1, 128)
+    own = jnp.concatenate([wqkv, wout], axis=2).reshape(layers, shard, 2 * SIDE, -1).transpose(2, 0, 1, 3)
+    own = jnp.pad(own, ((0, 0), (0, 0), (0, 16 - shard), (0, 0)))
     seg = jnp.broadcast_to(segments.astype(F32), (8, segments.shape[1]))
-    full, segs = attn_gather(own, seg)
-    full = full.reshape(3, 2 * SIDE**3, -1, 128).transpose(1, 0, 2, 3)
-    full = full.reshape(2 * SIDE**3, layers, shard, -1).transpose(1, 0, 2, 3)
-    return full.reshape(layers, 2 * SIDE**3 * shard, -1), segs[:, :, 0].reshape(1, -1)
+    full, segs = attn_gather(own, seg, pick)
+    return full.reshape(2 * SIDE, layers, D, -1), segs[:, :, 0].reshape(1, -1)
 
 
 def gather_experts(w_in, w_out, layer_index):
@@ -574,6 +854,7 @@
 ):
     count_q = tokens.shape[0]
     experts = lax.axis_size("grp")
+    blocks = lax.axis_size("seq")
     capacity = max(2, 3 * count_q * TOP // (2 * experts))
     window = (BACK + 1) * count_q
     span = window + count_q
@@ -599,8 +880,14 @@
     rank = jnp.sum(ranks * hot.astype(F32), axis=1).astype(jnp.int32)
     target = flat_routes * capacity + rank
     slots = jnp.arange(experts * capacity, dtype=jnp.int32)
-    dispatch = (slots[:, None] == target[None, :]).astype(BF)
-    dispatch_tokens = dispatch[:, :count_q] + dispatch[:, count_q:]
+    halves = jnp.arange(2 * experts * capacity, dtype=jnp.int32)
+    slot, right = halves // (2 * capacity) * capacity + halves % capacity, halves // capacity % 2
+    pairs_at, tokens_at, rows_at = [], [], []
+    for side in range(2):
+        mine = jnp.where(right == side, slot, -1)[:, None]
+        pairs_at.append((mine == target[None, :]).astype(BF))
+        tokens_at.append(pairs_at[-1][:, :count_q] + pairs_at[-1][:, count_q:])
+        rows_at.append((mine == slots[None, :]).astype(BF))
     route_hot = hot.astype(F32).reshape(TOP, count_q, experts)
 
     seg_own = segments[0].astype(F32)
@@ -608,36 +895,48 @@
     hidden_state = tokens.astype(F32)
     gains_a, gains_f = gain_attn.astype(F32), gain_ffn.astype(F32)
     stored = []
-    attn_full, segs = gather_attn(wqkv, wout, segments)
+    shard = wqkv.shape[1]
+    row = jnp.arange(blocks * shard, dtype=jnp.int32)[:, None]
+    pick = (row // shard * 16 + row % shard == jnp.arange(blocks * 16, dtype=jnp.int32)[None, :]).astype(BF)
+    attn_full, segs = gather_attn(wqkv, wout, segments, pick)
     seg_keys = lax.dynamic_slice_in_dim(segs, start, window, axis=1)
     expert_full = [gather_experts(w_in, w_out, l) for l in range(LAYERS)]
     for l in range(LAYERS):
-        qkv_mat, out_mat = attn_full[l][:, : 3 * D], attn_full[l][:, 3 * D :]
         first_mat, second_mat = expert_full[l]
         scale_one = inv_root(hidden_state)
         normed = (hidden_state * scale_one * gains_a[l]).astype(BF)
-        projected = dot(normed, qkv_mat).astype(BF)
+        projected = project(normed, attn_full, l, 0, QKV_BLOCKS, BF)
         queries = projected[:, :D]
         kv_own = projected[:, D:]
         kv = gather_keys(kv_own)
         off_arr = off.reshape(1)
         attended, lse = attention(off_arr, queries, kv, seg_col, seg_keys, bias_rows[l])
-        middle = hidden_state + dot(attended, out_mat)
+        middle = hidden_state + project(attended, attn_full, l, QKV_BLOCKS, 2, F32)
         scale_two = inv_root(middle)
         mixed_in = (middle * scale_two * gains_f[l]).astype(BF)
         router_probs = jax.nn.softmax(dot(mixed_in, router[l]), axis=-1)
         gate_values = jnp.sum(router_probs[None] * route_hot, axis=2)
-        send_rows = dot(dispatch_tokens, mixed_in).astype(BF)
-        expert_rows = to_peers(send_rows.reshape(experts, capacity, D)).reshape(-1, D)
-        pre_act = dot(expert_rows, first_mat)
-        activated = jax.nn.gelu(pre_act).astype(BF)
-        expert_out = dot(activated, second_mat).astype(BF)
-        returned = to_peers(expert_out.reshape(experts, capacity, D)).reshape(-1, D)
-        pair_out = dot(dispatch, returned, ((0,), (0,))).reshape(TOP, count_q, D)
+        if l < LAYERS - 1:
+            (expert_rows,) = exchange(0, (mixed_in, tokens_at, rows_at, BF))
+            expert_out, pre_act = expert_forward(expert_rows, first_mat, second_mat)
+            (pair_out,) = exchange(1, (expert_out, rows_at, pairs_at, F32))
+            last_grads = None
+        else:
+            grad_pairs = (gate_values[:, :, None] * cotangent[None]).astype(BF).reshape(-1, D)
+            expert_rows, grad_rows = exchange(
+                4, (mixed_in, tokens_at, rows_at, BF), (grad_pairs, pairs_at, rows_at, BF)
+            )
+            expert_out, grad_inputs, *last_grads = expert_back(expert_rows, grad_rows, None, first_mat, second_mat)
+            pair_out, grad_mixed = exchange(
+                5, (expert_out, rows_at, pairs_at, F32), (grad_inputs, rows_at, tokens_at, F32)
+            )
+            last_grads = (grad_mixed, *last_grads)
+            pre_act = None
+        pair_out = pair_out.reshape(TOP, count_q, D)
         new_state = middle + jnp.sum(gate_values[:, :, None] * pair_out, axis=0)
         stored.append(
             (hidden_state, scale_one, normed, queries, kv, lse, attended, middle, scale_two,
-             mixed_in, router_probs, gate_values, pair_out, expert_rows, pre_act, activated)
+             mixed_in, router_probs, gate_values, pair_out, expert_rows, pre_act)
         )
         hidden_state = new_state
     out_tokens = hidden_state.astype(BF)
@@ -649,23 +948,20 @@
     second_grads = [None] * LAYERS
     for l in reversed(range(LAYERS)):
         (state_in, scale_one, normed, queries, kv, lse, attended, middle, scale_two,
-         mixed_in, router_probs, gate_values, pair_out, expert_rows, pre_act, activated) = stored[l]
-        qkv_mat, out_mat = attn_full[l][:, : 3 * D], attn_full[l][:, 3 * D :]
+         mixed_in, router_probs, gate_values, pair_out, expert_rows, pre_act) = stored[l]
         first_mat, second_mat = expert_full[l]
         grad_gates = jnp.sum(grad_state[None] * pair_out, axis=2)
-        grad_pairs = (gate_values[:, :, None] * grad_state[None]).astype(BF).reshape(-1, D)
-        send_grads = dot(dispatch, grad_pairs).astype(BF)
-        grad_rows = to_peers(send_grads.reshape(experts, capacity, D)).reshape(-1, D)
-        grad_act = dot(grad_rows, second_mat, ((1,), (1,)))
-        _, gelu_pull = jax.vjp(jax.nn.gelu, pre_act)
-        grad_pre = gelu_pull(grad_act)[0].astype(BF)
-        grad_inputs = dot(grad_pre, first_mat, ((1,), (1,))).astype(BF)
-        grad_back = to_peers(grad_inputs.reshape(experts, capacity, D)).reshape(-1, D)
-        grad_second = dot(activated, grad_rows, ((0,), (0,))).astype(BF)
-        grad_first = dot(expert_rows, grad_pre, ((0,), (0,))).astype(BF)
-        first_grads[l] = lax.psum_scatter(grad_first, "seq", scatter_dimension=0, tiled=True).astype(F32)
-        second_grads[l] = lax.psum_scatter(grad_second, "seq", scatter_dimension=0, tiled=True).astype(F32)
-        grad_mixed = dot(dispatch_tokens, grad_back, ((0,), (0,)))
+        if l == LAYERS - 1:
+            grad_mixed, grad_first, grad_second = last_grads
+        else:
+            grad_pairs = (gate_values[:, :, None] * grad_state[None]).astype(BF).reshape(-1, D)
+            (grad_rows,) = exchange(2, (grad_pairs, pairs_at, rows_at, BF))
+            grad_inputs, grad_first, grad_second = expert_back(
+                expert_rows, grad_rows, pre_act, first_mat, second_mat
+            )
+            (grad_mixed,) = exchange(3, (grad_inputs, rows_at, tokens_at, F32))
+        first_grads[l] = lax.psum_scatter(grad_first, "seq", scatter_dimension=0, tiled=True)
+        second_grads[l] = lax.psum_scatter(grad_second, "seq", scatter_dimension=0, tiled=True)
         grad_probs = jnp.sum(grad_gates[:, :, None] * route_hot, axis=0)
         grad_logits = router_probs * (
             grad_probs - jnp.sum(router_probs * grad_probs, axis=-1, keepdims=True)
@@ -675,8 +971,11 @@
         grad_mid, gain_f_grad = norm_backward(middle, scale_two, gains_f[l], grad_mixed)
         grad_mid = grad_mid + grad_state
         branch_grad = grad_mid.astype(BF)
-        grad_out_proj = dot(attended, branch_grad, ((0,), (0,))).astype(BF)
-        grad_attended = dot(branch_grad, out_mat, ((1,), (1,))).astype(BF)
+        grad_attended = project_back(branch_grad, attn_full, l, QKV_BLOCKS, 2).astype(BF)
+        if l < LAYERS - 1:
+            grad_attended, first_grads[l + 1], second_grads[l + 1] = lax.optimization_barrier(
+                (grad_attended, first_grads[l + 1], second_grads[l + 1])
+            )
         dq, dkv, diag = attention_back(
             off_arr, queries, kv, seg_col, seg_keys, bias_rows[l], lse, grad_attended
         )
@@ -685,22 +984,18 @@
         )
         dkv_own = scatter_key_grads(dkv)
         grad_proj = jnp.concatenate([dq, dkv_own], axis=1)
-        grad_in_proj = dot(normed, grad_proj, ((0,), (0,))).astype(BF)
-        grad_normed = dot(grad_proj, qkv_mat, ((1,), (1,)))
+        grad_normed = project_back(grad_proj, attn_full, l, 0, QKV_BLOCKS)
         grad_prev, gain_a_grad = norm_backward(state_in, scale_one, gains_a[l], grad_normed)
         grad_state = grad_mid + grad_prev
-        attn_grads[l] = jnp.concatenate([grad_in_proj, grad_out_proj], axis=1)
+        attn_grads[l] = weight_grads(normed, attended, grad_proj, branch_grad)
         small[l] = (gain_a_grad, gain_f_grad, router_grad, table_grad)
     sizes = [D, D, D * experts, BUCKETS * HEADS]
     flat = jnp.concatenate([part.reshape(-1) for l in range(LAYERS) for part in small[l]])
     used = flat.size
     padded = -(-used // (3 * 8 * 128)) * 3 * 8 * 128
-    devices = 2 * SIDE**3
-    whole = jnp.stack(attn_grads).reshape(LAYERS, devices, -1, 128).transpose(1, 0, 2, 3)
-    whole = whole.reshape(devices, 3, -1, 128).transpose(1, 0, 2, 3)
-    whole = whole.reshape(3, SIDE, SIDE, SIDE, 2, -1, 128)
-    attn, flat = reduce_all(whole, jnp.pad(flat, (0, padded - used)).reshape(3, -1, 128))
-    attn = attn.reshape(LAYERS, -1, 4 * D)
+    whole = [g.reshape(SIDE, 2, SIDE, SIDE, 3, 16, -1) for g in attn_grads]
+    attn, flat = reduce_all(*whole, jnp.pad(flat, (0, padded - used)).reshape(3, -1, 128), pick)
+    attn = attn[:, :, :shard].astype(F32).transpose(1, 2, 0, 3).reshape(LAYERS, shard, -1)
     flat = flat.reshape(-1)[:used].reshape(LAYERS, -1)
     sums, at = [], 0
     for size in sizes:
@@ -715,8 +1010,8 @@
         sums[3].reshape(LAYERS, BUCKETS, HEADS),
         sums[1],
         sums[2].reshape(LAYERS, D, experts),
-        jnp.stack(first_grads)[:, None],
-        jnp.stack(second_grads)[:, None],
+        jnp.stack(first_grads)[:, None].astype(F32),
+        jnp.stack(second_grads)[:, None].astype(F32),
     )
 
 

time: 618 us -> 541 us (0.88)
  Pallas kernels: 236 us -> 438 us
  matrix products: 127 us -> 7.68 us
  local copies, waits for them, and re-layouts: 112 us -> 40.2 us
  starting transfers between devices: 33.3 us -> 0.49 us
  waiting for transfers between devices: 31.3 us -> 2.54 us
  blocking collectives: 14.6 us -> 0 us
  other arithmetic: 35.4 us -> 25.1 us
    pallas_call x2 -> x21, Pallas kernels: 108 us -> 301 us  [the longest x6 107 us: exchange(): pl.pallas_call(functools.partial(exchange_kernel, n), out_shape=tuple((ja...]
    dot_general x38 -> x6, matrix products: 118 us -> 1.5 us  [dot(): lax.dot_general(a, b, (contract, ((), ())), preferred_element_type=F32)]
    all_to_all x7 -> x0, starting transfers between devices: 32.8 us -> none  [to_peers(): return lax.all_to_all(rows, 'grp', split_axis=0, concat_axis=0, tiled=True)]
    all_to_all x7 -> x0, waiting for transfers between devices: 29.9 us -> none  [to_peers(): return lax.all_to_all(rows, 'grp', split_axis=0, concat_axis=0, tiled=True)]
    slice x4 -> x1, local copies, waits for them, and re-layouts: 25.7 us -> 0.01 us  [gather_attn(): return (full.reshape(2 * SIDE, layers, D, -1), segs[:, :, 0].reshape(1, -1))]
    another operation x2 -> x0, local copies, waits for them, and re-layouts: 17 us -> none  [on_device(): jnp.stack(attn_grads).reshape(LAYERS, devices, -1, 128)]
    squeeze x2 -> x0, local copies, waits for them, and re-layouts: 15.7 us -> none  [on_device(): qkv_mat, out_mat = (attn_full[l][:, :3 * D], attn_full[l][:, 3 * D:])]
    all_to_all x1 -> x0, blocking collectives: 14.6 us -> none  [to_peers(): return lax.all_to_all(rows, 'grp', split_axis=0, concat_axis=0, tiled=True)]
  transfers between devices with their start and end apart: 15 -> 8, of which waited for: 5 -> 0; matrix products, arithmetic and copies ran while one was open for 40% -> 8% of each run, Pallas kernels for 39% -> 79%
where the time goes in v3:
time: 541 us; the launch traced here: 530 us
  Pallas kernels  438 us (81%)
  local copies, waits for them, and re-layouts  40.2 us (7%)
  other arithmetic  25.1 us (5%)
  between operations  16.4 us (3%)
  matrix products  7.68 us (1%)
    pallas_call x6, Pallas kernels, exchange(): pl.pallas_call(functools.partial(exchange_kernel, n), out_shape=tuple((ja...  107 us
    pallas_call x2, Pallas kernels, gather_keys(): pl.pallas_call(kv_gather, out_shape=jax.ShapeDtypeStruct((2 * SIDE * own....  58.5 us
    pallas_call x1, Pallas kernels, attn_gather(): pl.pallas_call(attn_gather_kernel, out_shape=(jax.ShapeDtypeStruct((SIDE,...  58.5 us
    pallas_call x1, Pallas kernels, reduce_all(): pl.pallas_call(reduce_kernel, out_shape=(jax.ShapeDtypeStruct(rows, BF),...  57.9 us
    pallas_call x2, Pallas kernels, scatter_key_grads(): pl.pallas_call(kv_scatter, out_shape=jax.ShapeDtypeStruct(block, BF), in_...  51.3 us
    pallas_call x2, Pallas kernels, expert_back(): pl.pallas_call(functools.partial(expert_back_kernel, again), grid=(hidden...  33.1 us
    unnamed x281, local copies, waits for them, and re-layouts  24.8 us
    pallas_call x2, Pallas kernels, attention_back(): pl.pallas_call(attention_back_kernel, out_shape=(jax.ShapeDtypeStruct(que...  17.3 us
  transfers between devices with their start and end apart: 8, of which 0 were waited for; matrix products, arithmetic and copies ran while one was open for 8% of the time, Pallas kernels for 79%

profile of v3, /device:TPU:1, one launch (start us, length us, event | category | flops | bytes accessed | tf_op | source)
XLA Modules:
  0.0 530.5 jit_solution(5369752891580904548)
XLA Ops:
  7.2 2.4 fusion.77
  9.8 1.1 fusion.76
  12.6 58.5 %shard_map.204 = (bf16[4,2,2,4,4,3,16,384]{7,6,5,4,3,2,1,0:T(8,128)(2,1)S(1)}, f32[4,2,8,128]{3,2,1,0:T(8,128)S(1)}) custom-call(bf16[8,2,16,384]{3,2,1,0:T(8,128)(2,1)S(1)} %pad.8.own_ref, f32[8,128]{1,0:T(8,128)S(1)} %broadcast_in_dim.7.seg_ref, bf16[48,128]{1,0:T(8,128)(2,1)S(1)} %fusion.40.pick_ref), custom_call_target="tpu_custom_call" | custom-call | flops 1024 | bytes 1024 | tf_op jit(solution)/shard_map/pallas_call | solution.py:288
  71.1 3.7 copy-done
  76.9 3.5 shard_map.205
  80.4 1.0 slice.132.own_ref
  81.4 33.3 %shard_map.206.kv_ref = bf16[1024,1536]{1,0:T(8,128)(2,1)S(1)} custom-call(bf16[128,1536]{1,0:T(8,128)(2,1)S(1)} %slice.132.own_ref), custom_call_target="tpu_custom_call" | custom-call | flops 1024 | bytes 1024 | tf_op jit(solution)/shard_map/pallas_call | solution.py:646
  114.7 1.2 slice.131.q_ref
  117.7 5.2 shard_map.207
  123.6 2.5 shard_map.208
  127.1 1.1 multiply_reduce_fusion.10
  129.8 15.0 %shard_map.209.x_ref = bf16[384,768]{1,0:T(8,128)(2,1)S(1)} custom-call(bf16[128,768]{1,0:T(8,128)(2,1)S(1)} %multiply_convert_fusion.2.refs_0_, bf16[768,128]{1,0:T(8,128)(2,1)S(1)} %get-tuple-element.146.refs_1_.refs_8_.refs_3_, bf16[768,128]{1,0:T(8,128)(2,1)S(1)} %get-tuple-element.145.refs_2_.refs_9_.refs_4_, ...), custom_call_target="tpu_custom_call" | custom-call | flops 1024 | bytes 1024 | tf_op jit(solution)/shard_map/pallas_call | solution.py:713
  146.8 8.8 %shard_map.210 = (bf16[384,768]{1,0:T(8,128)(2,1)S(1)}, f32[384,3072]{1,0:T(8,128)}) custom-call(bf16[384,768]{1,0:T(8,128)(2,1)S(1)} %shard_map.209.x_ref, bf16[768,3072]{1,0:T(8,128)(2,1)} %bitcast.105, bf16[3072,768]{1,0:T(8,128)(2,1)} %bitcast.107), custom_call_target="tpu_custom_call" | custom-call | flops 1024 | bytes 1024 | tf_op jit(solution)/shard_map/pallas_call | solution.py:752
  155.6 14.8 %shard_map.211 = f32[256,768]{1,0:T(8,128)S(1)} custom-call(bf16[384,768]{1,0:T(8,128)(2,1)S(1)} %get-tuple-element.43.refs_0_, bf16[768,384]{1,0:T(8,128)(2,1)S(1)} %get-tuple-element.147.refs_3_.refs_1_.refs_8_.refs_6_, bf16[768,384]{1,0:T(8,128)(2,1)S(1)} %get-tuple-element.148.refs_4_.refs_2_.refs_9_.refs_7_, ...), custom_call_target="tpu_custom_call" | custom-call | flops 1024 | bytes 1024 | tf_op jit(solution)/shard_map/pallas_call | solution.py:713
  172.1 3.7 shard_map.212
  175.8 1.1 slice.140.own_ref
  177.0 25.2 %shard_map.213.kv_ref = bf16[1024,1536]{1,0:T(8,128)(2,1)S(1)} custom-call(bf16[128,1536]{1,0:T(8,128)(2,1)S(1)} %slice.140.own_ref), custom_call_target="tpu_custom_call" | custom-call | flops 1024 | bytes 1024 | tf_op jit(solution)/shard_map/pallas_call | solution.py:646
  202.2 0.9 slice.139.q_ref
  203.2 5.2 shard_map.214
  208.4 1.6 copy-done.3
  211.4 2.5 shard_map.215
  213.9 1.2 multiply_reduce_fusion.8
  217.9 23.9 %shard_map.216 = (bf16[384,768]{1,0:T(8,128)(2,1)S(1)}, bf16[384,768]{1,0:T(8,128)(2,1)S(1)}) custom-call(bf16[128,768]{1,0:T(8,128)(2,1)S(1)} %multiply_convert_fusion.refs_0_, bf16[768,128]{1,0:T(8,128)(2,1)S(1)} %copy-done.6, bf16[768,128]{1,0:T(8,128)(2,1)S(1)} %get-tuple-element.145.refs_2_.refs_9_.refs_4_, ...), custom_call_target="tpu_custom_call" | custom-call | flops 1024 | bytes 1024 | tf_op jit(solution)/shard_map/pallas_call | solution.py:713
  243.5 1.1 copy-done.29
  244.6 1.1 copy-done.31
  245.6 18.2 %shard_map.217 = (bf16[384,768]{1,0:T(8,128)(2,1)S(1)}, bf16[384,768]{1,0:T(8,128)(2,1)S(1)}, bf16[768,3072]{1,0:T(8,128)(2,1)}, bf16[3072,768]{1,0:T(8,128)(2,1)}) custom-call(bf16[384,768]{1,0:T(8,128)(2,1)S(1)} %copy-done.29, bf16[384,768]{1,0:T(8,128)(2,1)S(1)} %copy-done.31, bf16[768,3072]{1,0:T(8,128)(2,1)} %bitcast.109, bf16[3072,768]{1,0:T(8,128)(2,1)} %bitcast.110), custom_call_target="tpu_custom_call" | custom-call | flops 1024 | bytes 1024 | tf_op jit(solution)/shard_map/pallas_call | solution.py:810
  266.3 0.9 copy-done.7
  267.2 1.1 copy-done.25
  268.3 1.1 copy-done.27
  269.4 22.0 %shard_map.218 = (f32[256,768]{1,0:T(8,128)S(1)}, f32[128,768]{1,0:T(8,128)S(1)}) custom-call(bf16[384,768]{1,0:T(8,128)(2,1)S(1)} %copy-done.25, bf16[768,384]{1,0:T(8,128)(2,1)S(1)} %get-tuple-element.147.refs_3_.refs_1_.refs_8_.refs_6_, bf16[768,384]{1,0:T(8,128)(2,1)S(1)} %get-tuple-element.148.refs_4_.refs_2_.refs_9_.refs_7_, ...), custom_call_target="tpu_custom_call" | custom-call | flops 1024 | bytes 1024 | tf_op jit(solution)/shard_map/pallas_call | solution.py:713
  292.4 1.0 multiply_reduce_fusion.2
  293.5 0.9 fusion.75
  294.4 2.8 shard_map.219
  297.2 1.0 convert_element_type.191.grad_ref
  298.3 8.7 %shard_map.220 = (bf16[128,768]{1,0:T(8,128)(2,1)S(1)}, bf16[8,128,1536]{2,1,0:T(8,128)(2,1)S(1)}, f32[12,768]{1,0:T(8,128)S(1)}) custom-call(s32[1]{0:T(128)} %bitcast.off_ref, bf16[128,768]{1,0:T(8,128)(2,1)S(1)} %copy-done.16, bf16[1024,1536]{1,0:T(8,128)(2,1)S(1)} %copy-done.4, f32[128,1]{1,0:T(8,128)S(1)} %copy-done.19, ...), custom_call_target="tpu_custom_call" | custom-call | flops 1024 | bytes 1024 | tf_op jit(solution)/shard_map/pallas_call | solution.py:152
  307.0 25.3 %shard_map.221 = bf16[128,1536]{1,0:T(8,128)(2,1)S(1)} custom-call(bf16[8,128,1536]{2,1,0:T(8,128)(2,1)S(1)} %get-tuple-element.53.grads_ref), custom_call_target="tpu_custom_call" | custom-call | flops 1024 | bytes 1024 | tf_op jit(solution)/shard_map/pallas_call | solution.py:661
  332.3 0.9 pad_maximum_fusion.x_ref.proj_ref
  333.1 3.8 shard_map.222
  336.9 1.7 multiply_reduce_fusion.3
  338.7 1.1 subtract_add_fusion.1
  340.6 16.2 %shard_map.223.grad_ref = bf16[384,768]{1,0:T(8,128)(2,1)S(1)} custom-call(bf16[256,768]{1,0:T(8,128)(2,1)S(1)} %get-tuple-element.117.refs_0_, bf16[768,256]{1,0:T(8,128)(2,1)S(1)} %get-tuple-element.126.refs_3_.refs_6_.refs_1_, bf16[768,256]{1,0:T(8,128)(2,1)S(1)} %get-tuple-element.125.refs_4_.refs_7_.refs_2_, ...), custom_call_target="tpu_custom_call" | custom-call | flops 1024 | bytes 1024 | tf_op jit(solution)/shard_map/pallas_call | solution.py:713
  356.7 14.9 %shard_map.224 = (bf16[384,768]{1,0:T(8,128)(2,1)S(1)}, bf16[768,3072]{1,0:T(8,128)(2,1)}, bf16[3072,768]{1,0:T(8,128)(2,1)}) custom-call(bf16[384,768]{1,0:T(8,128)(2,1)S(1)} %shard_map.209.x_ref, bf16[384,768]{1,0:T(8,128)(2,1)S(1)} %shard_map.223.grad_ref, f32[384,3072]{1,0:T(8,128)} %get-tuple-element.54.refs_0_, bf16[768,3072]{1,0:T(8,128)(2,1)} %bitcast.106, ...), custom_call_target="tpu_custom_call" | custom-call | flops 1024 | bytes 1024 | tf_op jit(solution)/shard_map/pallas_call | solution.py:810
  372.5 5.0 shard_map.231
  377.6 14.8 %shard_map.225 = f32[128,768]{1,0:T(8,128)S(1)} custom-call(bf16[384,768]{1,0:T(8,128)(2,1)S(1)} %get-tuple-element.55.refs_0_, bf16[768,384]{1,0:T(8,128)(2,1)S(1)} %get-tuple-element.147.refs_3_.refs_1_.refs_8_.refs_6_, bf16[768,384]{1,0:T(8,128)(2,1)S(1)} %get-tuple-element.148.refs_4_.refs_2_.refs_9_.refs_7_, bf16[768,128]{1,0:T(8,128)(2,1)S(1)} %copy-done.8, ...), custom_call_target="tpu_custom_call" | custom-call | flops 1024 | bytes 1024 | tf_op jit(solution)/shard_map/pallas_call | solution.py:713
  392.6 1.0 multiply_reduce_fusion.4
  393.6 1.0 fusion.74
  394.6 2.8 shard_map.226
  397.4 1.7 convert_element_type.194.grad_ref
  399.2 1.1 fusion.69
  400.3 1.8 reshape.398
  402.1 1.8 fusion.70
  403.9 1.2 reshape.396
  405.1 1.0 fusion.20
  407.0 0.9 copy-done.23
  409.6 8.7 %shard_map.227 = (bf16[128,768]{1,0:T(8,128)(2,1)S(1)}, bf16[8,128,1536]{2,1,0:T(8,128)(2,1)S(1)}, f32[12,768]{1,0:T(8,128)S(1)}) custom-call(s32[1]{0:T(128)} %bitcast.off_ref, bf16[128,768]{1,0:T(8,128)(2,1)S(1)} %copy-done.14, bf16[1024,1536]{1,0:T(8,128)(2,1)S(1)} %copy-done.2, f32[128,1]{1,0:T(8,128)S(1)} %copy-done.20, ...), custom_call_target="tpu_custom_call" | custom-call | flops 1024 | bytes 1024 | tf_op jit(solution)/shard_map/pallas_call | solution.py:152
  418.3 26.0 %shard_map.228 = bf16[128,1536]{1,0:T(8,128)(2,1)S(1)} custom-call(bf16[8,128,1536]{2,1,0:T(8,128)(2,1)S(1)} %get-tuple-element.61.grads_ref), custom_call_target="tpu_custom_call" | custom-call | flops 1024 | bytes 1024 | tf_op jit(solution)/shard_map/pallas_call | solution.py:661
  444.3 0.9 pad_maximum_fusion.1.x_ref.proj_ref
  445.3 3.7 shard_map.229
  449.1 5.2 shard_map.230
  454.9 57.9 %shard_map.232 = (bf16[8,2,16,384]{3,2,1,0:T(8,128)(2,1)S(1)}, f32[3,80,128]{2,1,0:T(8,128)S(1)}) custom-call(bf16[4,2,4,4,3,16,384]{6,5,4,3,2,1,0:T(8,128)(2,1)} %bitcast.104, bf16[4,2,4,4,3,16,384]{6,5,4,3,2,1,0:T(8,128)(2,1)} %bitcast.103, f32[3,80,128]{2,1,0:T(8,128)S(1)} %bitcast.101, bf16[48,128]{1,0:T(8,128)(2,1)S(1)} %fusion.40.pick_ref), custom_call_target="tpu_custom_call" | custom-call | flops 1024 | bytes 1024 | tf_op jit(solution)/shard_map/pallas_call | solution.py:452
  514.7 0.9 copy.58
  516.4 2.6 maximum_convert_fusion.1
  519.6 2.6 maximum_convert_fusion
  522.3 0.9 fusion.15
  (379 shorter events, 29.4 us)
Async XLA Ops:
  7.2 139.6 %all-gather.9.cloned.1.call-start = ((), (), s32[]{:S(2)}) async-start(), calls=%async_computation.8 | async-start | bytes 5308416 | tf_op jit(solution)/shard_map/all_gather | solution.py:835
  9.7 65.1 %copy-start.128 = (bf16[2,768]{1,0:T(2,128)(2,1)S(1)}, bf16[2,768]{1,0:T(2,128)(2,1)}, u32[]{:S(2)}) copy-start(bf16[2,768]{1,0:T(2,128)(2,1)} %param.17) | copy-start | bytes 9220
  9.7 65.7 %copy-start.48 = (bf16[128,768]{1,0:T(8,128)(2,1)S(1)}, bf16[128,768]{1,0:T(8,128)(2,1)}, u32[]{:S(2)}) copy-start(bf16[128,768]{1,0:T(8,128)(2,1)} %param.13) | copy-start | bytes 589828
  9.7 137.1 %all-gather.11.cloned.1.call-start = ((), (), s32[]{:S(2)}) async-start(), calls=%async_computation.9 | async-start | bytes 5308416 | tf_op jit(solution)/shard_map/all_gather | solution.py:836
  10.9 232.6 %all-gather.13.cloned.1.call-start = ((), (), s32[]{:S(2)}) async-start(), calls=%async_computation.10 | async-start | bytes 5308416 | tf_op jit(solution)/shard_map/all_gather | solution.py:835
  11.6 231.9 %all-gather.15.cloned.1.call-start = ((), (), s32[]{:S(2)}) async-start(), calls=%async_computation.11 | async-start | bytes 5308416 | tf_op jit(solution)/shard_map/all_gather | solution.py:836
  12.2 393.9 %reduce-scatter.5.cloned.1.call-start = ((), (), s32[]{:S(2)}) async-start(), calls=%async_computation.4 | async-start | bytes 5308416 | tf_op jit(solution)/shard_map/reduce_scatter | solution.py:963
  80.4 35.6 %copy-start.127 = (s32[1024]{0:T(1024)S(1)}, s32[1024]{0:T(1024)}, u32[]{:S(2)}) copy-start(s32[1024]{0:T(1024)} %param.15) | copy-start | bytes 12292
  81.4 35.5 %copy-start.94 = (bf16[2,32,12]{1,0,2:T(2,128)(2,1)S(1)}, bf16[2,32,12]{1,0,2:T(2,128)(2,1)}, u32[]{:S(2)}) copy-start(bf16[2,32,12]{1,0,2:T(2,128)(2,1)} %param.20) | copy-start | bytes 4612
  114.7 8.2 %copy-start.1 = (bf16[1024,1536]{1,0:T(8,128)(2,1)}, bf16[1024,1536]{1,0:T(8,128)(2,1)S(1)}, u32[]{:S(2)}) copy-start(bf16[1024,1536]{1,0:T(8,128)(2,1)S(1)} %shard_map.206.kv_ref) | copy-start | bytes 9437188
  115.9 10.2 %copy-start.13 = (bf16[128,768]{1,0:T(8,128)(2,1)}, bf16[128,768]{1,0:T(8,128)(2,1)S(1)}, u32[]{:S(2)}) copy-start(bf16[128,768]{1,0:T(8,128)(2,1)S(1)} %slice.131.q_ref) | copy-start | bytes 589828
  116.9 9.3 %copy-start.17 = (f32[128,1]{1,0:T(8,128)}, f32[128,1]{1,0:T(8,128)S(1)}, u32[]{:S(2)}) copy-start(f32[128,1]{1,0:T(8,128)S(1)} %copy.47.segq_ref) | copy-start | bytes 1540
  116.9 9.2 %copy-start.97 = (pred[768]{0:T(1024)(128)(4,1)}, pred[768]{0:T(1024)(128)(4,1)S(1)}, u32[]{:S(2)}) copy-start(pred[768]{0:T(1024)(128)(4,1)S(1)} %compare_and_fusion) | copy-start | bytes 2308
  128.9 16.7 %copy-start.90 = (s32[2,128]{1,0:T(2,128)}, s32[2,128]{1,0:T(2,128)S(1)}, u32[]{:S(2)}) copy-start(s32[2,128]{1,0:T(2,128)S(1)} %get-tuple-element.123) | copy-start | bytes 3076
  129.0 15.8 %copy-start.11 = (bf16[128,768]{1,0:T(8,128)(2,1)}, bf16[128,768]{1,0:T(8,128)(2,1)S(1)}, u32[]{:S(2)}) copy-start(bf16[128,768]{1,0:T(8,128)(2,1)S(1)} %multiply_convert_fusion.2.refs_0_) | copy-start | bytes 589828
  129.4 15.3 %copy-start.61 = (bf16[2,768,16]{1,2,0:T(8,128)(2,1)S(1)}, bf16[2,768,16]{1,2,0:T(8,128)(2,1)}, u32[]{:S(2)}) copy-start(bf16[2,768,16]{1,2,0:T(8,128)(2,1)} %param.22) | copy-start | bytes 147460
  129.5 26.1 %copy-start.5 = (bf16[768,128]{1,0:T(8,128)(2,1)}, bf16[768,128]{1,0:T(8,128)(2,1)S(1)}, u32[]{:S(2)}) copy-start(bf16[768,128]{1,0:T(8,128)(2,1)S(1)} %get-tuple-element.146.refs_1_.refs_8_.refs_3_) | copy-start | bytes 589828
  155.6 14.8 %copy-start.103 = (f32[2,128]{1,0:T(2,128)S(1)}, f32[2,128]{1,0:T(2,128)}, u32[]{:S(2)}) copy-start(f32[2,128]{1,0:T(2,128)} %fusion.45) | copy-start | bytes 3076
  155.6 15.0 %copy-start.42 = (f32[128,768]{1,0:T(8,128)S(1)}, f32[128,768]{1,0:T(8,128)}, u32[]{:S(2)}) copy-start(f32[128,768]{1,0:T(8,128)} %copy-done.41) | copy-start | bytes 1179652
  155.6 15.8 %copy-start.83 = (f32[768]{0:T(1024)S(1)}, f32[768]{0:T(1024)}, u32[]{:S(2)}) copy-start(f32[768]{0:T(1024)} %get-tuple-element.100) | copy-start | bytes 9220
  170.7 43.2 %copy-start.44 = (f32[128,768]{1,0:T(8,128)}, f32[128,768]{1,0:T(8,128)S(1)}, u32[]{:S(2)}) copy-start(f32[128,768]{1,0:T(8,128)S(1)} %get-tuple-element.109) | copy-start | bytes 1179652
  175.8 27.4 %copy-start.18 = (f32[128,1]{1,0:T(8,128)S(1)}, f32[128,1]{1,0:T(8,128)}, u32[]{:S(2)}) copy-start(f32[128,1]{1,0:T(8,128)} %copy-done.17) | copy-start | bytes 1540
  177.0 31.4 %copy-start.34 = (f32[12,768]{1,0:T(8,128)}, f32[12,768]{1,0:T(8,128)S(1)}, u32[]{:S(2)}) copy-start(f32[12,768]{1,0:T(8,128)S(1)} %convolution_bitcast_fusion.bias_ref) | copy-start | bytes 110596
  203.2 5.2 copy-start.15
  211.4 5.2 copy-start.91
  211.4 6.4 %copy-start.52 = (f32[128,768]{1,0:T(8,128)S(1)}, f32[128,768]{1,0:T(8,128)}, u32[]{:S(2)}) copy-start(f32[128,768]{1,0:T(8,128)} %param.25) | copy-start | bytes 1179652
  265.5 140.6 %reduce-scatter.7.cloned.1.call-start = ((), (), s32[]{:S(2)}) async-start(), calls=%async_computation.5 | async-start | bytes 5308416 | tf_op jit(solution)/shard_map/reduce_scatter | solution.py:964
  266.1 250.3 %reduce-scatter.11.cloned.1.call-start = ((), (), s32[]{:S(2)}) async-start(), calls=%async_computation.7 | async-start | bytes 5308416 | tf_op jit(solution)/shard_map/reduce_scatter | solution.py:964
  269.4 22.1 %copy-start.53 = (f32[128,768]{1,0:T(8,128)S(1)}, f32[128,768]{1,0:T(8,128)}, u32[]{:S(2)}) copy-start(f32[128,768]{1,0:T(8,128)} %param.25) | copy-start | bytes 1179652
  269.4 22.3 %copy-start.92 = (s32[2,128]{1,0:T(2,128)S(1)}, s32[2,128]{1,0:T(2,128)}, u32[]{:S(2)}) copy-start(s32[2,128]{1,0:T(2,128)} %copy-done.90) | copy-start | bytes 3076
  269.4 22.3 %copy-start.68 = (f32[128,16]{0,1:T(8,128)S(1)}, f32[128,16]{0,1:T(8,128)}, u32[]{:S(2)}) copy-start(f32[128,16]{0,1:T(8,128)} %copy-done.67) | copy-start | bytes 24580
  269.4 22.3 %copy-start.110 = (f32[128]{0:T(128)S(1)}, f32[128]{0:T(128)}, u32[]{:S(2)}) copy-start(f32[128]{0:T(128)} %copy-done.109) | copy-start | bytes 1540
  269.4 22.3 %copy-start.118 = (f32[128]{0:T(128)S(1)}, f32[128]{0:T(128)}, u32[]{:S(2)}) copy-start(f32[128]{0:T(128)} %copy-done.117) | copy-start | bytes 1540
  269.4 22.4 %copy-start.106 = (f32[2,128]{1,0:T(2,128)S(1)}, f32[2,128]{1,0:T(2,128)}, u32[]{:S(2)}) copy-start(f32[2,128]{1,0:T(2,128)} %copy-done.105) | copy-start | bytes 3076
  307.0 26.2 %copy-start.40 = (f32[12,768]{1,0:T(8,128)}, f32[12,768]{1,0:T(8,128)S(1)}, u32[]{:S(2)}) copy-start(f32[12,768]{1,0:T(8,128)S(1)} %get-tuple-element.63) | copy-start | bytes 110596
  333.1 5.6 %copy-start.131 = (f32[128]{0:T(128)S(1)}, f32[128]{0:T(128)}, u32[]{:S(2)}) copy-start(f32[128]{0:T(128)} %get-tuple-element.133) | copy-start | bytes 1540
  339.8 31.9 %copy-start.54 = (f32[128,768]{1,0:T(8,128)}, f32[128,768]{1,0:T(8,128)S(1)}, u32[]{:S(2)}) copy-start(f32[128,768]{1,0:T(8,128)S(1)} %subtract_add_fusion.1) | copy-start | bytes 1179652
  371.7 147.9 %reduce-scatter.9.cloned.1.call-start = ((), (), s32[]{:S(2)}) async-start(), calls=%async_computation.6 | async-start | bytes 5308416 | tf_op jit(solution)/shard_map/reduce_scatter | solution.py:963
  377.5 14.9 %copy-start.93 = (s32[2,128]{1,0:T(2,128)S(1)}, s32[2,128]{1,0:T(2,128)}, u32[]{:S(2)}) copy-start(s32[2,128]{1,0:T(2,128)} %copy-done.90) | copy-start | bytes 3076
  377.5 14.9 %copy-start.126 = (f32[256]{0:T(256)S(1)}, f32[256]{0:T(256)}, u32[]{:S(2)}) copy-start(f32[256]{0:T(256)} %get-tuple-element.116) | copy-start | bytes 3076
  377.5 15.0 %copy-start.66 = (f32[128,16]{0,1:T(8,128)S(1)}, f32[128,16]{0,1:T(8,128)}, u32[]{:S(2)}) copy-start(f32[128,16]{0,1:T(8,128)} %copy-done.65) | copy-start | bytes 24580
  377.5 15.0 %copy-start.108 = (f32[128]{0:T(128)S(1)}, f32[128]{0:T(128)}, u32[]{:S(2)}) copy-start(f32[128]{0:T(128)} %copy-done.107) | copy-start | bytes 1540
  377.5 15.0 %copy-start.116 = (f32[128]{0:T(128)S(1)}, f32[128]{0:T(128)}, u32[]{:S(2)}) copy-start(f32[128]{0:T(128)} %copy-done.115) | copy-start | bytes 1540
  377.5 15.0 %copy-start.43 = (f32[128,768]{1,0:T(8,128)S(1)}, f32[128,768]{1,0:T(8,128)}, u32[]{:S(2)}) copy-start(f32[128,768]{1,0:T(8,128)} %copy-done.41) | copy-start | bytes 1179652
  377.6 15.0 %copy-start.64 = (bf16[2,768,16]{1,2,0:T(8,128)(2,1)S(1)}, bf16[2,768,16]{1,2,0:T(8,128)(2,1)}, u32[]{:S(2)}) copy-start(bf16[2,768,16]{1,2,0:T(8,128)(2,1)} %param.22) | copy-start | bytes 147460
  377.6 15.0 %copy-start.70 = (f32[128,16]{0,1:T(8,128)S(1)}, f32[128,16]{0,1:T(8,128)}, u32[]{:S(2)}) copy-start(f32[128,16]{0,1:T(8,128)} %copy-done.69) | copy-start | bytes 24580
  377.6 15.0 %copy-start.86 = (f32[768]{0:T(1024)S(1)}, f32[768]{0:T(1024)}, u32[]{:S(2)}) copy-start(f32[768]{0:T(1024)} %copy-done.85) | copy-start | bytes 9220
  377.6 15.0 %copy-start.120 = (f32[128]{0:T(128)S(1)}, f32[128]{0:T(128)}, u32[]{:S(2)}) copy-start(f32[128]{0:T(128)} %copy-done.119) | copy-start | bytes 1540
  377.6 16.0 %copy-start.55 = (f32[128,768]{1,0:T(8,128)S(1)}, f32[128,768]{1,0:T(8,128)}, u32[]{:S(2)}) copy-start(f32[128,768]{1,0:T(8,128)} %copy-done.54) | copy-start | bytes 1179652
  377.6 16.0 %copy-start.133 = (f32[128]{0:T(128)S(1)}, f32[128]{0:T(128)}, u32[]{:S(2)}) copy-start(f32[128]{0:T(128)} %get-tuple-element.131) | copy-start | bytes 1540
  394.6 7.5 %copy-start.12 = (bf16[128,768]{1,0:T(8,128)(2,1)S(1)}, bf16[128,768]{1,0:T(8,128)(2,1)}, u32[]{:S(2)}) copy-start(bf16[128,768]{1,0:T(8,128)(2,1)} %copy-done.11) | copy-start | bytes 589828
  394.6 11.5 %copy-start.2 = (bf16[1024,1536]{1,0:T(8,128)(2,1)S(1)}, bf16[1024,1536]{1,0:T(8,128)(2,1)}, u32[]{:S(2)}) copy-start(bf16[1024,1536]{1,0:T(8,128)(2,1)} %copy-done.1) | copy-start | bytes 9437188
  397.4 8.7 %copy-start.14 = (bf16[128,768]{1,0:T(8,128)(2,1)S(1)}, bf16[128,768]{1,0:T(8,128)(2,1)}, u32[]{:S(2)}) copy-start(bf16[128,768]{1,0:T(8,128)(2,1)} %copy-done.13) | copy-start | bytes 589828
  449.0 5.3 copy-start.80
  449.0 5.3 copy-start.99
  449.0 5.6 %copy-start.50 = (bf16[128,768]{1,0:T(8,128)(2,1)S(1)}, bf16[128,768]{1,0:T(8,128)(2,1)}, u32[]{:S(2)}) copy-start(bf16[128,768]{1,0:T(8,128)(2,1)} %param.13) | copy-start | bytes 589828
  449.0 5.6 %copy-start.51 = (f32[128,768]{1,0:T(8,128)S(1)}, f32[128,768]{1,0:T(8,128)}, u32[]{:S(2)}) copy-start(f32[128,768]{1,0:T(8,128)} %shard_map.229) | copy-start | bytes 1179652
  449.0 5.6 %copy-start.82 = (f32[768]{0:T(1024)S(1)}, f32[768]{0:T(1024)}, u32[]{:S(2)}) copy-start(f32[768]{0:T(1024)} %copy-done.81) | copy-start | bytes 9220
  449.0 5.6 %copy-start.114 = (f32[128]{0:T(128)S(1)}, f32[128]{0:T(128)}, u32[]{:S(2)}) copy-start(f32[128]{0:T(128)} %copy-done.113) | copy-start | bytes 1540
  449.0 5.7 %copy-start.77 = (f32[28416]{0:T(1024)S(1)}, f32[28416]{0:T(1024)}, u32[]{:S(2)}) copy-start(f32[28416]{0:T(1024)} %custom-call) | copy-start | bytes 340996
  449.1 5.7 %copy-start.102 = (f32[768]{0:T(1024)S(1)}, f32[768]{0:T(1024)}, u32[]{:S(2)}) copy-start(f32[768]{0:T(1024)} %get-tuple-element.94) | copy-start | bytes 9220
  449.1 5.8 %copy-start.100 = (f32[768]{0:T(1024)S(1)}, f32[768]{0:T(1024)}, u32[]{:S(2)}) copy-start(f32[768]{0:T(1024)} %get-tuple-element.92) | copy-start | bytes 9220
  449.1 5.8 %copy-start.101 = (f32[768]{0:T(1024)S(1)}, f32[768]{0:T(1024)}, u32[]{:S(2)}) copy-start(f32[768]{0:T(1024)} %get-tuple-element.90) | copy-start | bytes 9220
  449.1 5.8 %copy-start.60 = (f32[12288]{0:T(1024)S(1)}, f32[12288]{0:T(1024)}, u32[]{:S(2)}) copy-start(f32[12288]{0:T(1024)} %reshape.398) | copy-start | bytes 147460
  (80 other events, 189.7 us)
Sparse Core Ops, SparseCore 0:
  9.8 53.6 all-gather.8
  65.1 50.4 all-gather.10
  117.9 34.3 all-gather.12
  153.8 39.5 all-gather.14
  265.6 35.5 reduce-scatter.4
  303.5 46.5 reduce-scatter.6
  371.8 36.3 reduce-scatter.10
  410.6 49.9 reduce-scatter.8
